TPU v7x, 32 devices: a whole 2x2x4 slice. The times are simulated.
32 devices in a mesh: dp: 16 (over z, y, x), mp: 2 (over core).
Axes of the slice: x: 2, y: 2, z: 4, core: 2. Of those that a mesh axis runs over, the one named last changes fastest.
Arguments:
- embeddings: bfloat16 [49152, 1024], P('dp', 'mp'), may hold values from -24 to 24
- first_level: int32 [49152], P('dp'), may hold values from 0 to 1023, as said below
- second_level: int32 [1024, 1], P('dp'), may hold values from 0 to 1023
Outputs:
- first_centroids: bfloat16 [1024, 1024], P('dp', 'mp')
- second_centroids: bfloat16 [1024, 1024], P('dp', 'mp')
- scores: float32 [1024, 1024], P('dp', 'mp')
Inputs may be any that keep to these rules, and one draw needn't show every extreme that they name: `first_level`: the rows i * 3072 to (i + 1) * 3072 - 1 are assigned only to level-one centroids numbered from ((i + j) mod 16) * 64, that is to the centroids (i + j) * 64 to (i + j + 1) * 64 - 1 taken modulo 1024, for j from 0 to 7; every level-one centroid has at least one row. `second_level`: every level-two centroid is named by at least one level-one centroid.
All inputs are finite; a program needn't handle non-finite values.
Results may differ from a plain program's by a relative error of at most 0.012.
Values may be sent and summed in bfloat16 or wider, within the bound.
No kernel may reach another device: no remote copies, remote signals or barrier semaphores. Data moves between devices by JAX's collectives and lax.ppermute only.
A program may use at most 64 MiB of HBM per device.

v0:
```python
import jax
import jax.numpy as jnp
from jax import lax
from jax.sharding import PartitionSpec as P

CENT_DEV = 64
BAND = 8
K2 = 1024


def shifted(value, axis, steps):
    count = lax.axis_size(axis)
    pairs = [(source, (source + steps) % count) for source in range(count)]
    return lax.ppermute(value, axis, pairs)


def shards(embeddings, first_level, second_level):
    devices = lax.axis_size("dp")
    position = lax.axis_index("dp")
    half_width = embeddings.shape[1]
    band_width = BAND * CENT_DEV
    local_ids = (first_level - position * CENT_DEV) % (CENT_DEV * devices)
    block_rows = min(1024, embeddings.shape[0])
    blocks = embeddings.shape[0] // block_rows
    columns = jnp.arange(band_width, dtype=jnp.int32)

    def accumulate(running, pair):
        rows_block, ids_block = pair
        one_hot = (ids_block[:, None] == columns[None, :]).astype(jnp.bfloat16)
        totals = running[0] + jnp.einsum(
            "rk,rd->kd", one_hot, rows_block, preferred_element_type=jnp.float32
        )
        tallies = running[1] + jnp.sum(one_hot.astype(jnp.float32), axis=0)
        return ((totals, tallies), None)

    start_state = (
        jnp.zeros((band_width, half_width), jnp.float32),
        jnp.zeros((band_width,), jnp.float32),
    )
    (totals, tallies), unused = lax.scan(
        accumulate,
        start_state,
        (embeddings.reshape(blocks, block_rows, half_width), local_ids.reshape(blocks, block_rows)),
    )
    totals = totals.reshape(BAND, CENT_DEV, half_width)
    tallies = tallies.reshape(BAND, CENT_DEV)
    summed = totals[0]
    counted = tallies[0]
    for offset in range(1, BAND):
        moved = (
            shifted(totals[offset].astype(jnp.bfloat16), "dp", offset).astype(jnp.float32),
            shifted(tallies[offset].astype(jnp.bfloat16), "dp", offset).astype(jnp.float32),
        )
        summed = summed + moved[0]
        counted = counted + moved[1]
    first_centroids = (summed / counted[:, None]).astype(jnp.bfloat16)
    second_ids = jnp.arange(K2, dtype=jnp.int32)
    group_hot = (second_level == second_ids[None, :]).astype(jnp.bfloat16)
    group_totals = jnp.einsum(
        "ck,cd->kd", group_hot, first_centroids, preferred_element_type=jnp.float32
    )
    group_counts = jnp.sum(group_hot.astype(jnp.float32), axis=0)
    whole, whole_counts = lax.psum((group_totals, group_counts), "dp")
    every_centroid = (whole / whole_counts[:, None]).astype(jnp.bfloat16)
    owned_rows = K2 // devices
    second_centroids = lax.dynamic_slice_in_dim(
        every_centroid, position * owned_rows, owned_rows, 0
    )
    values = every_centroid.astype(jnp.float32)
    products = jnp.einsum(
        "cd,kd->ck", first_centroids, every_centroid, preferred_element_type=jnp.float32
    )
    partial_value = products - 0.5 * jnp.sum(values * values, axis=1)[None, :]
    scores = lax.psum_scatter(
        partial_value.astype(jnp.bfloat16), "mp", scatter_dimension=1, tiled=True
    ).astype(jnp.float32)
    return (first_centroids, second_centroids, scores)


def solution(mesh):
    placed = (P("dp", "mp"), P("dp"), P("dp", None))
    return jax.shard_map(
        shards,
        mesh=mesh,
        in_specs=placed,
        out_specs=(P("dp", "mp"), P("dp", "mp"), P("dp", "mp")),
        check_vma=False,
    )
```

profile of v0, /device:TPU:0, one launch (start us, length us, event | category | flops | bytes accessed | tf_op | source)
XLA Modules:
  0.0 195.4 jit_solution(15562190803789362735)
XLA Ops:
  8.0 7.9 %while.13 = (s32[]{:T(128)}, f32[512,512]{1,0:T(8,128)S(1)}, f32[512]{0:T(512)S(1)}, s32[3,1024]{1,0:T(4,128)S(1)}, bf16[3,1024,512]{2,1,0:T(8,128)(2,1)}, /*index=5*/s32[]{:T(128)}, s32[]{:T(128)}) while((s32[]{:T(128)}, f32[512,512]{1,0:T(8,128)S(1)}, f32[512]{0:T(512)S(1)}, s32[3,1024]{1,0:T(4,128)S(1)}, ...), condition=%wide.region_2.3_spmd.clone, body=%wide.region_0.2_spmd.clone.sunk | while | flops 540017152 | bytes 3170908 | solution.py:40
  8.0 2.3 %fusion.22 = f32[512,512]{1,0:T(8,128)S(1)} fusion(f32[512,512]{1,0:T(8,128)S(1)} %get-tuple-element.123, bf16[3,1024,512]{2,1,0:T(8,128)(2,1)} %get-tuple-element.133, s32[]{:T(128)} %get-tuple-element.122, s32[1024]{0:T(1024)S(1)} %bitcast.13, pred[]{:T(512)S(6)} %compare.4), kind=kOutput, calls=%fused_computation.5.clone.1 | convolution fusion | flops 537919488 | bytes 3150337 | tf_op jit(solution)/shard_map/while/body/eval_jaxpr/rk,rd->kd/dot_general | solution.py:30
  10.7 2.3 %fusion.22 = f32[512,512]{1,0:T(8,128)S(1)} fusion(f32[512,512]{1,0:T(8,128)S(1)} %get-tuple-element.123, bf16[3,1024,512]{2,1,0:T(8,128)(2,1)} %get-tuple-element.133, s32[]{:T(128)} %get-tuple-element.122, s32[1024]{0:T(1024)S(1)} %bitcast.13, pred[]{:T(512)S(6)} %compare.4), kind=kOutput, calls=%fused_computation.5.clone.1 | convolution fusion | flops 537919488 | bytes 3150337 | tf_op jit(solution)/shard_map/while/body/eval_jaxpr/rk,rd->kd/dot_general | solution.py:30
  13.3 2.3 %fusion.22 = f32[512,512]{1,0:T(8,128)S(1)} fusion(f32[512,512]{1,0:T(8,128)S(1)} %get-tuple-element.123, bf16[3,1024,512]{2,1,0:T(8,128)(2,1)} %get-tuple-element.133, s32[]{:T(128)} %get-tuple-element.122, s32[1024]{0:T(1024)S(1)} %bitcast.13, pred[]{:T(512)S(6)} %compare.4), kind=kOutput, calls=%fused_computation.5.clone.1 | convolution fusion | flops 537919488 | bytes 3150337 | tf_op jit(solution)/shard_map/while/body/eval_jaxpr/rk,rd->kd/dot_general | solution.py:30
  16.0 3.0 %collective-permute-start = (bf16[64,512]{1,0:T(8,128)(2,1)S(1)}, bf16[64,512]{1,0:T(8,128)(2,1)S(1)}, u32[]{:S(2)}, u32[]{:S(2)}) collective-permute-start(bf16[64,512]{1,0:T(8,128)(2,1)S(1)} %get-tuple-element.70), channel_id=1, source_target_pairs={{0,2},{2,4},{4,6},{6,8},{8,10},{10,12},{12,14},{14,16},{16,18},{18... | collective-permute-start | bytes 196616 | tf_op jit(solution)/shard_map/ppermute | solution.py:14
  19.0 1.5 collective-permute-start.1
  20.6 1.6 collective-permute-start.10
  22.2 2.5 %collective-permute-start.11 = (bf16[64]{0:T(256)(128)(2,1)S(1)}, bf16[64]{0:T(256)(128)(2,1)S(1)}, u32[]{:S(2)}, u32[]{:S(2)}) collective-permute-start(bf16[64]{0:T(256)(128)(2,1)S(1)} %get-tuple-element.80), channel_id=1, source_target_pairs={{0,10},{2,12},{4,14},{6,16},{8,18},{10,20},{12,22},{14,24},{16,26}... | collective-permute-start | bytes 392 | tf_op jit(solution)/shard_map/ppermute | solution.py:14
  24.7 1.2 collective-permute-start.12
  26.0 3.4 %collective-permute-start.13 = (bf16[64]{0:T(256)(128)(2,1)S(1)}, bf16[64]{0:T(256)(128)(2,1)S(1)}, u32[]{:S(2)}, u32[]{:S(2)}) collective-permute-start(bf16[64]{0:T(256)(128)(2,1)S(1)} %get-tuple-element.78), channel_id=1, source_target_pairs={{0,14},{2,16},{4,18},{6,20},{8,22},{10,24},{12,26},{14,28},{16,30}... | collective-permute-start | bytes 392 | tf_op jit(solution)/shard_map/ppermute | solution.py:14
  30.1 2.4 %collective-permute-start.8 = (bf16[64]{0:T(256)(128)(2,1)S(1)}, bf16[64]{0:T(256)(128)(2,1)S(1)}, u32[]{:S(2)}, u32[]{:S(2)}) collective-permute-start(bf16[64]{0:T(256)(128)(2,1)S(1)} %get-tuple-element.83), channel_id=1, source_target_pairs={{0,4},{2,6},{4,8},{6,10},{8,12},{10,14},{12,16},{14,18},{16,20},{1... | collective-permute-start | bytes 392 | tf_op jit(solution)/shard_map/ppermute | solution.py:14
  32.5 3.1 %collective-permute-start.9 = (bf16[64]{0:T(256)(128)(2,1)S(1)}, bf16[64]{0:T(256)(128)(2,1)S(1)}, u32[]{:S(2)}, u32[]{:S(2)}) collective-permute-start(bf16[64]{0:T(256)(128)(2,1)S(1)} %get-tuple-element.82), channel_id=1, source_target_pairs={{0,6},{2,8},{4,10},{6,12},{8,14},{10,16},{12,18},{14,20},{16,22},{... | collective-permute-start | bytes 392 | tf_op jit(solution)/shard_map/ppermute | solution.py:14
  35.6 0.9 collective-permute-done.7
  36.5 2.2 %collective-permute-done.9 = bf16[64]{0:T(256)(128)(2,1)S(1)} collective-permute-done((bf16[64]{0:T(256)(128)(2,1)S(1)}, bf16[64]{0:T(256)(128)(2,1)S(1)}, u32[]{:S(2)}, u32[]{:S(2)}) %collective-permute-start.9) | collective-permute-done | bytes 160 | tf_op jit(solution)/shard_map/ppermute | solution.py:14
  39.3 1.4 collective-permute-start.5
  40.7 4.1 %collective-permute-start.6 = (bf16[64,512]{1,0:T(8,128)(2,1)S(1)}, bf16[64,512]{1,0:T(8,128)(2,1)S(1)}, u32[]{:S(2)}, u32[]{:S(2)}) collective-permute-start(bf16[64,512]{1,0:T(8,128)(2,1)S(1)} %get-tuple-element.71), channel_id=1, source_target_pairs={{0,14},{2,16},{4,18},{6,20},{8,22},{10,24},{12,26},{14,28},{16,30}... | collective-permute-start | bytes 196616 | tf_op jit(solution)/shard_map/ppermute | solution.py:14
  44.9 2.3 %collective-permute-done.4 = bf16[64,512]{1,0:T(8,128)(2,1)S(1)} collective-permute-done((bf16[64,512]{1,0:T(8,128)(2,1)S(1)}, bf16[64,512]{1,0:T(8,128)(2,1)S(1)}, u32[]{:S(2)}, u32[]{:S(2)}) %collective-permute-start.4) | collective-permute-done | bytes 65568 | tf_op jit(solution)/shard_map/ppermute | solution.py:14
  47.3 1.9 fusion.11
  49.4 41.0 %psum.15 = f32[1024]{0:T(1024)S(1)} all-reduce(f32[1024]{0:T(1024)S(1)} %convert_reduce_fusion.1), channel_id=1, replica_groups=mesh['dp'=16,'mp'=2] {'dp'}, use_global_device_ids=true, to_apply=%region_5.6 | all-reduce | flops 1024 | bytes 8192 | tf_op jit(solution)/shard_map/psum | solution.py:63
  90.3 86.5 %all-reduce.2.cloned.1.call-done = f32[1024,512]{1,0:T(8,128)} async-done(((f32[1024,512]{1,0:T(8,128)}), f32[1024,512]{1,0:T(8,128)}) %all-reduce.2.cloned.1.call-update) | async-done | bytes 2097168 | tf_op jit(solution)/shard_map/psum | solution.py:63
  176.9 2.0 %multiply_reduce_fusion = (f32[1024]{0:T(1024)S(1)}, bf16[1024,512]{1,0:T(8,128)(2,1)S(1)}) fusion(f32[1024,512]{1,0:T(8,128)} %all-reduce.2.cloned.1.call-done, f32[1024]{0:T(1024)S(1)} %psum.15), kind=kLoop, calls=%fused_computation.12 | loop fusion | flops 2620416 | bytes 3153920 | tf_op jit(solution)/shard_map/reduce_sum | solution.py:73
  178.9 1.1 fusion.9
  180.7 6.4 %reduce-scatter.2.cloned.1.call-done = bf16[64,512]{1,0:T(8,128)(2,1)} async-done(((bf16[64,1024]{1,0:T(8,128)(2,1)}), bf16[64,512]{1,0:T(8,128)(2,1)}) %reduce-scatter.2.cloned.1.call-update) | async-done | bytes 65552 | tf_op jit(solution)/shard_map/reduce_scatter | solution.py:74
  187.1 1.5 convert_element_type.103
  (45 shorter events, 4.2 us)
Async XLA Ops:
  7.2 169.7 %all-reduce.2.cloned.1.call-start = ((), (), s32[]{:S(2)}) async-start(), calls=%async_computation.1 | async-start | bytes 4194304 | tf_op jit(solution)/shard_map/psum | solution.py:63
  15.9 31.4 %copy-start.1 = (s32[64,1]{0,1:T(1,128)S(1)}, s32[64,1]{0,1:T(1,128)}, u32[]{:S(2)}) copy-start(s32[64,1]{0,1:T(1,128)} %param.7) | copy-start | bytes 772
  16.0 23.3 %collective-permute-start = (bf16[64,512]{1,0:T(8,128)(2,1)S(1)}, bf16[64,512]{1,0:T(8,128)(2,1)S(1)}, u32[]{:S(2)}, u32[]{:S(2)}) collective-permute-start(bf16[64,512]{1,0:T(8,128)(2,1)S(1)} %get-tuple-element.70), channel_id=1, source_target_pairs={{0,2},{2,4},{4,6},{6,8},{8,10},{10,12},{12,14},{14,16},{16,18},{18... | collective-permute-start | bytes 196616 | tf_op jit(solution)/shard_map/ppermute | solution.py:14
  19.0 21.7 %collective-permute-start.1 = (bf16[64,512]{1,0:T(8,128)(2,1)S(1)}, bf16[64,512]{1,0:T(8,128)(2,1)S(1)}, u32[]{:S(2)}, u32[]{:S(2)}) collective-permute-start(bf16[64,512]{1,0:T(8,128)(2,1)S(1)} %get-tuple-element.76), channel_id=1, source_target_pairs={{0,4},{2,6},{4,8},{6,10},{8,12},{10,14},{12,16},{14,18},{16,20},{1... | collective-permute-start | bytes 196616 | tf_op jit(solution)/shard_map/ppermute | solution.py:14
  20.6 5.3 %collective-permute-start.10 = (bf16[64]{0:T(256)(128)(2,1)S(1)}, bf16[64]{0:T(256)(128)(2,1)S(1)}, u32[]{:S(2)}, u32[]{:S(2)}) collective-permute-start(bf16[64]{0:T(256)(128)(2,1)S(1)} %get-tuple-element.81), channel_id=1, source_target_pairs={{0,8},{2,10},{4,12},{6,14},{8,16},{10,18},{12,20},{14,22},{16,24},... | collective-permute-start | bytes 392 | tf_op jit(solution)/shard_map/ppermute | solution.py:14
  22.2 7.1 %collective-permute-start.11 = (bf16[64]{0:T(256)(128)(2,1)S(1)}, bf16[64]{0:T(256)(128)(2,1)S(1)}, u32[]{:S(2)}, u32[]{:S(2)}) collective-permute-start(bf16[64]{0:T(256)(128)(2,1)S(1)} %get-tuple-element.80), channel_id=1, source_target_pairs={{0,10},{2,12},{4,14},{6,16},{8,18},{10,20},{12,22},{14,24},{16,26}... | collective-permute-start | bytes 392 | tf_op jit(solution)/shard_map/ppermute | solution.py:14
  24.7 5.3 %collective-permute-start.12 = (bf16[64]{0:T(256)(128)(2,1)S(1)}, bf16[64]{0:T(256)(128)(2,1)S(1)}, u32[]{:S(2)}, u32[]{:S(2)}) collective-permute-start(bf16[64]{0:T(256)(128)(2,1)S(1)} %get-tuple-element.79), channel_id=1, source_target_pairs={{0,12},{2,14},{4,16},{6,18},{8,20},{10,22},{12,24},{14,26},{16,28}... | collective-permute-start | bytes 392 | tf_op jit(solution)/shard_map/ppermute | solution.py:14
  26.0 6.5 %collective-permute-start.13 = (bf16[64]{0:T(256)(128)(2,1)S(1)}, bf16[64]{0:T(256)(128)(2,1)S(1)}, u32[]{:S(2)}, u32[]{:S(2)}) collective-permute-start(bf16[64]{0:T(256)(128)(2,1)S(1)} %get-tuple-element.78), channel_id=1, source_target_pairs={{0,14},{2,16},{4,18},{6,20},{8,22},{10,24},{12,26},{14,28},{16,30}... | collective-permute-start | bytes 392 | tf_op jit(solution)/shard_map/ppermute | solution.py:14
  29.4 7.1 %collective-permute-start.7 = (bf16[64]{0:T(256)(128)(2,1)S(1)}, bf16[64]{0:T(256)(128)(2,1)S(1)}, u32[]{:S(2)}, u32[]{:S(2)}) collective-permute-start(bf16[64]{0:T(256)(128)(2,1)S(1)} %get-tuple-element.77), channel_id=1, source_target_pairs={{0,2},{2,4},{4,6},{6,8},{8,10},{10,12},{12,14},{14,16},{16,18},{18... | collective-permute-start | bytes 392 | tf_op jit(solution)/shard_map/ppermute | solution.py:14
  30.1 6.4 %collective-permute-start.8 = (bf16[64]{0:T(256)(128)(2,1)S(1)}, bf16[64]{0:T(256)(128)(2,1)S(1)}, u32[]{:S(2)}, u32[]{:S(2)}) collective-permute-start(bf16[64]{0:T(256)(128)(2,1)S(1)} %get-tuple-element.83), channel_id=1, source_target_pairs={{0,4},{2,6},{4,8},{6,10},{8,12},{10,14},{12,16},{14,18},{16,20},{1... | collective-permute-start | bytes 392 | tf_op jit(solution)/shard_map/ppermute | solution.py:14
  32.5 6.2 %collective-permute-start.9 = (bf16[64]{0:T(256)(128)(2,1)S(1)}, bf16[64]{0:T(256)(128)(2,1)S(1)}, u32[]{:S(2)}, u32[]{:S(2)}) collective-permute-start(bf16[64]{0:T(256)(128)(2,1)S(1)} %get-tuple-element.82), channel_id=1, source_target_pairs={{0,6},{2,8},{4,10},{6,12},{8,14},{10,16},{12,18},{14,20},{16,22},{... | collective-permute-start | bytes 392 | tf_op jit(solution)/shard_map/ppermute | solution.py:14
  36.5 8.4 %collective-permute-start.2 = (bf16[64,512]{1,0:T(8,128)(2,1)S(1)}, bf16[64,512]{1,0:T(8,128)(2,1)S(1)}, u32[]{:S(2)}, u32[]{:S(2)}) collective-permute-start(bf16[64,512]{1,0:T(8,128)(2,1)S(1)} %get-tuple-element.75), channel_id=1, source_target_pairs={{0,6},{2,8},{4,10},{6,12},{8,14},{10,16},{12,18},{14,20},{16,22},{... | collective-permute-start | bytes 196616 | tf_op jit(solution)/shard_map/ppermute | solution.py:14
  36.5 8.4 %collective-permute-start.3 = (bf16[64,512]{1,0:T(8,128)(2,1)S(1)}, bf16[64,512]{1,0:T(8,128)(2,1)S(1)}, u32[]{:S(2)}, u32[]{:S(2)}) collective-permute-start(bf16[64,512]{1,0:T(8,128)(2,1)S(1)} %get-tuple-element.74), channel_id=1, source_target_pairs={{0,8},{2,10},{4,12},{6,14},{8,16},{10,18},{12,20},{14,22},{16,24},... | collective-permute-start | bytes 196616 | tf_op jit(solution)/shard_map/ppermute | solution.py:14
  38.7 8.5 %collective-permute-start.4 = (bf16[64,512]{1,0:T(8,128)(2,1)S(1)}, bf16[64,512]{1,0:T(8,128)(2,1)S(1)}, u32[]{:S(2)}, u32[]{:S(2)}) collective-permute-start(bf16[64,512]{1,0:T(8,128)(2,1)S(1)} %get-tuple-element.73), channel_id=1, source_target_pairs={{0,10},{2,12},{4,14},{6,16},{8,18},{10,20},{12,22},{14,24},{16,26}... | collective-permute-start | bytes 196616 | tf_op jit(solution)/shard_map/ppermute | solution.py:14
  39.3 7.9 %collective-permute-start.5 = (bf16[64,512]{1,0:T(8,128)(2,1)S(1)}, bf16[64,512]{1,0:T(8,128)(2,1)S(1)}, u32[]{:S(2)}, u32[]{:S(2)}) collective-permute-start(bf16[64,512]{1,0:T(8,128)(2,1)S(1)} %get-tuple-element.72), channel_id=1, source_target_pairs={{0,12},{2,14},{4,16},{6,18},{8,20},{10,22},{12,24},{14,26},{16,28}... | collective-permute-start | bytes 196616 | tf_op jit(solution)/shard_map/ppermute | solution.py:14
  40.7 6.5 %collective-permute-start.6 = (bf16[64,512]{1,0:T(8,128)(2,1)S(1)}, bf16[64,512]{1,0:T(8,128)(2,1)S(1)}, u32[]{:S(2)}, u32[]{:S(2)}) collective-permute-start(bf16[64,512]{1,0:T(8,128)(2,1)S(1)} %get-tuple-element.71), channel_id=1, source_target_pairs={{0,14},{2,16},{4,18},{6,20},{8,22},{10,24},{12,26},{14,28},{16,30}... | collective-permute-start | bytes 196616 | tf_op jit(solution)/shard_map/ppermute | solution.py:14
  47.3 131.6 %copy-start = (bf16[64,512]{1,0:T(8,128)(2,1)}, bf16[64,512]{1,0:T(8,128)(2,1)S(1)}, u32[]{:S(2)}) copy-start(bf16[64,512]{1,0:T(8,128)(2,1)S(1)} %divide_convert_fusion.1) | copy-start | bytes 196612
  49.2 137.9 %reduce-scatter.2.cloned.1.call-start = ((), (), s32[]{:S(2)}) async-start(), calls=%async_computation.2 | async-start | bytes 196608 | tf_op jit(solution)/shard_map/reduce_scatter | solution.py:74
Sparse Core Ops, SparseCore 0:
  49.3 127.5 all-reduce.1
  180.2 6.8 reduce-scatter.1
where the time goes:
time: 196 us; the launch traced here: 195 us
  waiting for transfers between devices  98.6 us (50%)
  blocking collectives  41 us (21%)
  starting transfers between devices  25.5 us (13%)
  between operations  14.2 us (7%)
  matrix products  9.88 us (5%)
  other arithmetic  5.37 us (3%)
    psum x1, waiting for transfers between devices, shards(): whole, whole_counts = lax.psum((group_totals, group_counts), 'dp')  86.5 us
    psum x1, blocking collectives, shards(): whole, whole_counts = lax.psum((group_totals, group_counts), 'dp')  41 us
    ppermute x14, starting transfers between devices, shifted(): return lax.ppermute(value, axis, pairs)  25.4 us
    dot_general x3, matrix products, accumulate(): jnp.einsum('rk,rd->kd', one_hot, rows_block, preferred_element_type=jnp.f...  6.92 us
    reduce_scatter x1, waiting for transfers between devices, shards(): lax.psum_scatter(partial_value.astype(jnp.bfloat16), 'mp', scatter_dimens...  6.38 us
    ppermute x14, waiting for transfers between devices, shifted(): return lax.ppermute(value, axis, pairs)  5.64 us
  transfers between devices with their start and end apart: 16, of which 7 were waited for; matrix products, arithmetic and copies ran while one was open for 0% of the time, Pallas kernels for 0%

commit v1 on v0

v1 whole, which is shorter than its diff:
```python
import functools

import jax
import jax.numpy as jnp
from jax import lax
from jax.experimental import pallas as pl
from jax.experimental.pallas import tpu as pltpu
from jax.sharding import PartitionSpec as P

BAND = 8
K2 = 1024
GROUP = 4
META = 16
BASE = 256
LANES = 128
BF16 = jnp.bfloat16
F32 = jnp.float32


def whole():
    return pl.BlockSpec(memory_space=pltpu.VMEM)


def exchanged(value, pairs):
    return lax.ppermute(value, ("dp", "mp"), pairs)


def iota(shape, dim):
    return lax.broadcasted_iota(jnp.int32, shape, dim)


def split_digits(row):
    high = jnp.floor(row * (1.0 / BASE))
    return high, row - high * BASE


def as_column(row, cent):
    hit = iota((cent, LANES), 0) == iota((cent, LANES), 1)
    return jnp.sum(jnp.where(hit, row, 0.0), axis=1, keepdims=True)


def as_row(column):
    rows = column.shape[0]
    hit = iota((rows, LANES), 0) == iota((rows, LANES), 1)
    return jnp.sum(jnp.where(hit, column, 0.0), axis=0, keepdims=True)


def sum_kernel(devices, cent, ids_ref, rows_ref, group_ref, own_ref, own_meta_ref, *rest):
    sends, (totals, tallies) = rest[:-2], rest[-2:]
    step = pl.program_id(0)
    block = ids_ref.shape[-1]
    position = lax.axis_index("dp")
    mate = position % GROUP
    offset = ids_ref[0] - position * cent
    offset = jnp.where(offset < 0, offset + devices * cent, offset)
    ahead = offset // cent + mate
    partner = (ahead % GROUP) ^ mate
    slot = jnp.where(ahead // GROUP == 1, 1, 0)
    label = partner * (2 * cent) + slot * cent + offset % cent
    labels = 2 * GROUP * cent
    hit = iota((labels, block), 0) == label
    one_hot = jnp.where(hit, 1.0, 0.0).astype(BF16)
    part = lax.dot_general(
        one_hot, rows_ref[...], (((1,), (0,)), ((), ())), preferred_element_type=F32
    )
    count = one_hot[:, :LANES]
    for start in range(LANES, block, LANES):
        count = count + one_hot[:, start : start + LANES]

    @pl.when(step == 0)
    def _():
        totals[...] = part
        tallies[...] = count.astype(F32)

    @pl.when(step > 0)
    def _():
        totals[...] += part
        tallies[...] += count.astype(F32)

    @pl.when(step == pl.num_programs(0) - 1)
    def _():
        ids = as_row(group_ref[...].astype(F32))
        id_high, id_low = split_digits(ids)
        ones = jnp.ones((8, LANES), F32)
        counts = lax.dot_general(
            ones.astype(BF16),
            tallies[...].astype(BF16),
            (((1,), (1,)), ((), ())),
            preferred_element_type=F32,
        )
        pair = 2 * cent
        own_ref[...] = totals[:pair]
        for index in range(GROUP):
            count_row = counts[:1, index * pair : (index + 1) * pair]
            high, low = split_digits(count_row)
            meta = jnp.concatenate(
                [high, low, id_high, id_low, jnp.zeros((META - 4, LANES), F32)], axis=0
            )
            if index == 0:
                own_meta_ref[...] = meta
            else:
                sends[index - 1][:pair] = totals[index * pair : (index + 1) * pair].astype(BF16)
                sends[index - 1][pair:, :LANES] = meta.astype(BF16)
                sends[index - 1][pair:, LANES:] = jnp.zeros(
                    (META, sends[index - 1].shape[1] - LANES), BF16
                )


def band_sums(devices, cent, ids, rows, group):
    count, width = rows.shape
    block = min(1024, count)
    steps = count // block
    pair = 2 * cent
    send = jax.ShapeDtypeStruct((pair + META, width), BF16)
    fixed = lambda step: (0, 0)
    return pl.pallas_call(
        functools.partial(sum_kernel, devices, cent),
        grid=(steps,),
        in_specs=[
            pl.BlockSpec((1, 1, block), lambda step: (step, 0, 0)),
            pl.BlockSpec((block, width), lambda step: (step, 0)),
            pl.BlockSpec(group.shape, fixed),
        ],
        out_specs=[
            pl.BlockSpec((pair, width), fixed),
            pl.BlockSpec((META, LANES), fixed),
        ]
        + [pl.BlockSpec((pair + META, width), fixed)] * (GROUP - 1),
        out_shape=[
            jax.ShapeDtypeStruct((pair, width), F32),
            jax.ShapeDtypeStruct((META, LANES), F32),
        ]
        + [send] * (GROUP - 1),
        scratch_shapes=[
            pltpu.VMEM((GROUP * pair, width), F32),
            pltpu.VMEM((GROUP * pair, LANES), F32),
        ],
        compiler_params=pltpu.CompilerParams(vmem_limit_bytes=32 * 2**20),
    )(ids.reshape(steps, 1, block), rows, group)


def group_kernel(cent, own, own_meta, one, two, three, base_ref, base_meta_ref, next_ref, far_ref):
    mate = lax.axis_index("dp") % GROUP
    pair = 2 * cent
    lane = iota((1, LANES), 1)
    near = own[:cent]
    middle = own[cent:]
    far = jnp.zeros_like(near)
    counts = own_meta[0:1] * BASE + own_meta[1:2]
    far_counts = jnp.zeros_like(counts)
    for index, got in ((1, one), (2, two), (3, three)):
        before = (mate ^ index) < mate
        first = got[:cent].astype(F32)
        near = near + jnp.where(before, first, 0.0)
        far = far + jnp.where(before, 0.0, first)
        middle = middle + got[cent:pair].astype(F32)
        meta = got[pair:, :LANES].astype(F32)
        row = meta[0:1] * BASE + meta[1:2]
        mask = (lane >= cent) | before
        counts = counts + jnp.where(mask, row, 0.0)
        far_counts = far_counts + jnp.where(mask, 0.0, row)
        base_meta_ref[2 + 2 * index : 4 + 2 * index] = meta[2:4]
    base_ref[...] = near
    base_meta_ref[0:1] = counts
    base_meta_ref[1:2] = jnp.zeros_like(counts)
    base_meta_ref[2:4] = own_meta[2:4]
    base_meta_ref[10:] = jnp.zeros((META - 10, LANES), F32)
    for send, sums, row in ((next_ref, middle, counts), (far_ref, far, far_counts)):
        high, low = split_digits(row)
        meta = jnp.concatenate([high, low, jnp.zeros((META - 2, LANES), F32)], axis=0)
        send[:cent] = sums.astype(BF16)
        send[cent:, :LANES] = meta.astype(BF16)
        send[cent:, LANES:] = jnp.zeros((META, send.shape[1] - LANES), BF16)


def group_sums(cent, own, own_meta, got):
    width = own.shape[1]
    send = jax.ShapeDtypeStruct((cent + META, width), BF16)
    return pl.pallas_call(
        functools.partial(group_kernel, cent),
        in_specs=[whole()] * 5,
        out_specs=[whole()] * 4,
        out_shape=[
            jax.ShapeDtypeStruct((cent, width), F32),
            jax.ShapeDtypeStruct((META, LANES), F32),
            send,
            send,
        ],
    )(own, own_meta, *got)


def mean_kernel(cent, base, base_meta, one, two, mean_ref, send_ref):
    sums = base[...] + one[:cent].astype(F32) + two[:cent].astype(F32)
    first = one[cent:, :LANES].astype(F32)
    second = two[cent:, :LANES].astype(F32)
    middle = first[0:1] * BASE + first[1:2]
    row = base_meta[0:1] + pltpu.roll(middle, LANES - cent, 1) + second[0:1] * BASE + second[1:2]
    mean = (sums / as_column(row, cent)).astype(BF16)
    mean_ref[...] = mean
    send_ref[:cent] = mean
    send_ref[cent:, :LANES] = base_meta[...].astype(BF16)
    send_ref[cent:, LANES:] = jnp.zeros((META, mean.shape[1] - LANES), BF16)


def means(cent, base, base_meta, got):
    width = base.shape[1]
    return pl.pallas_call(
        functools.partial(mean_kernel, cent),
        in_specs=[whole()] * 4,
        out_specs=[whole()] * 2,
        out_shape=[
            jax.ShapeDtypeStruct((cent, width), BF16),
            jax.ShapeDtypeStruct((cent + META, width), BF16),
        ],
    )(base, base_meta, *got)


def line_kernel(cent, *refs):
    blocks, (line_ref, ids_ref) = refs[:-2], refs[-2:]
    lane = iota((1, LANES), 1)
    for index, block in enumerate(blocks):
        line_ref[index * cent : (index + 1) * cent] = block[:cent]
    metas = [block[cent:, :LANES].astype(F32) for block in blocks]
    for index in range(GROUP):
        at = 2 + 2 * index
        rows = [meta[at : at + 1] * BASE + meta[at + 1 : at + 2] for meta in metas]
        joined = []
        for left, right in zip(rows[0::2], rows[1::2]):
            joined.append(jnp.where(lane < cent, left, pltpu.roll(right, cent, 1)))
        ids_ref[index : index + 1] = jnp.concatenate(joined, axis=1).astype(jnp.int32)


def line(cent, blocks):
    width = blocks[0].shape[1]
    return pl.pallas_call(
        functools.partial(line_kernel, cent),
        in_specs=[whole()] * len(blocks),
        out_specs=[whole()] * 2,
        out_shape=[
            jax.ShapeDtypeStruct((len(blocks) * cent, width), BF16),
            jax.ShapeDtypeStruct((8, len(blocks) * cent), jnp.int32),
        ],
    )(*blocks)


def score_kernel(owned, ids, mean, *refs):
    blocks, (second_ref, keep_ref, send_ref, sums) = refs[:-4], refs[-4:]
    count = jnp.zeros((K2, 1), F32)
    for index, block in enumerate(blocks):
        hit = iota((K2, block.shape[0]), 0) == ids[index : index + 1]
        one_hot = jnp.where(hit, 1.0, 0.0)
        count = count + jnp.sum(one_hot, axis=1, keepdims=True)
        part = jnp.dot(one_hot.astype(BF16), block[...], preferred_element_type=F32)
        if index == 0:
            sums[...] = part
        else:
            sums[...] += part
    second = (sums[...] / count).astype(BF16)
    values = second.astype(F32)
    sums[...] = values
    start = pl.multiple_of(lax.axis_index("dp") * owned, owned)
    second_ref[...] = sums[pl.ds(start, owned)].astype(BF16)
    norms = 0.5 * jnp.sum(values * values, axis=1, keepdims=True)
    row = jnp.concatenate(
        [as_row(norms[at : at + LANES]) for at in range(0, K2, LANES)], axis=1
    )
    products = lax.dot_general(
        mean[...], second, (((1,), (1,)), ((), ())), preferred_element_type=F32
    )
    scores = products - row
    half = K2 // 2
    low = lax.axis_index("mp") == 0
    keep_ref[...] = jnp.where(low, scores[:, :half], scores[:, half:])
    send_ref[...] = jnp.where(low, scores[:, half:], scores[:, :half]).astype(BF16)


def second_level_scores(owned, ids, mean, blocks):
    cent, width = mean.shape
    return pl.pallas_call(
        functools.partial(score_kernel, owned),
        in_specs=[whole()] * (2 + len(blocks)),
        out_specs=[whole()] * 3,
        out_shape=[
            jax.ShapeDtypeStruct((owned, width), BF16),
            jax.ShapeDtypeStruct((cent, K2 // 2), F32),
            jax.ShapeDtypeStruct((cent, K2 // 2), BF16),
        ],
        scratch_shapes=[pltpu.VMEM((K2, width), F32)],
        compiler_params=pltpu.CompilerParams(vmem_limit_bytes=32 * 2**20),
    )(ids, mean, *blocks)


def summed_scores(devices, second_level, first_centroids):
    second_ids = jnp.arange(K2, dtype=jnp.int32)
    group_hot = (second_level == second_ids[None, :]).astype(BF16)
    group_totals = jnp.einsum("ck,cd->kd", group_hot, first_centroids, preferred_element_type=F32)
    group_counts = jnp.sum(group_hot.astype(F32), axis=0)
    total, total_counts = lax.psum((group_totals, group_counts), "dp")
    every = (total / total_counts[:, None]).astype(BF16)
    owned = K2 // devices
    second = lax.dynamic_slice_in_dim(every, lax.axis_index("dp") * owned, owned, 0)
    values = every.astype(F32)
    products = jnp.einsum("cd,kd->ck", first_centroids, every, preferred_element_type=F32)
    partial_value = products - 0.5 * jnp.sum(values * values, axis=1)[None, :]
    scores = lax.psum_scatter(
        partial_value.astype(BF16), "mp", scatter_dimension=1, tiled=True
    ).astype(F32)
    return second, scores


def shards(embeddings, first_level, second_level):
    devices = lax.axis_size("dp")
    cores = lax.axis_size("mp")
    cent = second_level.shape[0]
    everyone = [(d, c) for d in range(devices) for c in range(cores)]

    def partner(value, index):
        return exchanged(value, [(d * cores + c, (d ^ index) * cores + c) for d, c in everyone])

    def ahead(value, steps):
        return exchanged(
            value, [(d * cores + c, (d + steps) % devices * cores + c) for d, c in everyone]
        )

    own, own_meta, *sends = band_sums(devices, cent, first_level, embeddings, second_level)
    got = [partner(send, index + 1) for index, send in enumerate(sends)]
    base, base_meta, following, far = group_sums(cent, own, own_meta, got)
    got = [ahead(following, GROUP), ahead(far, 2 * GROUP)]
    mean, send = means(cent, base, base_meta, got)
    if devices * cent > K2 or cores != 2:
        return (mean, *summed_scores(devices, second_level, mean))
    blocks = [send] + [ahead(send, steps) for steps in range(GROUP, devices, GROUP)]
    row, ids = line(cent, blocks)
    rows = [row] + [partner(row, index) for index in range(1, GROUP)]
    second, keep, send = second_level_scores(K2 // devices, ids, mean, rows)
    got = exchanged(send, [(d * cores + c, d * cores + (c ^ 1)) for d, c in everyone])
    return mean, second, keep + got.astype(F32)


def solution(mesh):
    placed = (P("dp", "mp"), P("dp"), P("dp", None))
    return jax.shard_map(
        shards,
        mesh=mesh,
        in_specs=placed,
        out_specs=(P("dp", "mp"), P("dp", "mp"), P("dp", "mp")),
        check_vma=False,
    )
```

time: 196 us -> 63.7 us (0.33)
  waiting for transfers between devices: 98.6 us -> 26.6 us
  blocking collectives: 41 us -> 0 us
  between operations: 14.2 us -> 0.68 us
  Pallas kernels: 0 us -> 10.4 us
  starting transfers between devices: 25.5 us -> 15.2 us
  matrix products: 9.88 us -> 0 us
  local copies, waits for them, and re-layouts: 0.81 us -> 9.71 us
  other arithmetic: 5.37 us -> 0.67 us
    psum x1 -> x0, waiting for transfers between devices: 86.5 us -> none  [shards(): whole, whole_counts = lax.psum((group_totals, group_counts), 'dp')]
    psum x1 -> x0, blocking collectives: 41 us -> none  [shards(): whole, whole_counts = lax.psum((group_totals, group_counts), 'dp')]
    ppermute x14 -> x12, waiting for transfers between devices: 5.64 us -> 26.6 us  [exchanged(): return lax.ppermute(value, ('dp', 'mp'), pairs)]
    pallas_call x0 -> x5, Pallas kernels: none -> 10.4 us  [the longest x1 2.7 us: band_sums(): pl.pallas_call(functools.partial(sum_kernel, devices, cent), grid=(steps,...]
    ppermute x14 -> x12, starting transfers between devices: 25.4 us -> 15.2 us  [exchanged(): return lax.ppermute(value, ('dp', 'mp'), pairs)]
    dot_general x5 -> x0, matrix products: 9.88 us -> none  [the longest x3 6.92 us: accumulate(): jnp.einsum('rk,rd->kd', one_hot, rows_block, preferred_element_type=jnp.f...]
    unnamed x4 -> x31, local copies, waits for them, and re-layouts: 0.01 us -> 9.71 us
    reduce_scatter x1 -> x0, waiting for transfers between devices: 6.38 us -> none  [shards(): lax.psum_scatter(partial_value.astype(jnp.bfloat16), 'mp', scatter_dimens...]
  transfers between devices with their start and end apart: 16 -> 12, of which waited for: 7 -> 9; matrix products, arithmetic and copies ran while one was open for 0% -> 0% of each run, Pallas kernels for 0% -> 0%
where the time goes in v1:
time: 63.7 us; the launch traced here: 63.3 us
  waiting for transfers between devices  26.6 us (42%)
  starting transfers between devices  15.2 us (24%)
  Pallas kernels  10.4 us (16%)
  local copies, waits for them, and re-layouts  9.71 us (15%)
  between operations  0.68 us (1%)
  other arithmetic  0.67 us (1%)
    ppermute x12, waiting for transfers between devices, exchanged(): return lax.ppermute(value, ('dp', 'mp'), pairs)  26.6 us
    ppermute x12, starting transfers between devices, exchanged(): return lax.ppermute(value, ('dp', 'mp'), pairs)  15.2 us
    unnamed x31, local copies, waits for them, and re-layouts  9.71 us
    pallas_call x1, Pallas kernels, band_sums(): pl.pallas_call(functools.partial(sum_kernel, devices, cent), grid=(steps,...  2.7 us
    pallas_call x1, Pallas kernels, second_level_scores(): pl.pallas_call(functools.partial(score_kernel, owned), in_specs=[whole()]...  2.22 us
    pallas_call x1, Pallas kernels, group_sums(): pl.pallas_call(functools.partial(group_kernel, cent), in_specs=[whole()]...  1.91 us
    pallas_call x1, Pallas kernels, means(): pl.pallas_call(functools.partial(mean_kernel, cent), in_specs=[whole()] *...  1.83 us
    pallas_call x1, Pallas kernels, line(): pl.pallas_call(functools.partial(line_kernel, cent), in_specs=[whole()] *...  1.73 us
  transfers between devices with their start and end apart: 12, of which 9 were waited for; matrix products, arithmetic and copies ran while one was open for 0% of the time, Pallas kernels for 0%

profile of v1, /device:TPU:0, one launch (start us, length us, event | category | flops | bytes accessed | tf_op | source)
XLA Modules:
  0.0 63.3 jit_solution(1274974413775304930)
XLA Ops:
  1.4 1.9 %copy-done = bf16[3072,512]{1,0:T(8,128)(2,1)S(1)} copy-done((bf16[3072,512]{1,0:T(8,128)(2,1)S(1)}, bf16[3072,512]{1,0:T(8,128)(2,1)}, u32[]{:S(2)}) %copy-start) | copy-done | bytes 3145752
  4.0 2.7 %shard_map.58 = (f32[128,512]{1,0:T(8,128)S(1)}, f32[16,128]{1,0:T(8,128)S(1)}, bf16[144,512]{1,0:T(8,128)(2,1)S(1)}, bf16[144,512]{1,0:T(8,128)(2,1)S(1)}, bf16[144,512]{1,0:T(8,128)(2,1)S(1)}) custom-call(s32[3,1,1024]{2,1,0:T(1,128)S(1)} %bitcast.1, bf16[3072,512]{1,0:T(8,128)(2,1)S(1)} %copy-done, s32[64,1]{1,0:T(8,128)S(1)} %copy.6.group_ref), custom_call_target="tpu_custom_call" | custom-call | tf_op jit(solution)/shard_map/pallas_call | solution.py:116
  8.0 2.9 %collective-permute-start = (bf16[144,512]{1,0:T(8,128)(2,1)S(1)}, bf16[144,512]{1,0:T(8,128)(2,1)S(1)}, u32[]{:S(2)}, u32[]{:S(2)}) collective-permute-start(bf16[144,512]{1,0:T(8,128)(2,1)S(1)} %get-tuple-element.21), channel_id=1, source_target_pairs={{0,2},{1,3},{2,0},{3,1},{4,6},{5,7},{6,4},{7,5},{8,10},{9,11},{10,... | collective-permute-start | bytes 442376 | tf_op jit(solution)/shard_map/ppermute | solution.py:25
  10.9 1.5 %collective-permute-start.1 = (bf16[144,512]{1,0:T(8,128)(2,1)S(1)}, bf16[144,512]{1,0:T(8,128)(2,1)S(1)}, u32[]{:S(2)}, u32[]{:S(2)}) collective-permute-start(bf16[144,512]{1,0:T(8,128)(2,1)S(1)} %get-tuple-element.22), channel_id=1, source_target_pairs={{0,4},{1,5},{2,6},{3,7},{4,0},{5,1},{6,2},{7,3},{8,12},{9,13},{10,... | collective-permute-start | bytes 442376 | tf_op jit(solution)/shard_map/ppermute | solution.py:25
  12.4 2.8 %collective-permute-done.one = bf16[144,512]{1,0:T(8,128)(2,1)S(1)} collective-permute-done((bf16[144,512]{1,0:T(8,128)(2,1)S(1)}, bf16[144,512]{1,0:T(8,128)(2,1)S(1)}, u32[]{:S(2)}, u32[]{:S(2)}) %collective-permute-start) | collective-permute-done | bytes 147488 | tf_op jit(solution)/shard_map/ppermute | solution.py:25
  15.2 4.2 %collective-permute-done.1.two = bf16[144,512]{1,0:T(8,128)(2,1)S(1)} collective-permute-done((bf16[144,512]{1,0:T(8,128)(2,1)S(1)}, bf16[144,512]{1,0:T(8,128)(2,1)S(1)}, u32[]{:S(2)}, u32[]{:S(2)}) %collective-permute-start.1) | collective-permute-done | bytes 147488 | tf_op jit(solution)/shard_map/ppermute | solution.py:25
  20.1 1.9 %shard_map.59 = (f32[64,512]{1,0:T(8,128)}, f32[16,128]{1,0:T(8,128)}, bf16[80,512]{1,0:T(8,128)(2,1)}, bf16[80,512]{1,0:T(8,128)(2,1)}) custom-call(f32[128,512]{1,0:T(8,128)} %copy-done.2, f32[16,128]{1,0:T(8,128)} %copy-done.5, bf16[144,512]{1,0:T(8,128)(2,1)} %copy-done.7, bf16[144,512]{1,0:T(8,128)(2,1)} %copy-done.8, bf16[144,512]{1,0:T(8,128)(2,1)} %copy-done.9), custom_call_target="tpu_custom_call" | custom-call | tf_op jit(solution)/shard_map/pallas_call | solution.py:179
  22.0 1.6 %collective-permute-start.3 = (bf16[80,512]{1,0:T(8,128)(2,1)}, bf16[80,512]{1,0:T(8,128)(2,1)S(1)}, u32[]{:S(2)}, u32[]{:S(2)}) collective-permute-start(bf16[80,512]{1,0:T(8,128)(2,1)} %get-tuple-element.26), channel_id=1, source_target_pairs={{0,8},{1,9},{2,10},{3,11},{4,12},{5,13},{6,14},{7,15},{8,16},{9,17... | collective-permute-start | bytes 245768 | tf_op jit(solution)/shard_map/ppermute | solution.py:25
  23.6 2.6 %collective-permute-start.4 = (bf16[80,512]{1,0:T(8,128)(2,1)}, bf16[80,512]{1,0:T(8,128)(2,1)S(1)}, u32[]{:S(2)}, u32[]{:S(2)}) collective-permute-start(bf16[80,512]{1,0:T(8,128)(2,1)} %get-tuple-element.27), channel_id=1, source_target_pairs={{0,16},{1,17},{2,18},{3,19},{4,20},{5,21},{6,22},{7,23},{8,24},{9,... | collective-permute-start | bytes 245768 | tf_op jit(solution)/shard_map/ppermute | solution.py:25
  26.2 2.5 %collective-permute-done.3.one = bf16[80,512]{1,0:T(8,128)(2,1)S(1)} collective-permute-done((bf16[80,512]{1,0:T(8,128)(2,1)}, bf16[80,512]{1,0:T(8,128)(2,1)S(1)}, u32[]{:S(2)}, u32[]{:S(2)}) %collective-permute-start.3) | collective-permute-done | bytes 81952 | tf_op jit(solution)/shard_map/ppermute | solution.py:25
  28.6 2.2 %collective-permute-done.4.two = bf16[80,512]{1,0:T(8,128)(2,1)S(1)} collective-permute-done((bf16[80,512]{1,0:T(8,128)(2,1)}, bf16[80,512]{1,0:T(8,128)(2,1)S(1)}, u32[]{:S(2)}, u32[]{:S(2)}) %collective-permute-start.4) | collective-permute-done | bytes 81952 | tf_op jit(solution)/shard_map/ppermute | solution.py:25
  31.4 1.8 %shard_map.60 = (bf16[64,512]{1,0:T(8,128)(2,1)}, bf16[80,512]{1,0:T(8,128)(2,1)}) custom-call(f32[64,512]{1,0:T(8,128)} %get-tuple-element.24.base, f32[16,128]{1,0:T(8,128)} %get-tuple-element.25.base_meta, bf16[80,512]{1,0:T(8,128)(2,1)} %copy-done.13, bf16[80,512]{1,0:T(8,128)(2,1)} %copy-done.14), custom_call_target="tpu_custom_call" | custom-call | tf_op jit(solution)/shard_map/pallas_call | solution.py:207
  33.3 2.0 %collective-permute-start.7 = (bf16[80,512]{1,0:T(8,128)(2,1)}, bf16[80,512]{1,0:T(8,128)(2,1)S(1)}, u32[]{:S(2)}, u32[]{:S(2)}) collective-permute-start(bf16[80,512]{1,0:T(8,128)(2,1)} %get-tuple-element.29.refs_0_), channel_id=1, source_target_pairs={{0,24},{1,25},{2,26},{3,27},{4,28},{5,29},{6,30},{7,31},{8,0},{9,1... | collective-permute-start | bytes 245768 | tf_op jit(solution)/shard_map/ppermute | solution.py:25
  35.3 1.1 %collective-permute-start.5 = (bf16[80,512]{1,0:T(8,128)(2,1)}, bf16[80,512]{1,0:T(8,128)(2,1)S(1)}, u32[]{:S(2)}, u32[]{:S(2)}) collective-permute-start(bf16[80,512]{1,0:T(8,128)(2,1)} %get-tuple-element.29.refs_0_), channel_id=1, source_target_pairs={{0,8},{1,9},{2,10},{3,11},{4,12},{5,13},{6,14},{7,15},{8,16},{9,17... | collective-permute-start | bytes 245768 | tf_op jit(solution)/shard_map/ppermute | solution.py:25
  36.3 1.6 %collective-permute-done.7.refs_3_ = bf16[80,512]{1,0:T(8,128)(2,1)S(1)} collective-permute-done((bf16[80,512]{1,0:T(8,128)(2,1)}, bf16[80,512]{1,0:T(8,128)(2,1)S(1)}, u32[]{:S(2)}, u32[]{:S(2)}) %collective-permute-start.7) | collective-permute-done | bytes 81952 | tf_op jit(solution)/shard_map/ppermute | solution.py:25
  37.9 4.2 %collective-permute-done.6.refs_2_ = bf16[80,512]{1,0:T(8,128)(2,1)S(1)} collective-permute-done((bf16[80,512]{1,0:T(8,128)(2,1)}, bf16[80,512]{1,0:T(8,128)(2,1)S(1)}, u32[]{:S(2)}, u32[]{:S(2)}) %collective-permute-start.6) | collective-permute-done | bytes 81952 | tf_op jit(solution)/shard_map/ppermute | solution.py:25
  43.4 1.7 %shard_map.61 = (bf16[256,512]{1,0:T(8,128)(2,1)}, s32[8,256]{1,0:T(8,128)}) custom-call(bf16[80,512]{1,0:T(8,128)(2,1)} %get-tuple-element.29.refs_0_, bf16[80,512]{1,0:T(8,128)(2,1)} %copy-done.12, bf16[80,512]{1,0:T(8,128)(2,1)} %copy-done.11, bf16[80,512]{1,0:T(8,128)(2,1)} %copy-done.10), custom_call_target="tpu_custom_call" | custom-call | tf_op jit(solution)/shard_map/pallas_call | solution.py:235
  45.1 1.1 %collective-permute-start.10 = (bf16[256,512]{1,0:T(8,128)(2,1)}, bf16[256,512]{1,0:T(8,128)(2,1)S(1)}, u32[]{:S(2)}, u32[]{:S(2)}) collective-permute-start(bf16[256,512]{1,0:T(8,128)(2,1)} %get-tuple-element.31.refs_0_), channel_id=1, source_target_pairs={{0,6},{1,7},{2,4},{3,5},{4,2},{5,3},{6,0},{7,1},{8,14},{9,15},{10,... | collective-permute-start | bytes 786440 | tf_op jit(solution)/shard_map/ppermute | solution.py:25
  46.2 2.2 %collective-permute-start.9 = (bf16[256,512]{1,0:T(8,128)(2,1)}, bf16[256,512]{1,0:T(8,128)(2,1)S(1)}, u32[]{:S(2)}, u32[]{:S(2)}) collective-permute-start(bf16[256,512]{1,0:T(8,128)(2,1)} %get-tuple-element.31.refs_0_), channel_id=1, source_target_pairs={{0,4},{1,5},{2,6},{3,7},{4,0},{5,1},{6,2},{7,3},{8,12},{9,13},{10,... | collective-permute-start | bytes 786440 | tf_op jit(solution)/shard_map/ppermute | solution.py:25
  48.6 5.4 %collective-permute-done.10.refs_3_ = bf16[256,512]{1,0:T(8,128)(2,1)S(1)} collective-permute-done((bf16[256,512]{1,0:T(8,128)(2,1)}, bf16[256,512]{1,0:T(8,128)(2,1)S(1)}, u32[]{:S(2)}, u32[]{:S(2)}) %collective-permute-start.10) | collective-permute-done | bytes 262176 | tf_op jit(solution)/shard_map/ppermute | solution.py:25
  54.0 2.7 %collective-permute-done.9.refs_2_ = bf16[256,512]{1,0:T(8,128)(2,1)S(1)} collective-permute-done((bf16[256,512]{1,0:T(8,128)(2,1)}, bf16[256,512]{1,0:T(8,128)(2,1)S(1)}, u32[]{:S(2)}, u32[]{:S(2)}) %collective-permute-start.9) | collective-permute-done | bytes 262176 | tf_op jit(solution)/shard_map/ppermute | solution.py:25
  56.6 0.9 %copy-done.1 = bf16[256,512]{1,0:T(8,128)(2,1)S(1)} copy-done((bf16[256,512]{1,0:T(8,128)(2,1)S(1)}, bf16[256,512]{1,0:T(8,128)(2,1)}, u32[]{:S(2)}) %copy-start.1) | copy-done | bytes 262168
  59.1 2.2 %shard_map.62 = (bf16[64,512]{1,0:T(8,128)(2,1)}, f32[64,512]{1,0:T(8,128)S(1)}, bf16[64,512]{1,0:T(8,128)(2,1)S(1)}) custom-call(s32[8,256]{1,0:T(8,128)S(1)} %copy-done.6, bf16[64,512]{1,0:T(8,128)(2,1)S(1)} %copy-done.3, bf16[256,512]{1,0:T(8,128)(2,1)S(1)} %copy-done.1, bf16[256,512]{1,0:T(8,128)(2,1)S(1)} %collective-permute-done.8.refs_1_, ...), custom_call_target="tpu_custom_call" | custom-call | tf_op jit(solution)/shard_map/pallas_call | solution.py:279
  61.4 1.3 %collective-permute-done.11 = bf16[64,512]{1,0:T(8,128)(2,1)S(1)} collective-permute-done((bf16[64,512]{1,0:T(8,128)(2,1)S(1)}, bf16[64,512]{1,0:T(8,128)(2,1)S(1)}, u32[]{:S(2)}, u32[]{:S(2)}) %collective-permute-start.11) | collective-permute-done | bytes 65568 | tf_op jit(solution)/shard_map/ppermute | solution.py:25
  (37 shorter events, 7.7 us)
Async XLA Ops:
  1.4 1.9 %copy-start = (bf16[3072,512]{1,0:T(8,128)(2,1)S(1)}, bf16[3072,512]{1,0:T(8,128)(2,1)}, u32[]{:S(2)}) copy-start(bf16[3072,512]{1,0:T(8,128)(2,1)} %rows_ref.1) | copy-start | bytes 9437188
  3.3 0.7 %copy-start.4 = (s32[3072]{0:T(1024)S(1)}, s32[3072]{0:T(1024)}, u32[]{:S(2)}) copy-start(s32[3072]{0:T(1024)} %param.4) | copy-start | bytes 36868
  6.7 0.7 %copy-start.2 = (f32[128,512]{1,0:T(8,128)}, f32[128,512]{1,0:T(8,128)S(1)}, u32[]{:S(2)}) copy-start(f32[128,512]{1,0:T(8,128)S(1)} %get-tuple-element.19.own) | copy-start | bytes 786436
  8.0 7.2 %collective-permute-start = (bf16[144,512]{1,0:T(8,128)(2,1)S(1)}, bf16[144,512]{1,0:T(8,128)(2,1)S(1)}, u32[]{:S(2)}, u32[]{:S(2)}) collective-permute-start(bf16[144,512]{1,0:T(8,128)(2,1)S(1)} %get-tuple-element.21), channel_id=1, source_target_pairs={{0,2},{1,3},{2,0},{3,1},{4,6},{5,7},{6,4},{7,5},{8,10},{9,11},{10,... | collective-permute-start | bytes 442376 | tf_op jit(solution)/shard_map/ppermute | solution.py:25
  10.9 8.5 %collective-permute-start.1 = (bf16[144,512]{1,0:T(8,128)(2,1)S(1)}, bf16[144,512]{1,0:T(8,128)(2,1)S(1)}, u32[]{:S(2)}, u32[]{:S(2)}) collective-permute-start(bf16[144,512]{1,0:T(8,128)(2,1)S(1)} %get-tuple-element.22), channel_id=1, source_target_pairs={{0,4},{1,5},{2,6},{3,7},{4,0},{5,1},{6,2},{7,3},{8,12},{9,13},{10,... | collective-permute-start | bytes 442376 | tf_op jit(solution)/shard_map/ppermute | solution.py:25
  12.4 7.0 %collective-permute-start.2 = (bf16[144,512]{1,0:T(8,128)(2,1)S(1)}, bf16[144,512]{1,0:T(8,128)(2,1)S(1)}, u32[]{:S(2)}, u32[]{:S(2)}) collective-permute-start(bf16[144,512]{1,0:T(8,128)(2,1)S(1)} %get-tuple-element.23), channel_id=1, source_target_pairs={{0,6},{1,7},{2,4},{3,5},{4,2},{5,3},{6,0},{7,1},{8,14},{9,15},{10,... | collective-permute-start | bytes 442376 | tf_op jit(solution)/shard_map/ppermute | solution.py:25
  15.2 4.2 %copy-start.7 = (bf16[144,512]{1,0:T(8,128)(2,1)}, bf16[144,512]{1,0:T(8,128)(2,1)S(1)}, u32[]{:S(2)}) copy-start(bf16[144,512]{1,0:T(8,128)(2,1)S(1)} %collective-permute-done.one) | copy-start | bytes 442372
  19.4 0.7 %copy-start.8 = (bf16[144,512]{1,0:T(8,128)(2,1)}, bf16[144,512]{1,0:T(8,128)(2,1)S(1)}, u32[]{:S(2)}) copy-start(bf16[144,512]{1,0:T(8,128)(2,1)S(1)} %collective-permute-done.1.two) | copy-start | bytes 442372
  19.4 0.7 %copy-start.9 = (bf16[144,512]{1,0:T(8,128)(2,1)}, bf16[144,512]{1,0:T(8,128)(2,1)S(1)}, u32[]{:S(2)}) copy-start(bf16[144,512]{1,0:T(8,128)(2,1)S(1)} %collective-permute-done.2.three) | copy-start | bytes 442372
  22.0 6.6 %collective-permute-start.3 = (bf16[80,512]{1,0:T(8,128)(2,1)}, bf16[80,512]{1,0:T(8,128)(2,1)S(1)}, u32[]{:S(2)}, u32[]{:S(2)}) collective-permute-start(bf16[80,512]{1,0:T(8,128)(2,1)} %get-tuple-element.26), channel_id=1, source_target_pairs={{0,8},{1,9},{2,10},{3,11},{4,12},{5,13},{6,14},{7,15},{8,16},{9,17... | collective-permute-start | bytes 245768 | tf_op jit(solution)/shard_map/ppermute | solution.py:25
  23.6 7.2 %collective-permute-start.4 = (bf16[80,512]{1,0:T(8,128)(2,1)}, bf16[80,512]{1,0:T(8,128)(2,1)S(1)}, u32[]{:S(2)}, u32[]{:S(2)}) collective-permute-start(bf16[80,512]{1,0:T(8,128)(2,1)} %get-tuple-element.27), channel_id=1, source_target_pairs={{0,16},{1,17},{2,18},{3,19},{4,20},{5,21},{6,22},{7,23},{8,24},{9,... | collective-permute-start | bytes 245768 | tf_op jit(solution)/shard_map/ppermute | solution.py:25
  28.6 2.2 %copy-start.13 = (bf16[80,512]{1,0:T(8,128)(2,1)}, bf16[80,512]{1,0:T(8,128)(2,1)S(1)}, u32[]{:S(2)}) copy-start(bf16[80,512]{1,0:T(8,128)(2,1)S(1)} %collective-permute-done.3.one) | copy-start | bytes 245764
  30.8 0.6 %copy-start.14 = (bf16[80,512]{1,0:T(8,128)(2,1)}, bf16[80,512]{1,0:T(8,128)(2,1)S(1)}, u32[]{:S(2)}) copy-start(bf16[80,512]{1,0:T(8,128)(2,1)S(1)} %collective-permute-done.4.two) | copy-start | bytes 245764
  33.3 4.7 %collective-permute-start.7 = (bf16[80,512]{1,0:T(8,128)(2,1)}, bf16[80,512]{1,0:T(8,128)(2,1)S(1)}, u32[]{:S(2)}, u32[]{:S(2)}) collective-permute-start(bf16[80,512]{1,0:T(8,128)(2,1)} %get-tuple-element.29.refs_0_), channel_id=1, source_target_pairs={{0,24},{1,25},{2,26},{3,27},{4,28},{5,29},{6,30},{7,31},{8,0},{9,1... | collective-permute-start | bytes 245768 | tf_op jit(solution)/shard_map/ppermute | solution.py:25
  35.3 6.9 %collective-permute-start.6 = (bf16[80,512]{1,0:T(8,128)(2,1)}, bf16[80,512]{1,0:T(8,128)(2,1)S(1)}, u32[]{:S(2)}, u32[]{:S(2)}) collective-permute-start(bf16[80,512]{1,0:T(8,128)(2,1)} %get-tuple-element.29.refs_0_), channel_id=1, source_target_pairs={{0,16},{1,17},{2,18},{3,19},{4,20},{5,21},{6,22},{7,23},{8,24},{9,... | collective-permute-start | bytes 245768 | tf_op jit(solution)/shard_map/ppermute | solution.py:25
  35.3 6.9 %collective-permute-start.5 = (bf16[80,512]{1,0:T(8,128)(2,1)}, bf16[80,512]{1,0:T(8,128)(2,1)S(1)}, u32[]{:S(2)}, u32[]{:S(2)}) collective-permute-start(bf16[80,512]{1,0:T(8,128)(2,1)} %get-tuple-element.29.refs_0_), channel_id=1, source_target_pairs={{0,8},{1,9},{2,10},{3,11},{4,12},{5,13},{6,14},{7,15},{8,16},{9,17... | collective-permute-start | bytes 245768 | tf_op jit(solution)/shard_map/ppermute | solution.py:25
  37.9 4.2 %copy-start.10 = (bf16[80,512]{1,0:T(8,128)(2,1)}, bf16[80,512]{1,0:T(8,128)(2,1)S(1)}, u32[]{:S(2)}) copy-start(bf16[80,512]{1,0:T(8,128)(2,1)S(1)} %collective-permute-done.7.refs_3_) | copy-start | bytes 245764
  45.1 8.9 %collective-permute-start.10 = (bf16[256,512]{1,0:T(8,128)(2,1)}, bf16[256,512]{1,0:T(8,128)(2,1)S(1)}, u32[]{:S(2)}, u32[]{:S(2)}) collective-permute-start(bf16[256,512]{1,0:T(8,128)(2,1)} %get-tuple-element.31.refs_0_), channel_id=1, source_target_pairs={{0,6},{1,7},{2,4},{3,5},{4,2},{5,3},{6,0},{7,1},{8,14},{9,15},{10,... | collective-permute-start | bytes 786440 | tf_op jit(solution)/shard_map/ppermute | solution.py:25
  46.2 10.4 %collective-permute-start.9 = (bf16[256,512]{1,0:T(8,128)(2,1)}, bf16[256,512]{1,0:T(8,128)(2,1)S(1)}, u32[]{:S(2)}, u32[]{:S(2)}) collective-permute-start(bf16[256,512]{1,0:T(8,128)(2,1)} %get-tuple-element.31.refs_0_), channel_id=1, source_target_pairs={{0,4},{1,5},{2,6},{3,7},{4,0},{5,1},{6,2},{7,3},{8,12},{9,13},{10,... | collective-permute-start | bytes 786440 | tf_op jit(solution)/shard_map/ppermute | solution.py:25
  48.4 8.2 %collective-permute-start.8 = (bf16[256,512]{1,0:T(8,128)(2,1)}, bf16[256,512]{1,0:T(8,128)(2,1)S(1)}, u32[]{:S(2)}, u32[]{:S(2)}) collective-permute-start(bf16[256,512]{1,0:T(8,128)(2,1)} %get-tuple-element.31.refs_0_), channel_id=1, source_target_pairs={{0,2},{1,3},{2,0},{3,1},{4,6},{5,7},{6,4},{7,5},{8,10},{9,11},{10,... | collective-permute-start | bytes 786440 | tf_op jit(solution)/shard_map/ppermute | solution.py:25
  56.6 1.0 %copy-start.1 = (bf16[256,512]{1,0:T(8,128)(2,1)S(1)}, bf16[256,512]{1,0:T(8,128)(2,1)}, u32[]{:S(2)}) copy-start(bf16[256,512]{1,0:T(8,128)(2,1)} %get-tuple-element.31.refs_0_) | copy-start | bytes 786436
  57.6 0.8 %copy-start.3 = (bf16[64,512]{1,0:T(8,128)(2,1)S(1)}, bf16[64,512]{1,0:T(8,128)(2,1)}, u32[]{:S(2)}) copy-start(bf16[64,512]{1,0:T(8,128)(2,1)} %get-tuple-element.16.mean) | copy-start | bytes 196612
  58.4 0.7 %copy-start.6 = (s32[8,256]{1,0:T(8,128)S(1)}, s32[8,256]{1,0:T(8,128)}, u32[]{:S(2)}) copy-start(s32[8,256]{1,0:T(8,128)} %get-tuple-element.30.ids) | copy-start | bytes 24580
  61.3 1.3 %collective-permute-start.11 = (bf16[64,512]{1,0:T(8,128)(2,1)S(1)}, bf16[64,512]{1,0:T(8,128)(2,1)S(1)}, u32[]{:S(2)}, u32[]{:S(2)}) collective-permute-start(bf16[64,512]{1,0:T(8,128)(2,1)S(1)} %get-tuple-element.34), channel_id=1, source_target_pairs={{0,1},{1,0},{2,3},{3,2},{4,5},{5,4},{6,7},{7,6},{8,9},{9,8},{10,11... | collective-permute-start | bytes 196616 | tf_op jit(solution)/shard_map/ppermute | solution.py:25
  (3 other events, 1.9 us)

commit v2 on v1

v2 whole, which is shorter than its diff:
```python
import functools

import jax
import jax.numpy as jnp
from jax import lax
from jax.experimental import pallas as pl
from jax.experimental.pallas import tpu as pltpu
from jax.sharding import PartitionSpec as P

BAND = 8
K2 = 1024
GROUP = 4
META = 16
BASE = 256
LANES = 128
BF16 = jnp.bfloat16
F32 = jnp.float32


def small():
    return pltpu.CompilerParams(vmem_limit_bytes=16 * 2**20)


def whole():
    return pl.BlockSpec(memory_space=pltpu.VMEM)


def exchanged(value, pairs):
    return lax.ppermute(value, ("dp", "mp"), pairs)


def iota(shape, dim):
    return lax.broadcasted_iota(jnp.int32, shape, dim)


def split_digits(row):
    high = jnp.floor(row * (1.0 / BASE))
    return high, row - high * BASE


def as_column(row, cent):
    hit = iota((cent, LANES), 0) == iota((cent, LANES), 1)
    return jnp.sum(jnp.where(hit, row, 0.0), axis=1, keepdims=True)


def as_row(column):
    rows = column.shape[0]
    hit = iota((rows, LANES), 0) == iota((rows, LANES), 1)
    return jnp.sum(jnp.where(hit, column, 0.0), axis=0, keepdims=True)


def one_hot_of(rows, label):
    hit = lax.broadcasted_iota(jnp.int16, (rows, label.shape[1]), 0) == label.astype(jnp.int16)
    return jnp.where(hit, jnp.ones((), BF16), jnp.zeros((), BF16))


def sum_kernel(devices, cent, ids_hbm, rows_hbm, group_ref, own_ref, own_meta_ref, *rest):
    sends, (ids_ref, rows_ref, totals, arrived) = rest[:-4], rest[-4:]
    steps, block = rows_ref.shape[:2]
    ids_copy = pltpu.make_async_copy(ids_hbm, ids_ref, arrived.at[steps])
    ids_copy.start()
    copies = [
        pltpu.make_async_copy(
            rows_hbm.at[step * block : (step + 1) * block], rows_ref.at[step], arrived.at[step]
        )
        for step in range(steps)
    ]
    for copy in copies:
        copy.start()
    position = lax.axis_index("dp")
    mate = position % GROUP
    labels = 2 * GROUP * cent
    ids_copy.wait()
    tallies = jnp.zeros((labels, LANES), BF16)
    for step in range(steps):
        offset = ids_ref[:, step * block : (step + 1) * block] - position * cent
        offset = jnp.where(offset < 0, offset + devices * cent, offset)
        ahead = offset // cent + mate
        partner = (ahead % GROUP) ^ mate
        slot = jnp.where(ahead // GROUP == 1, 1, 0)
        label = partner * (2 * cent) + slot * cent + offset % cent
        one_hot = one_hot_of(labels, label)
        for start in range(0, block, LANES):
            tallies = tallies + one_hot[:, start : start + LANES]
        copies[step].wait()
        part = jnp.dot(one_hot, rows_ref[step], preferred_element_type=F32)
        if step == 0:
            totals[...] = part
        else:
            totals[...] += part
    id_high, id_low = split_digits(group_ref[...].astype(F32))
    id_digits = jnp.concatenate([id_high, id_low], axis=0)
    counts = lax.dot_general(
        jnp.ones((8, LANES), BF16), tallies, (((1,), (1,)), ((), ())), preferred_element_type=F32
    )
    pair = 2 * cent
    own_ref[...] = totals[:pair]
    for index in range(GROUP):
        high, low = split_digits(counts[:1, index * pair : (index + 1) * pair])
        meta = jnp.concatenate([high, low, jnp.zeros((META - 2, LANES), F32)], axis=0)
        if index == 0:
            own_meta_ref[...] = meta
            own_meta_ref[2:4, :cent] = id_digits
        else:
            send = sends[index - 1]
            send[:pair] = totals[index * pair : (index + 1) * pair].astype(BF16)
            send[pair:, :LANES] = meta.astype(BF16)
            send[pair:, LANES:] = jnp.zeros((META, send.shape[1] - LANES), BF16)
            send[pair + 2 : pair + 4, :cent] = id_digits.astype(BF16)


def band_sums(devices, cent, ids, rows, group):
    count, width = rows.shape
    steps = 4
    block = count // steps
    pair = 2 * cent
    send = jax.ShapeDtypeStruct((pair + META, width), BF16)
    return pl.pallas_call(
        functools.partial(sum_kernel, devices, cent),
        in_specs=[pl.BlockSpec(memory_space=pltpu.HBM)] * 2 + [whole()],
        out_specs=[whole()] * (GROUP + 1),
        out_shape=[
            jax.ShapeDtypeStruct((pair, width), F32),
            jax.ShapeDtypeStruct((META, LANES), F32),
        ]
        + [send] * (GROUP - 1),
        scratch_shapes=[
            pltpu.VMEM((1, count), jnp.int32),
            pltpu.VMEM((steps, block, width), BF16),
            pltpu.VMEM((GROUP * pair, width), F32),
            pltpu.SemaphoreType.DMA((steps + 1,)),
        ],
        compiler_params=small(),
    )(
        pltpu.with_memory_space_constraint(ids.reshape(1, count), pltpu.HBM),
        pltpu.with_memory_space_constraint(rows, pltpu.HBM),
        group.reshape(1, cent),
    )


def group_kernel(cent, own, own_meta, one, two, three, base_ref, base_meta_ref, next_ref, far_ref):
    mate = lax.axis_index("dp") % GROUP
    pair = 2 * cent
    lane = iota((1, LANES), 1)
    near = own[:cent]
    middle = own[cent:]
    far = jnp.zeros_like(near)
    counts = own_meta[0:1] * BASE + own_meta[1:2]
    far_counts = jnp.zeros_like(counts)
    id_digits = [own_meta[2:4]]
    for index, got in ((1, one), (2, two), (3, three)):
        before = (mate ^ index) < mate
        first = got[:cent].astype(F32)
        near = near + jnp.where(before, first, 0.0)
        far = far + jnp.where(before, 0.0, first)
        middle = middle + got[cent:pair].astype(F32)
        meta = got[pair:, :LANES].astype(F32)
        row = meta[0:1] * BASE + meta[1:2]
        mask = (lane >= cent) | before
        counts = counts + jnp.where(mask, row, 0.0)
        far_counts = far_counts + jnp.where(mask, 0.0, row)
        id_digits.append(meta[2:4])
    id_digits = jnp.concatenate(id_digits, axis=0)
    padding = jnp.zeros((META - 2 - 2 * GROUP, LANES), F32)

    def meta_of(row):
        high, low = split_digits(row)
        return jnp.concatenate([high, low, id_digits, padding], axis=0)

    base_ref[...] = near
    base_meta_ref[...] = meta_of(counts)
    for send, sums, row in ((next_ref, middle, counts), (far_ref, far, far_counts)):
        send[:cent] = sums.astype(BF16)
        send[cent:, :LANES] = meta_of(row).astype(BF16)
        send[cent:, LANES:] = jnp.zeros((META, send.shape[1] - LANES), BF16)


def group_sums(cent, own, own_meta, got):
    width = own.shape[1]
    send = jax.ShapeDtypeStruct((cent + META, width), BF16)
    return pl.pallas_call(
        functools.partial(group_kernel, cent),
        in_specs=[whole()] * 5,
        out_specs=[whole()] * 4,
        out_shape=[
            jax.ShapeDtypeStruct((cent, width), F32),
            jax.ShapeDtypeStruct((META, LANES), F32),
            send,
            send,
        ],
        compiler_params=small(),
    )(own, own_meta, *got)


def mean_kernel(cent, base, base_meta, one, two, mean_ref, plain_ref, send_ref):
    sums = base[...] + one[:cent].astype(F32) + two[:cent].astype(F32)
    metas = [base_meta[...], one[cent:, :LANES].astype(F32), two[cent:, :LANES].astype(F32)]
    rows = [meta[0:1] * BASE + meta[1:2] for meta in metas]
    row = rows[0] + pltpu.roll(rows[1], LANES - cent, 1) + rows[2]
    mean = (sums / as_column(row, cent)).astype(BF16)
    mean_ref[...] = mean
    plain_ref[...] = mean
    send_ref[:cent] = mean
    for index, meta in enumerate(metas):
        send_ref[cent:, index * LANES : (index + 1) * LANES] = meta.astype(BF16)
    known = len(metas) * LANES
    send_ref[cent:, known:] = jnp.zeros((META, mean.shape[1] - known), BF16)


def means(cent, base, base_meta, got):
    width = base.shape[1]
    mean = jax.ShapeDtypeStruct((cent, width), BF16)
    return pl.pallas_call(
        functools.partial(mean_kernel, cent),
        in_specs=[whole()] * 4,
        out_specs=[whole()] * 3,
        out_shape=[mean, mean, jax.ShapeDtypeStruct((cent + META, width), BF16)],
        compiler_params=small(),
    )(base, base_meta, *got)


def near_kernel(cent, own, got, near_ref, ids_ref):
    near_ref[:cent] = own[:cent]
    near_ref[cent:] = got[:cent]
    odd = lax.axis_index("dp") // GROUP % 2 == 1
    lane = iota((1, LANES), 1)

    def ids_of(block, steps, index):
        meta = block[cent:, steps * LANES : (steps + 1) * LANES].astype(F32)
        at = 2 + 2 * index
        return meta[at : at + 1] * BASE + meta[at + 1 : at + 2]

    near_rows, far_rows = [], []
    for index in range(GROUP):
        near_rows.append((ids_of(own, 0, index), ids_of(got, 0, index)))
        last = jnp.where(odd, ids_of(got, 2, index), ids_of(own, 1, index))
        far_rows.append((ids_of(own, 2, index), last))
    rows = [
        jnp.where(lane < cent, left, pltpu.roll(right, cent, 1))
        for left, right in near_rows + far_rows
    ]
    ids_ref[...] = jnp.concatenate(rows, axis=0).astype(jnp.int32)


def near_rows(cent, own, got):
    width = own.shape[1]
    return pl.pallas_call(
        functools.partial(near_kernel, cent),
        in_specs=[whole()] * 2,
        out_specs=[whole()] * 2,
        out_shape=[
            jax.ShapeDtypeStruct((2 * cent, width), BF16),
            jax.ShapeDtypeStruct((2 * GROUP, LANES), jnp.int32),
        ],
        compiler_params=small(),
    )(own, got)


def far_kernel(first, second, far_ref):
    rows = first.shape[0]
    far_ref[:rows] = first[...]
    far_ref[rows:] = second[...]


def far_rows(first, second):
    rows, width = first.shape
    return pl.pallas_call(
        far_kernel,
        in_specs=[whole()] * 2,
        out_specs=whole(),
        out_shape=jax.ShapeDtypeStruct((2 * rows, width), BF16),
        compiler_params=small(),
    )(first, second)


def ids_row(ids, base, order):
    low = lax.axis_index("mp") == 0
    first = ids[base + order : base + order + 1]
    if order in (0, GROUP - 1):
        return first
    other = ids[base + GROUP - 1 - order : base + GROUP - order]
    return jnp.where(low, first, other)


def gather_kernel(ids, *refs):
    blocks, (sums_ref, tally_ref) = refs[:-2], refs[-2:]
    tally = jnp.zeros((K2, LANES), BF16)
    labels = [ids_row(ids, 0, order) for order in range(GROUP)]
    labels += [ids_row(ids, GROUP, order) for order in range(GROUP - 1)]
    total = None
    for label, block in zip(labels, blocks):
        one_hot = one_hot_of(K2, label)
        tally = tally + one_hot
        part = jnp.dot(one_hot, block[...], preferred_element_type=F32)
        total = part if total is None else total + part
    sums_ref[...] = total
    tally_ref[...] = tally


def gathered_sums(ids, blocks):
    width = blocks[0].shape[1]
    return pl.pallas_call(
        gather_kernel,
        in_specs=[whole()] * (1 + len(blocks)),
        out_specs=[whole()] * 2,
        out_shape=[
            jax.ShapeDtypeStruct((K2, width), F32),
            jax.ShapeDtypeStruct((K2, LANES), BF16),
        ],
        compiler_params=small(),
    )(ids, *blocks)


def score_kernel(owned, ids, mean, sums, tally, block, second_ref, keep_ref, send_ref, values_ref):
    one_hot = one_hot_of(K2, ids_row(ids, GROUP, GROUP - 1))
    count = jnp.sum((tally[...] + one_hot).astype(F32), axis=1, keepdims=True)
    total = sums[...] + jnp.dot(one_hot, block[...], preferred_element_type=F32)
    second = (total * (1.0 / count)).astype(BF16)
    values = second.astype(F32)
    values_ref[...] = values
    start = pl.multiple_of(lax.axis_index("dp") * owned, owned)
    second_ref[...] = values_ref[pl.ds(start, owned)].astype(BF16)
    norms = 0.5 * jnp.sum(values * values, axis=1, keepdims=True)
    row = jnp.concatenate(
        [as_row(norms[at : at + LANES]) for at in range(0, K2, LANES)], axis=1
    )
    products = lax.dot_general(
        mean[...], second, (((1,), (1,)), ((), ())), preferred_element_type=F32
    )
    scores = products - row
    half = K2 // 2
    low = lax.axis_index("mp") == 0
    keep_ref[...] = jnp.where(low, scores[:, :half], scores[:, half:])
    send_ref[...] = jnp.where(low, scores[:, half:], scores[:, :half]).astype(BF16)


def second_level_scores(owned, ids, mean, sums, tally, block):
    cent, width = mean.shape
    return pl.pallas_call(
        functools.partial(score_kernel, owned),
        in_specs=[whole()] * 5,
        out_specs=[whole()] * 3,
        out_shape=[
            jax.ShapeDtypeStruct((owned, width), BF16),
            jax.ShapeDtypeStruct((cent, K2 // 2), F32),
            jax.ShapeDtypeStruct((cent, K2 // 2), BF16),
        ],
        scratch_shapes=[pltpu.VMEM((K2, width), F32)],
        compiler_params=small(),
    )(ids, mean, sums, tally, block)


def summed_scores(devices, second_level, first_centroids):
    second_ids = jnp.arange(K2, dtype=jnp.int32)
    group_hot = (second_level == second_ids[None, :]).astype(BF16)
    group_totals = jnp.einsum("ck,cd->kd", group_hot, first_centroids, preferred_element_type=F32)
    group_counts = jnp.sum(group_hot.astype(F32), axis=0)
    total, total_counts = lax.psum((group_totals, group_counts), "dp")
    every = (total / total_counts[:, None]).astype(BF16)
    owned = K2 // devices
    second = lax.dynamic_slice_in_dim(every, lax.axis_index("dp") * owned, owned, 0)
    values = every.astype(F32)
    products = jnp.einsum("cd,kd->ck", first_centroids, every, preferred_element_type=F32)
    partial_value = products - 0.5 * jnp.sum(values * values, axis=1)[None, :]
    scores = lax.psum_scatter(
        partial_value.astype(BF16), "mp", scatter_dimension=1, tiled=True
    ).astype(F32)
    return second, scores


def shards(embeddings, first_level, second_level):
    devices = lax.axis_size("dp")
    cores = lax.axis_size("mp")
    cent = second_level.shape[0]
    everyone = [(d, c) for d in range(devices) for c in range(cores)]

    def partner(value, index):
        return exchanged(value, [(d * cores + c, (d ^ index) * cores + c) for d, c in everyone])

    def ahead(value, steps):
        return exchanged(
            value, [(d * cores + c, (d + steps) % devices * cores + c) for d, c in everyone]
        )

    own, own_meta, *sends = band_sums(devices, cent, first_level, embeddings, second_level)
    got = [partner(send, index + 1) for index, send in enumerate(sends)]
    base, base_meta, following, far = group_sums(cent, own, own_meta, got)
    got = [ahead(following, GROUP), ahead(far, 2 * GROUP)]
    mean, plain, send = means(cent, base, base_meta, got)
    if devices != GROUP * GROUP or cores != 2 or devices * cent > K2:
        return (mean, *summed_scores(devices, second_level, mean))

    def sideways(value, steps):
        return exchanged(
            value, [(d * cores + c, (d ^ steps[c]) * cores + c) for d, c in everyone]
        )

    def plane_rows(value):
        first = sideways(value, (1, 2))
        second = sideways(value, (2, 1))
        return [value, first, second, sideways(first, (2, 1))]

    near, ids = near_rows(cent, send, partner(send, GROUP))
    far = far_rows(partner(plain, 2 * GROUP), partner(plain, 3 * GROUP))
    *blocks, last = plane_rows(near) + plane_rows(far)
    sums, tally = gathered_sums(ids, blocks)
    second, keep, send = second_level_scores(K2 // devices, ids, plain, sums, tally, last)
    got = exchanged(send, [(d * cores + c, d * cores + (c ^ 1)) for d, c in everyone])
    return mean, second, keep + got.astype(F32)


def solution(mesh):
    placed = (P("dp", "mp"), P("dp"), P("dp", None))
    return jax.shard_map(
        shards,
        mesh=mesh,
        in_specs=placed,
        out_specs=(P("dp", "mp"), P("dp", "mp"), P("dp", "mp")),
        check_vma=False,
    )
```

time: 63.7 us -> 49.2 us (0.77)
  local copies, waits for them, and re-layouts: 9.71 us -> 0.65 us
  waiting for transfers between devices: 26.6 us -> 21.3 us
  starting transfers between devices: 15.2 us -> 18.1 us
  Pallas kernels: 10.4 us -> 7.54 us
    unnamed x31 -> x2, local copies, waits for them, and re-layouts: 9.71 us -> 0.65 us
    ppermute x12 -> x15, waiting for transfers between devices: 26.6 us -> 21.3 us  [exchanged(): return lax.ppermute(value, ('dp', 'mp'), pairs)]
    ppermute x12 -> x15, starting transfers between devices: 15.2 us -> 18.1 us  [exchanged(): return lax.ppermute(value, ('dp', 'mp'), pairs)]
    pallas_call x1, Pallas kernels: 1.91 us -> 0.13 us  [group_sums(): pl.pallas_call(functools.partial(group_kernel, cent), in_specs=[whole()]...]
    pallas_call x1, Pallas kernels: 1.83 us -> 0.8 us  [means(): pl.pallas_call(functools.partial(mean_kernel, cent), in_specs=[whole()] *...]
    pallas_call x1, Pallas kernels: 2.22 us -> 1.23 us  [second_level_scores(): pl.pallas_call(functools.partial(score_kernel, owned), in_specs=[whole()]...]
    pallas_call x2 -> x4, Pallas kernels: 4.43 us -> 5.38 us  [the longest x1 3.25 us: band_sums(): pl.pallas_call(functools.partial(sum_kernel, devices, cent), in_specs=[pl...]
  transfers between devices with their start and end apart: 12 -> 15, of which waited for: 9 -> 12; matrix products, arithmetic and copies ran while one was open for 0% -> 0% of each run, Pallas kernels for 0% -> 4%
where the time goes in v2:
time: 49.2 us; the launch traced here: 48.9 us
  waiting for transfers between devices  21.3 us (43%)
  starting transfers between devices  18.1 us (37%)
  Pallas kernels  7.54 us (15%)
  between operations  0.68 us (1%)
  other arithmetic  0.67 us (1%)
  local copies, waits for them, and re-layouts  0.65 us (1%)
    ppermute x15, waiting for transfers between devices, exchanged(): return lax.ppermute(value, ('dp', 'mp'), pairs)  21.3 us
    ppermute x15, starting transfers between devices, exchanged(): return lax.ppermute(value, ('dp', 'mp'), pairs)  18.1 us
    pallas_call x1, Pallas kernels, band_sums(): pl.pallas_call(functools.partial(sum_kernel, devices, cent), in_specs=[pl...  3.25 us
    pallas_call x1, Pallas kernels, gathered_sums(): pl.pallas_call(gather_kernel, in_specs=[whole()] * (1 + len(blocks)), out...  2.03 us
    pallas_call x1, Pallas kernels, second_level_scores(): pl.pallas_call(functools.partial(score_kernel, owned), in_specs=[whole()]...  1.23 us
  transfers between devices with their start and end apart: 15, of which 12 were waited for; matrix products, arithmetic and copies ran while one was open for 0% of the time, Pallas kernels for 4%

profile of v2, /device:TPU:0, one launch (start us, length us, event | category | flops | bytes accessed | tf_op | source)
XLA Modules:
  0.0 48.9 jit_solution(4293657546091648249)
XLA Ops:
  1.3 3.2 %shard_map.58 = (f32[128,512]{1,0:T(8,128)S(1)}, f32[16,128]{1,0:T(8,128)S(1)}, bf16[144,512]{1,0:T(8,128)(2,1)S(1)}, bf16[144,512]{1,0:T(8,128)(2,1)S(1)}, bf16[144,512]{1,0:T(8,128)(2,1)S(1)}) custom-call(s32[1,3072]{1,0:T(1,128)} %bitcast.3, bf16[3072,512]{1,0:T(8,128)(2,1)} %rows_hbm.1, s32[1,64]{1,0:T(1,128)S(1)} %bitcast.2), custom_call_target="tpu_custom_call" | custom-call | tf_op jit(solution)/shard_map/pallas_call | solution.py:118
  4.5 3.0 %collective-permute-start = (bf16[144,512]{1,0:T(8,128)(2,1)S(1)}, bf16[144,512]{1,0:T(8,128)(2,1)S(1)}, u32[]{:S(2)}, u32[]{:S(2)}) collective-permute-start(bf16[144,512]{1,0:T(8,128)(2,1)S(1)} %get-tuple-element.24), channel_id=1, source_target_pairs={{0,2},{1,3},{2,0},{3,1},{4,6},{5,7},{6,4},{7,5},{8,10},{9,11},{10,... | collective-permute-start | bytes 442376 | tf_op jit(solution)/shard_map/ppermute | solution.py:29
  7.5 1.5 %collective-permute-start.1 = (bf16[144,512]{1,0:T(8,128)(2,1)S(1)}, bf16[144,512]{1,0:T(8,128)(2,1)S(1)}, u32[]{:S(2)}, u32[]{:S(2)}) collective-permute-start(bf16[144,512]{1,0:T(8,128)(2,1)S(1)} %get-tuple-element.25), channel_id=1, source_target_pairs={{0,4},{1,5},{2,6},{3,7},{4,0},{5,1},{6,2},{7,3},{8,12},{9,13},{10,... | collective-permute-start | bytes 442376 | tf_op jit(solution)/shard_map/ppermute | solution.py:29
  9.1 2.8 %collective-permute-done.one = bf16[144,512]{1,0:T(8,128)(2,1)S(1)} collective-permute-done((bf16[144,512]{1,0:T(8,128)(2,1)S(1)}, bf16[144,512]{1,0:T(8,128)(2,1)S(1)}, u32[]{:S(2)}, u32[]{:S(2)}) %collective-permute-start) | collective-permute-done | bytes 147488 | tf_op jit(solution)/shard_map/ppermute | solution.py:29
  11.8 4.2 %collective-permute-done.1.two = bf16[144,512]{1,0:T(8,128)(2,1)S(1)} collective-permute-done((bf16[144,512]{1,0:T(8,128)(2,1)S(1)}, bf16[144,512]{1,0:T(8,128)(2,1)S(1)}, u32[]{:S(2)}, u32[]{:S(2)}) %collective-permute-start.1) | collective-permute-done | bytes 147488 | tf_op jit(solution)/shard_map/ppermute | solution.py:29
  16.2 1.6 %collective-permute-start.3 = (bf16[80,512]{1,0:T(8,128)(2,1)S(1)}, bf16[80,512]{1,0:T(8,128)(2,1)S(1)}, u32[]{:S(2)}, u32[]{:S(2)}) collective-permute-start(bf16[80,512]{1,0:T(8,128)(2,1)S(1)} %get-tuple-element.29), channel_id=1, source_target_pairs={{0,8},{1,9},{2,10},{3,11},{4,12},{5,13},{6,14},{7,15},{8,16},{9,17... | collective-permute-start | bytes 245768 | tf_op jit(solution)/shard_map/ppermute | solution.py:29
  17.8 2.6 %collective-permute-start.4 = (bf16[80,512]{1,0:T(8,128)(2,1)S(1)}, bf16[80,512]{1,0:T(8,128)(2,1)S(1)}, u32[]{:S(2)}, u32[]{:S(2)}) collective-permute-start(bf16[80,512]{1,0:T(8,128)(2,1)S(1)} %get-tuple-element.30), channel_id=1, source_target_pairs={{0,16},{1,17},{2,18},{3,19},{4,20},{5,21},{6,22},{7,23},{8,24},{9,... | collective-permute-start | bytes 245768 | tf_op jit(solution)/shard_map/ppermute | solution.py:29
  20.4 2.3 %collective-permute-done.3.one = bf16[80,512]{1,0:T(8,128)(2,1)S(1)} collective-permute-done((bf16[80,512]{1,0:T(8,128)(2,1)S(1)}, bf16[80,512]{1,0:T(8,128)(2,1)S(1)}, u32[]{:S(2)}, u32[]{:S(2)}) %collective-permute-start.3) | collective-permute-done | bytes 81952 | tf_op jit(solution)/shard_map/ppermute | solution.py:29
  22.7 2.1 %collective-permute-done.4.two = bf16[80,512]{1,0:T(8,128)(2,1)S(1)} collective-permute-done((bf16[80,512]{1,0:T(8,128)(2,1)S(1)}, bf16[80,512]{1,0:T(8,128)(2,1)S(1)}, u32[]{:S(2)}, u32[]{:S(2)}) %collective-permute-start.4) | collective-permute-done | bytes 81952 | tf_op jit(solution)/shard_map/ppermute | solution.py:29
  24.8 0.8 %shard_map.60 = (bf16[64,512]{1,0:T(8,128)(2,1)}, bf16[64,512]{1,0:T(8,128)(2,1)S(1)}, bf16[80,512]{1,0:T(8,128)(2,1)S(1)}) custom-call(f32[64,512]{1,0:T(8,128)S(1)} %get-tuple-element.27.base, f32[16,128]{1,0:T(8,128)S(1)} %get-tuple-element.28.base_meta, bf16[80,512]{1,0:T(8,128)(2,1)S(1)} %collective-permute-done.3.one, ...), custom_call_target="tpu_custom_call" | custom-call | tf_op jit(solution)/shard_map/pallas_call | solution.py:213
  25.6 2.5 %collective-permute-start.9 = (bf16[64,512]{1,0:T(8,128)(2,1)S(1)}, bf16[64,512]{1,0:T(8,128)(2,1)S(1)}, u32[]{:S(2)}, u32[]{:S(2)}) collective-permute-start(bf16[64,512]{1,0:T(8,128)(2,1)S(1)} %get-tuple-element.34.mean), channel_id=1, source_target_pairs={{0,16},{1,17},{2,18},{3,19},{4,20},{5,21},{6,22},{7,23},{8,24},{9,... | collective-permute-start | bytes 196616 | tf_op jit(solution)/shard_map/ppermute | solution.py:29
  28.1 1.9 %collective-permute-start.10 = (bf16[64,512]{1,0:T(8,128)(2,1)S(1)}, bf16[64,512]{1,0:T(8,128)(2,1)S(1)}, u32[]{:S(2)}, u32[]{:S(2)}) collective-permute-start(bf16[64,512]{1,0:T(8,128)(2,1)S(1)} %get-tuple-element.34.mean), channel_id=1, source_target_pairs={{0,24},{1,25},{2,26},{3,27},{4,28},{5,29},{6,30},{7,31},{8,16},{9,... | collective-permute-start | bytes 196616 | tf_op jit(solution)/shard_map/ppermute | solution.py:29
  30.4 1.4 %collective-permute-start.6 = (bf16[128,512]{1,0:T(8,128)(2,1)S(1)}, bf16[128,512]{1,0:T(8,128)(2,1)S(1)}, u32[]{:S(2)}, u32[]{:S(2)}) collective-permute-start(bf16[128,512]{1,0:T(8,128)(2,1)S(1)} %get-tuple-element.35.refs_0_), channel_id=1, source_target_pairs={{0,2},{1,5},{2,0},{3,7},{4,6},{5,1},{6,4},{7,3},{8,10},{9,13},{10,... | collective-permute-start | bytes 393224 | tf_op jit(solution)/shard_map/ppermute | solution.py:29
  31.8 1.1 %collective-permute-done.9.first = bf16[64,512]{1,0:T(8,128)(2,1)S(1)} collective-permute-done((bf16[64,512]{1,0:T(8,128)(2,1)S(1)}, bf16[64,512]{1,0:T(8,128)(2,1)S(1)}, u32[]{:S(2)}, u32[]{:S(2)}) %collective-permute-start.9) | collective-permute-done | bytes 65568 | tf_op jit(solution)/shard_map/ppermute | solution.py:29
  32.9 1.4 %collective-permute-done.10.second = bf16[64,512]{1,0:T(8,128)(2,1)S(1)} collective-permute-done((bf16[64,512]{1,0:T(8,128)(2,1)S(1)}, bf16[64,512]{1,0:T(8,128)(2,1)S(1)}, u32[]{:S(2)}, u32[]{:S(2)}) %collective-permute-start.10) | collective-permute-done | bytes 65568 | tf_op jit(solution)/shard_map/ppermute | solution.py:29
  34.3 1.3 %collective-permute-start.11 = (bf16[128,512]{1,0:T(8,128)(2,1)S(1)}, bf16[128,512]{1,0:T(8,128)(2,1)S(1)}, u32[]{:S(2)}, u32[]{:S(2)}) collective-permute-start(bf16[128,512]{1,0:T(8,128)(2,1)S(1)} %shard_map.62.refs_4_), channel_id=1, source_target_pairs={{0,2},{1,5},{2,0},{3,7},{4,6},{5,1},{6,4},{7,3},{8,10},{9,13},{10,... | collective-permute-start | bytes 393224 | tf_op jit(solution)/shard_map/ppermute | solution.py:29
  35.6 2.0 %collective-permute-start.7 = (bf16[128,512]{1,0:T(8,128)(2,1)S(1)}, bf16[128,512]{1,0:T(8,128)(2,1)S(1)}, u32[]{:S(2)}, u32[]{:S(2)}) collective-permute-start(bf16[128,512]{1,0:T(8,128)(2,1)S(1)} %get-tuple-element.35.refs_0_), channel_id=1, source_target_pairs={{0,4},{1,3},{2,6},{3,1},{4,0},{5,7},{6,2},{7,5},{8,12},{9,11},{10,... | collective-permute-start | bytes 393224 | tf_op jit(solution)/shard_map/ppermute | solution.py:29
  37.7 3.1 %collective-permute-done.11.refs_5_ = bf16[128,512]{1,0:T(8,128)(2,1)S(1)} collective-permute-done((bf16[128,512]{1,0:T(8,128)(2,1)S(1)}, bf16[128,512]{1,0:T(8,128)(2,1)S(1)}, u32[]{:S(2)}, u32[]{:S(2)}) %collective-permute-start.11) | collective-permute-done | bytes 131104 | tf_op jit(solution)/shard_map/ppermute | solution.py:29
  41.0 1.0 %collective-permute-done.7.refs_2_ = bf16[128,512]{1,0:T(8,128)(2,1)S(1)} collective-permute-done((bf16[128,512]{1,0:T(8,128)(2,1)S(1)}, bf16[128,512]{1,0:T(8,128)(2,1)S(1)}, u32[]{:S(2)}, u32[]{:S(2)}) %collective-permute-start.7) | collective-permute-done | bytes 131104 | tf_op jit(solution)/shard_map/ppermute | solution.py:29
  42.0 1.4 %collective-permute-done.8.refs_3_ = bf16[128,512]{1,0:T(8,128)(2,1)S(1)} collective-permute-done((bf16[128,512]{1,0:T(8,128)(2,1)S(1)}, bf16[128,512]{1,0:T(8,128)(2,1)S(1)}, u32[]{:S(2)}, u32[]{:S(2)}) %collective-permute-start.8) | collective-permute-done | bytes 131104 | tf_op jit(solution)/shard_map/ppermute | solution.py:29
  43.4 2.0 %shard_map.63 = (f32[1024,512]{1,0:T(8,128)S(1)}, bf16[1024,128]{1,0:T(8,128)(2,1)S(1)}) custom-call(s32[8,128]{1,0:T(8,128)S(1)} %get-tuple-element.33.ids, bf16[128,512]{1,0:T(8,128)(2,1)S(1)} %get-tuple-element.35.refs_0_, bf16[128,512]{1,0:T(8,128)(2,1)S(1)} %collective-permute-done.6.refs_1_, bf16[128,512]{1,0:T(8,128)(2,1)S(1)} %collective-permute-done.7.refs_2_, ...), custom_call_target="tpu_custom_call" | custom-call | tf_op jit(solution)/shard_map/pallas_call | solution.py:302
  45.8 1.2 %shard_map.64 = (bf16[64,512]{1,0:T(8,128)(2,1)}, f32[64,512]{1,0:T(8,128)S(1)}, bf16[64,512]{1,0:T(8,128)(2,1)S(1)}) custom-call(s32[8,128]{1,0:T(8,128)S(1)} %get-tuple-element.33.ids, bf16[64,512]{1,0:T(8,128)(2,1)S(1)} %get-tuple-element.34.mean, f32[1024,512]{1,0:T(8,128)S(1)} %get-tuple-element.36.sums, bf16[1024,128]{1,0:T(8,128)(2,1)S(1)} %get-tuple-element.37.tally, ...), custom_call_target="tpu_custom_call" | custom-call | tf_op jit(solution)/shard_map/pallas_call | solution.py:339
  47.0 1.3 %collective-permute-done.14 = bf16[64,512]{1,0:T(8,128)(2,1)S(1)} collective-permute-done((bf16[64,512]{1,0:T(8,128)(2,1)S(1)}, bf16[64,512]{1,0:T(8,128)(2,1)S(1)}, u32[]{:S(2)}, u32[]{:S(2)}) %collective-permute-start.14) | collective-permute-done | bytes 65568 | tf_op jit(solution)/shard_map/ppermute | solution.py:29
  48.3 0.7 %convert_add_fusion = f32[64,512]{1,0:T(8,128)} fusion(f32[64,512]{1,0:T(8,128)S(1)} %get-tuple-element.39, bf16[64,512]{1,0:T(8,128)(2,1)S(1)} %collective-permute-done.14), kind=kLoop, calls=%fused_computation | loop fusion | flops 65536 | bytes 327680 | tf_op jit(solution)/shard_map/add | solution.py:409
  (16 shorter events, 1.8 us)
Async XLA Ops:
  0.6 0.7 %copy-start = (s32[64,1]{0,1:T(1,128)S(1)}, s32[64,1]{0,1:T(1,128)}, u32[]{:S(2)}) copy-start(s32[64,1]{0,1:T(1,128)} %param.5) | copy-start | bytes 772
  4.5 7.3 %collective-permute-start = (bf16[144,512]{1,0:T(8,128)(2,1)S(1)}, bf16[144,512]{1,0:T(8,128)(2,1)S(1)}, u32[]{:S(2)}, u32[]{:S(2)}) collective-permute-start(bf16[144,512]{1,0:T(8,128)(2,1)S(1)} %get-tuple-element.24), channel_id=1, source_target_pairs={{0,2},{1,3},{2,0},{3,1},{4,6},{5,7},{6,4},{7,5},{8,10},{9,11},{10,... | collective-permute-start | bytes 442376 | tf_op jit(solution)/shard_map/ppermute | solution.py:29
  7.5 8.5 %collective-permute-start.1 = (bf16[144,512]{1,0:T(8,128)(2,1)S(1)}, bf16[144,512]{1,0:T(8,128)(2,1)S(1)}, u32[]{:S(2)}, u32[]{:S(2)}) collective-permute-start(bf16[144,512]{1,0:T(8,128)(2,1)S(1)} %get-tuple-element.25), channel_id=1, source_target_pairs={{0,4},{1,5},{2,6},{3,7},{4,0},{5,1},{6,2},{7,3},{8,12},{9,13},{10,... | collective-permute-start | bytes 442376 | tf_op jit(solution)/shard_map/ppermute | solution.py:29
  9.1 7.0 %collective-permute-start.2 = (bf16[144,512]{1,0:T(8,128)(2,1)S(1)}, bf16[144,512]{1,0:T(8,128)(2,1)S(1)}, u32[]{:S(2)}, u32[]{:S(2)}) collective-permute-start(bf16[144,512]{1,0:T(8,128)(2,1)S(1)} %get-tuple-element.26), channel_id=1, source_target_pairs={{0,6},{1,7},{2,4},{3,5},{4,2},{5,3},{6,0},{7,1},{8,14},{9,15},{10,... | collective-permute-start | bytes 442376 | tf_op jit(solution)/shard_map/ppermute | solution.py:29
  16.2 6.5 %collective-permute-start.3 = (bf16[80,512]{1,0:T(8,128)(2,1)S(1)}, bf16[80,512]{1,0:T(8,128)(2,1)S(1)}, u32[]{:S(2)}, u32[]{:S(2)}) collective-permute-start(bf16[80,512]{1,0:T(8,128)(2,1)S(1)} %get-tuple-element.29), channel_id=1, source_target_pairs={{0,8},{1,9},{2,10},{3,11},{4,12},{5,13},{6,14},{7,15},{8,16},{9,17... | collective-permute-start | bytes 245768 | tf_op jit(solution)/shard_map/ppermute | solution.py:29
  17.8 7.0 %collective-permute-start.4 = (bf16[80,512]{1,0:T(8,128)(2,1)S(1)}, bf16[80,512]{1,0:T(8,128)(2,1)S(1)}, u32[]{:S(2)}, u32[]{:S(2)}) collective-permute-start(bf16[80,512]{1,0:T(8,128)(2,1)S(1)} %get-tuple-element.30), channel_id=1, source_target_pairs={{0,16},{1,17},{2,18},{3,19},{4,20},{5,21},{6,22},{7,23},{8,24},{9,... | collective-permute-start | bytes 245768 | tf_op jit(solution)/shard_map/ppermute | solution.py:29
  25.6 4.7 %collective-permute-start.5 = (bf16[80,512]{1,0:T(8,128)(2,1)S(1)}, bf16[80,512]{1,0:T(8,128)(2,1)S(1)}, u32[]{:S(2)}, u32[]{:S(2)}) collective-permute-start(bf16[80,512]{1,0:T(8,128)(2,1)S(1)} %get-tuple-element.32.own), channel_id=1, source_target_pairs={{0,8},{1,9},{2,10},{3,11},{4,12},{5,13},{6,14},{7,15},{8,0},{9,1},... | collective-permute-start | bytes 245768 | tf_op jit(solution)/shard_map/ppermute | solution.py:29
  25.6 7.3 %collective-permute-start.9 = (bf16[64,512]{1,0:T(8,128)(2,1)S(1)}, bf16[64,512]{1,0:T(8,128)(2,1)S(1)}, u32[]{:S(2)}, u32[]{:S(2)}) collective-permute-start(bf16[64,512]{1,0:T(8,128)(2,1)S(1)} %get-tuple-element.34.mean), channel_id=1, source_target_pairs={{0,16},{1,17},{2,18},{3,19},{4,20},{5,21},{6,22},{7,23},{8,24},{9,... | collective-permute-start | bytes 196616 | tf_op jit(solution)/shard_map/ppermute | solution.py:29
  28.1 6.2 %collective-permute-start.10 = (bf16[64,512]{1,0:T(8,128)(2,1)S(1)}, bf16[64,512]{1,0:T(8,128)(2,1)S(1)}, u32[]{:S(2)}, u32[]{:S(2)}) collective-permute-start(bf16[64,512]{1,0:T(8,128)(2,1)S(1)} %get-tuple-element.34.mean), channel_id=1, source_target_pairs={{0,24},{1,25},{2,26},{3,27},{4,28},{5,29},{6,30},{7,31},{8,16},{9,... | collective-permute-start | bytes 196616 | tf_op jit(solution)/shard_map/ppermute | solution.py:29
  30.4 7.3 %collective-permute-start.6 = (bf16[128,512]{1,0:T(8,128)(2,1)S(1)}, bf16[128,512]{1,0:T(8,128)(2,1)S(1)}, u32[]{:S(2)}, u32[]{:S(2)}) collective-permute-start(bf16[128,512]{1,0:T(8,128)(2,1)S(1)} %get-tuple-element.35.refs_0_), channel_id=1, source_target_pairs={{0,2},{1,5},{2,0},{3,7},{4,6},{5,1},{6,4},{7,3},{8,10},{9,13},{10,... | collective-permute-start | bytes 393224 | tf_op jit(solution)/shard_map/ppermute | solution.py:29
  34.3 6.5 %collective-permute-start.11 = (bf16[128,512]{1,0:T(8,128)(2,1)S(1)}, bf16[128,512]{1,0:T(8,128)(2,1)S(1)}, u32[]{:S(2)}, u32[]{:S(2)}) collective-permute-start(bf16[128,512]{1,0:T(8,128)(2,1)S(1)} %shard_map.62.refs_4_), channel_id=1, source_target_pairs={{0,2},{1,5},{2,0},{3,7},{4,6},{5,1},{6,4},{7,3},{8,10},{9,13},{10,... | collective-permute-start | bytes 393224 | tf_op jit(solution)/shard_map/ppermute | solution.py:29
  35.6 5.4 %collective-permute-start.12 = (bf16[128,512]{1,0:T(8,128)(2,1)S(1)}, bf16[128,512]{1,0:T(8,128)(2,1)S(1)}, u32[]{:S(2)}, u32[]{:S(2)}) collective-permute-start(bf16[128,512]{1,0:T(8,128)(2,1)S(1)} %shard_map.62.refs_4_), channel_id=1, source_target_pairs={{0,4},{1,3},{2,6},{3,1},{4,0},{5,7},{6,2},{7,5},{8,12},{9,11},{10,... | collective-permute-start | bytes 393224 | tf_op jit(solution)/shard_map/ppermute | solution.py:29
  35.6 6.4 %collective-permute-start.7 = (bf16[128,512]{1,0:T(8,128)(2,1)S(1)}, bf16[128,512]{1,0:T(8,128)(2,1)S(1)}, u32[]{:S(2)}, u32[]{:S(2)}) collective-permute-start(bf16[128,512]{1,0:T(8,128)(2,1)S(1)} %get-tuple-element.35.refs_0_), channel_id=1, source_target_pairs={{0,4},{1,3},{2,6},{3,1},{4,0},{5,7},{6,2},{7,5},{8,12},{9,11},{10,... | collective-permute-start | bytes 393224 | tf_op jit(solution)/shard_map/ppermute | solution.py:29
  37.6 5.7 %collective-permute-start.8 = (bf16[128,512]{1,0:T(8,128)(2,1)S(1)}, bf16[128,512]{1,0:T(8,128)(2,1)S(1)}, u32[]{:S(2)}, u32[]{:S(2)}) collective-permute-start(bf16[128,512]{1,0:T(8,128)(2,1)S(1)} %collective-permute-done.6.refs_1_), channel_id=1, source_target_pairs={{0,4},{1,3},{2,6},{3,1},{4,0},{5,7},{6,2},{7,5},{8,12},{9,11},{10,... | collective-permute-start | bytes 393224 | tf_op jit(solution)/shard_map/ppermute | solution.py:29
  40.8 5.0 %collective-permute-start.13 = (bf16[128,512]{1,0:T(8,128)(2,1)S(1)}, bf16[128,512]{1,0:T(8,128)(2,1)S(1)}, u32[]{:S(2)}, u32[]{:S(2)}) collective-permute-start(bf16[128,512]{1,0:T(8,128)(2,1)S(1)} %collective-permute-done.11.refs_5_), channel_id=1, source_target_pairs={{0,4},{1,3},{2,6},{3,1},{4,0},{5,7},{6,2},{7,5},{8,12},{9,11},{10,... | collective-permute-start | bytes 393224 | tf_op jit(solution)/shard_map/ppermute | solution.py:29
  47.0 1.3 %collective-permute-start.14 = (bf16[64,512]{1,0:T(8,128)(2,1)S(1)}, bf16[64,512]{1,0:T(8,128)(2,1)S(1)}, u32[]{:S(2)}, u32[]{:S(2)}) collective-permute-start(bf16[64,512]{1,0:T(8,128)(2,1)S(1)} %get-tuple-element.40), channel_id=1, source_target_pairs={{0,1},{1,0},{2,3},{3,2},{4,5},{5,4},{6,7},{7,6},{8,9},{9,8},{10,11... | collective-permute-start | bytes 196616 | tf_op jit(solution)/shard_map/ppermute | solution.py:29

commit v3 on v2

--- a/solution.py
+++ b/solution.py
@@ -10,7 +10,7 @@
 BAND = 8
 K2 = 1024
 GROUP = 4
-META = 16
+META = 8
 BASE = 256
 LANES = 128
 BF16 = jnp.bfloat16
@@ -54,11 +54,12 @@
     return jnp.where(hit, jnp.ones((), BF16), jnp.zeros((), BF16))
 
 
-def sum_kernel(devices, cent, ids_hbm, rows_hbm, group_ref, own_ref, own_meta_ref, *rest):
-    sends, (ids_ref, rows_ref, totals, arrived) = rest[:-4], rest[-4:]
+def sum_kernel(devices, cent, ids_hbm, rows_hbm, group_hbm, own_ref, own_meta_ref, *rest):
+    sends, (ids_ref, rows_ref, group_ref, totals, arrived) = rest[:-5], rest[-5:]
     steps, block = rows_ref.shape[:2]
     ids_copy = pltpu.make_async_copy(ids_hbm, ids_ref, arrived.at[steps])
     ids_copy.start()
+    group_copy = pltpu.make_async_copy(group_hbm, group_ref, arrived.at[steps + 1])
     copies = [
         pltpu.make_async_copy(
             rows_hbm.at[step * block : (step + 1) * block], rows_ref.at[step], arrived.at[step]
@@ -67,6 +68,7 @@
     ]
     for copy in copies:
         copy.start()
+    group_copy.start()
     position = lax.axis_index("dp")
     mate = position % GROUP
     labels = 2 * GROUP * cent
@@ -88,6 +90,7 @@
             totals[...] = part
         else:
             totals[...] += part
+    group_copy.wait()
     id_high, id_low = split_digits(group_ref[...].astype(F32))
     id_digits = jnp.concatenate([id_high, id_low], axis=0)
     counts = lax.dot_general(
@@ -99,14 +102,15 @@
         high, low = split_digits(counts[:1, index * pair : (index + 1) * pair])
         meta = jnp.concatenate([high, low, jnp.zeros((META - 2, LANES), F32)], axis=0)
         if index == 0:
-            own_meta_ref[...] = meta
-            own_meta_ref[2:4, :cent] = id_digits
+            own_meta_ref[:, :LANES] = meta
+            own_meta_ref[:, LANES:] = jnp.zeros((META, LANES), F32)
+            own_meta_ref[:2, LANES : LANES + cent] = id_digits
         else:
             send = sends[index - 1]
             send[:pair] = totals[index * pair : (index + 1) * pair].astype(BF16)
             send[pair:, :LANES] = meta.astype(BF16)
             send[pair:, LANES:] = jnp.zeros((META, send.shape[1] - LANES), BF16)
-            send[pair + 2 : pair + 4, :cent] = id_digits.astype(BF16)
+            send[pair : pair + 2, LANES : LANES + cent] = id_digits.astype(BF16)
 
 
 def band_sums(devices, cent, ids, rows, group):
@@ -117,24 +121,25 @@
     send = jax.ShapeDtypeStruct((pair + META, width), BF16)
     return pl.pallas_call(
         functools.partial(sum_kernel, devices, cent),
-        in_specs=[pl.BlockSpec(memory_space=pltpu.HBM)] * 2 + [whole()],
+        in_specs=[pl.BlockSpec(memory_space=pltpu.HBM)] * 3,
         out_specs=[whole()] * (GROUP + 1),
         out_shape=[
             jax.ShapeDtypeStruct((pair, width), F32),
-            jax.ShapeDtypeStruct((META, LANES), F32),
+            jax.ShapeDtypeStruct((META, 2 * LANES), F32),
         ]
         + [send] * (GROUP - 1),
         scratch_shapes=[
             pltpu.VMEM((1, count), jnp.int32),
             pltpu.VMEM((steps, block, width), BF16),
+            pltpu.VMEM((1, cent), jnp.int32),
             pltpu.VMEM((GROUP * pair, width), F32),
-            pltpu.SemaphoreType.DMA((steps + 1,)),
+            pltpu.SemaphoreType.DMA((steps + 2,)),
         ],
         compiler_params=small(),
     )(
         pltpu.with_memory_space_constraint(ids.reshape(1, count), pltpu.HBM),
         pltpu.with_memory_space_constraint(rows, pltpu.HBM),
-        group.reshape(1, cent),
+        pltpu.with_memory_space_constraint(group.reshape(1, cent), pltpu.HBM),
     )
 
 
@@ -145,34 +150,34 @@
     near = own[:cent]
     middle = own[cent:]
     far = jnp.zeros_like(near)
-    counts = own_meta[0:1] * BASE + own_meta[1:2]
+    counts = own_meta[0:1, :LANES] * BASE + own_meta[1:2, :LANES]
     far_counts = jnp.zeros_like(counts)
-    id_digits = [own_meta[2:4]]
+    id_digits = [own_meta[0:2, LANES:]]
     for index, got in ((1, one), (2, two), (3, three)):
         before = (mate ^ index) < mate
         first = got[:cent].astype(F32)
         near = near + jnp.where(before, first, 0.0)
         far = far + jnp.where(before, 0.0, first)
         middle = middle + got[cent:pair].astype(F32)
-        meta = got[pair:, :LANES].astype(F32)
-        row = meta[0:1] * BASE + meta[1:2]
+        meta = got[pair:, : 2 * LANES].astype(F32)
+        row = meta[0:1, :LANES] * BASE + meta[1:2, :LANES]
         mask = (lane >= cent) | before
         counts = counts + jnp.where(mask, row, 0.0)
         far_counts = far_counts + jnp.where(mask, 0.0, row)
-        id_digits.append(meta[2:4])
+        id_digits.append(meta[0:2, LANES:])
     id_digits = jnp.concatenate(id_digits, axis=0)
-    padding = jnp.zeros((META - 2 - 2 * GROUP, LANES), F32)
 
     def meta_of(row):
         high, low = split_digits(row)
-        return jnp.concatenate([high, low, id_digits, padding], axis=0)
+        digits = jnp.concatenate([high, low, jnp.zeros((META - 2, LANES), F32)], axis=0)
+        return jnp.concatenate([digits, id_digits], axis=1)
 
     base_ref[...] = near
     base_meta_ref[...] = meta_of(counts)
     for send, sums, row in ((next_ref, middle, counts), (far_ref, far, far_counts)):
         send[:cent] = sums.astype(BF16)
-        send[cent:, :LANES] = meta_of(row).astype(BF16)
-        send[cent:, LANES:] = jnp.zeros((META, send.shape[1] - LANES), BF16)
+        send[cent:, : 2 * LANES] = meta_of(row).astype(BF16)
+        send[cent:, 2 * LANES :] = jnp.zeros((META, send.shape[1] - 2 * LANES), BF16)
 
 
 def group_sums(cent, own, own_meta, got):
@@ -184,7 +189,7 @@
         out_specs=[whole()] * 4,
         out_shape=[
             jax.ShapeDtypeStruct((cent, width), F32),
-            jax.ShapeDtypeStruct((META, LANES), F32),
+            jax.ShapeDtypeStruct((META, 2 * LANES), F32),
             send,
             send,
         ],
@@ -192,17 +197,17 @@
     )(own, own_meta, *got)
 
 
-def mean_kernel(cent, base, base_meta, one, two, mean_ref, plain_ref, send_ref):
+def mean_kernel(cent, base, base_meta, one, two, mean_ref, send_ref):
     sums = base[...] + one[:cent].astype(F32) + two[:cent].astype(F32)
-    metas = [base_meta[...], one[cent:, :LANES].astype(F32), two[cent:, :LANES].astype(F32)]
-    rows = [meta[0:1] * BASE + meta[1:2] for meta in metas]
+    metas = [meta[...].astype(F32) for meta in (base_meta, one.at[cent:], two.at[cent:])]
+    rows = [meta[0:1, :LANES] * BASE + meta[1:2, :LANES] for meta in metas]
     row = rows[0] + pltpu.roll(rows[1], LANES - cent, 1) + rows[2]
     mean = (sums / as_column(row, cent)).astype(BF16)
     mean_ref[...] = mean
-    plain_ref[...] = mean
     send_ref[:cent] = mean
     for index, meta in enumerate(metas):
-        send_ref[cent:, index * LANES : (index + 1) * LANES] = meta.astype(BF16)
+        ids = meta[:, LANES : 2 * LANES].astype(BF16)
+        send_ref[cent:, index * LANES : (index + 1) * LANES] = ids
     known = len(metas) * LANES
     send_ref[cent:, known:] = jnp.zeros((META, mean.shape[1] - known), BF16)
 
@@ -213,8 +218,8 @@
     return pl.pallas_call(
         functools.partial(mean_kernel, cent),
         in_specs=[whole()] * 4,
-        out_specs=[whole()] * 3,
-        out_shape=[mean, mean, jax.ShapeDtypeStruct((cent + META, width), BF16)],
+        out_specs=[whole()] * 2,
+        out_shape=[mean, jax.ShapeDtypeStruct((cent + META, width), BF16)],
         compiler_params=small(),
     )(base, base_meta, *got)
 
@@ -227,7 +232,7 @@
 
     def ids_of(block, steps, index):
         meta = block[cent:, steps * LANES : (steps + 1) * LANES].astype(F32)
-        at = 2 + 2 * index
+        at = 2 * index
         return meta[at : at + 1] * BASE + meta[at + 1 : at + 2]
 
     near_rows, far_rows = [], []
@@ -256,19 +261,20 @@
     )(own, got)
 
 
-def far_kernel(first, second, far_ref):
+def join_kernel(first, second, out_ref):
     rows = first.shape[0]
-    far_ref[:rows] = first[...]
-    far_ref[rows:] = second[...]
-
-
-def far_rows(first, second):
+    out_ref[:rows] = first[...]
+    out_ref[rows:] = second[...]
+
+
+def joined(first, second):
     rows, width = first.shape
     return pl.pallas_call(
-        far_kernel,
+        join_kernel,
         in_specs=[whole()] * 2,
         out_specs=whole(),
         out_shape=jax.ShapeDtypeStruct((2 * rows, width), BF16),
+        cost_estimate=pl.CostEstimate(flops=100000000000, bytes_accessed=300000000, transcendentals=0),
         compiler_params=small(),
     )(first, second)
 
@@ -282,19 +288,23 @@
     return jnp.where(low, first, other)
 
 
+def gathered(ids, base, blocks):
+    one_hots = [one_hot_of(K2, ids_row(ids, base, order)) for order in range(GROUP)]
+    rows = [block[...] for block in blocks]
+    if len(rows) == GROUP:
+        rows[2:] = [jnp.concatenate(rows[2:], axis=0)]
+    rows[:2] = [jnp.concatenate(rows[:2], axis=0)]
+    total = None
+    for index, row in enumerate(rows):
+        one_hot = jnp.concatenate(one_hots[2 * index : 2 * index + 2], axis=1)
+        part = jnp.dot(one_hot, row, preferred_element_type=F32)
+        total = part if total is None else total + part
+    return total, sum(one_hots[1:], one_hots[0])
+
+
 def gather_kernel(ids, *refs):
     blocks, (sums_ref, tally_ref) = refs[:-2], refs[-2:]
-    tally = jnp.zeros((K2, LANES), BF16)
-    labels = [ids_row(ids, 0, order) for order in range(GROUP)]
-    labels += [ids_row(ids, GROUP, order) for order in range(GROUP - 1)]
-    total = None
-    for label, block in zip(labels, blocks):
-        one_hot = one_hot_of(K2, label)
-        tally = tally + one_hot
-        part = jnp.dot(one_hot, block[...], preferred_element_type=F32)
-        total = part if total is None else total + part
-    sums_ref[...] = total
-    tally_ref[...] = tally
+    sums_ref[...], tally_ref[...] = gathered(ids, 0, blocks)
 
 
 def gathered_sums(ids, blocks):
@@ -311,15 +321,20 @@
     )(ids, *blocks)
 
 
-def score_kernel(owned, ids, mean, sums, tally, block, second_ref, keep_ref, send_ref, values_ref):
-    one_hot = one_hot_of(K2, ids_row(ids, GROUP, GROUP - 1))
-    count = jnp.sum((tally[...] + one_hot).astype(F32), axis=1, keepdims=True)
-    total = sums[...] + jnp.dot(one_hot, block[...], preferred_element_type=F32)
-    second = (total * (1.0 / count)).astype(BF16)
+def score_kernel(owned, ids, mean, sums, tally, *refs):
+    blocks, refs = refs[:-7], refs[-7:]
+    mean_hbm, second_hbm, keep_ref, send_ref, values_ref, second_ref, sent = refs
+    mean_copy = pltpu.make_async_copy(mean, mean_hbm, sent.at[0])
+    mean_copy.start()
+    total, tally_here = gathered(ids, GROUP, blocks)
+    count = jnp.sum((tally[...] + tally_here).astype(F32), axis=1, keepdims=True)
+    second = ((sums[...] + total) * (1.0 / count)).astype(BF16)
     values = second.astype(F32)
     values_ref[...] = values
     start = pl.multiple_of(lax.axis_index("dp") * owned, owned)
     second_ref[...] = values_ref[pl.ds(start, owned)].astype(BF16)
+    second_copy = pltpu.make_async_copy(second_ref, second_hbm, sent.at[1])
+    second_copy.start()
     norms = 0.5 * jnp.sum(values * values, axis=1, keepdims=True)
     row = jnp.concatenate(
         [as_row(norms[at : at + LANES]) for at in range(0, K2, LANES)], axis=1
@@ -332,22 +347,30 @@
     low = lax.axis_index("mp") == 0
     keep_ref[...] = jnp.where(low, scores[:, :half], scores[:, half:])
     send_ref[...] = jnp.where(low, scores[:, half:], scores[:, :half]).astype(BF16)
-
-
-def second_level_scores(owned, ids, mean, sums, tally, block):
+    mean_copy.wait()
+    second_copy.wait()
+
+
+def second_level_scores(owned, ids, mean, sums, tally, blocks):
     cent, width = mean.shape
+    hbm = pl.BlockSpec(memory_space=pltpu.HBM)
     return pl.pallas_call(
         functools.partial(score_kernel, owned),
-        in_specs=[whole()] * 5,
-        out_specs=[whole()] * 3,
+        in_specs=[whole()] * (4 + len(blocks)),
+        out_specs=[hbm, hbm, whole(), whole()],
         out_shape=[
+            jax.ShapeDtypeStruct((cent, width), BF16),
             jax.ShapeDtypeStruct((owned, width), BF16),
             jax.ShapeDtypeStruct((cent, K2 // 2), F32),
             jax.ShapeDtypeStruct((cent, K2 // 2), BF16),
         ],
-        scratch_shapes=[pltpu.VMEM((K2, width), F32)],
-        compiler_params=small(),
-    )(ids, mean, sums, tally, block)
+        scratch_shapes=[
+            pltpu.VMEM((K2, width), F32),
+            pltpu.VMEM((owned, width), BF16),
+            pltpu.SemaphoreType.DMA((2,)),
+        ],
+        compiler_params=small(),
+    )(ids, mean, sums, tally, *blocks)
 
 
 def summed_scores(devices, second_level, first_centroids):
@@ -386,7 +409,7 @@
     got = [partner(send, index + 1) for index, send in enumerate(sends)]
     base, base_meta, following, far = group_sums(cent, own, own_meta, got)
     got = [ahead(following, GROUP), ahead(far, 2 * GROUP)]
-    mean, plain, send = means(cent, base, base_meta, got)
+    mean, send = means(cent, base, base_meta, got)
     if devices != GROUP * GROUP or cores != 2 or devices * cent > K2:
         return (mean, *summed_scores(devices, second_level, mean))
 
@@ -396,15 +419,18 @@
         )
 
     def plane_rows(value):
+        return [value, sideways(value, (1, 2)), sideways(value, (2, 1)), partner(value, 3)]
+
+    def relayed_rows(value):
         first = sideways(value, (1, 2))
-        second = sideways(value, (2, 1))
-        return [value, first, second, sideways(first, (2, 1))]
+        return [value, first, sideways(joined(value, first), (2, 1))]
 
     near, ids = near_rows(cent, send, partner(send, GROUP))
-    far = far_rows(partner(plain, 2 * GROUP), partner(plain, 3 * GROUP))
-    *blocks, last = plane_rows(near) + plane_rows(far)
-    sums, tally = gathered_sums(ids, blocks)
-    second, keep, send = second_level_scores(K2 // devices, ids, plain, sums, tally, last)
+    far = joined(partner(mean, 2 * GROUP), partner(mean, 3 * GROUP))
+    sums, tally = gathered_sums(ids, plane_rows(near))
+    mean, second, keep, send = second_level_scores(
+        K2 // devices, ids, mean, sums, tally, plane_rows(far)
+    )
     got = exchanged(send, [(d * cores + c, d * cores + (c ^ 1)) for d, c in everyone])
     return mean, second, keep + got.astype(F32)
 

time: 49.2 us -> 44.7 us (0.909)
  waiting for transfers between devices: 21.3 us -> 17.3 us
  starting transfers between devices: 18.1 us -> 19.8 us
  Pallas kernels: 7.54 us -> 6.06 us
  local copies, waits for them, and re-layouts: 0.65 us -> 0 us
    ppermute x15, waiting for transfers between devices: 21.3 us -> 17.3 us  [exchanged(): return lax.ppermute(value, ('dp', 'mp'), pairs)]
    ppermute x15, starting transfers between devices: 18.1 us -> 19.8 us  [exchanged(): return lax.ppermute(value, ('dp', 'mp'), pairs)]
    pallas_call x1, Pallas kernels: 2.03 us -> 0.71 us  [gathered_sums(): pl.pallas_call(gather_kernel, in_specs=[whole()] * (1 + len(blocks)), out...]
    unnamed x2 -> x0, local copies, waits for them, and re-layouts: 0.65 us -> none
    pallas_call x1, Pallas kernels: 0.8 us -> 0.17 us  [means(): pl.pallas_call(functools.partial(mean_kernel, cent), in_specs=[whole()] *...]
  transfers between devices with their start and end apart: 15 -> 15, of which waited for: 12 -> 10; matrix products, arithmetic and copies ran while one was open for 0% -> 0% of each run, Pallas kernels for 4% -> 2%
where the time goes in v3:
time: 44.7 us; the launch traced here: 44.5 us
  starting transfers between devices  19.8 us (44%)
  waiting for transfers between devices  17.3 us (39%)
  Pallas kernels  6.06 us (14%)
  between operations  0.68 us (2%)
  other arithmetic  0.67 us (1%)
    ppermute x15, starting transfers between devices, exchanged(): return lax.ppermute(value, ('dp', 'mp'), pairs)  19.8 us
    ppermute x15, waiting for transfers between devices, exchanged(): return lax.ppermute(value, ('dp', 'mp'), pairs)  17.3 us
    pallas_call x1, Pallas kernels, band_sums(): pl.pallas_call(functools.partial(sum_kernel, devices, cent), in_specs=[pl...  3.44 us
    pallas_call x1, Pallas kernels, second_level_scores(): pl.pallas_call(functools.partial(score_kernel, owned), in_specs=[whole()]...  1.5 us
  transfers between devices with their start and end apart: 15, of which 10 were waited for; matrix products, arithmetic and copies ran while one was open for 0% of the time, Pallas kernels for 2%

profile of v3, /device:TPU:0, one launch (start us, length us, event | category | flops | bytes accessed | tf_op | source)
XLA Modules:
  0.0 44.5 jit_solution(16213560911500995565)
XLA Ops:
  0.6 3.4 %shard_map.58 = (f32[128,512]{1,0:T(8,128)S(1)}, f32[8,256]{1,0:T(8,128)S(1)}, bf16[136,512]{1,0:T(8,128)(2,1)S(1)}, bf16[136,512]{1,0:T(8,128)(2,1)S(1)}, bf16[136,512]{1,0:T(8,128)(2,1)S(1)}) custom-call(s32[1,3072]{1,0:T(1,128)} %bitcast.2, bf16[3072,512]{1,0:T(8,128)(2,1)} %rows_hbm.1, s32[1,64]{1,0:T(1,128)} %bitcast.3), custom_call_target="tpu_custom_call" | custom-call | tf_op jit(solution)/shard_map/pallas_call | solution.py:122
  4.1 3.0 %collective-permute-start = (bf16[136,512]{1,0:T(8,128)(2,1)S(1)}, bf16[136,512]{1,0:T(8,128)(2,1)S(1)}, u32[]{:S(2)}, u32[]{:S(2)}) collective-permute-start(bf16[136,512]{1,0:T(8,128)(2,1)S(1)} %get-tuple-element.24), channel_id=1, source_target_pairs={{0,2},{1,3},{2,0},{3,1},{4,6},{5,7},{6,4},{7,5},{8,10},{9,11},{10,... | collective-permute-start | bytes 417800 | tf_op jit(solution)/shard_map/ppermute | solution.py:29
  7.1 1.5 %collective-permute-start.1 = (bf16[136,512]{1,0:T(8,128)(2,1)S(1)}, bf16[136,512]{1,0:T(8,128)(2,1)S(1)}, u32[]{:S(2)}, u32[]{:S(2)}) collective-permute-start(bf16[136,512]{1,0:T(8,128)(2,1)S(1)} %get-tuple-element.25), channel_id=1, source_target_pairs={{0,4},{1,5},{2,6},{3,7},{4,0},{5,1},{6,2},{7,3},{8,12},{9,13},{10,... | collective-permute-start | bytes 417800 | tf_op jit(solution)/shard_map/ppermute | solution.py:29
  8.6 2.5 %collective-permute-done.one = bf16[136,512]{1,0:T(8,128)(2,1)S(1)} collective-permute-done((bf16[136,512]{1,0:T(8,128)(2,1)S(1)}, bf16[136,512]{1,0:T(8,128)(2,1)S(1)}, u32[]{:S(2)}, u32[]{:S(2)}) %collective-permute-start) | collective-permute-done | bytes 139296 | tf_op jit(solution)/shard_map/ppermute | solution.py:29
  11.2 4.0 %collective-permute-done.1.two = bf16[136,512]{1,0:T(8,128)(2,1)S(1)} collective-permute-done((bf16[136,512]{1,0:T(8,128)(2,1)S(1)}, bf16[136,512]{1,0:T(8,128)(2,1)S(1)}, u32[]{:S(2)}, u32[]{:S(2)}) %collective-permute-start.1) | collective-permute-done | bytes 139296 | tf_op jit(solution)/shard_map/ppermute | solution.py:29
  15.3 1.6 %collective-permute-start.3 = (bf16[72,512]{1,0:T(8,128)(2,1)S(1)}, bf16[72,512]{1,0:T(8,128)(2,1)S(1)}, u32[]{:S(2)}, u32[]{:S(2)}) collective-permute-start(bf16[72,512]{1,0:T(8,128)(2,1)S(1)} %get-tuple-element.29), channel_id=1, source_target_pairs={{0,8},{1,9},{2,10},{3,11},{4,12},{5,13},{6,14},{7,15},{8,16},{9,17... | collective-permute-start | bytes 221192 | tf_op jit(solution)/shard_map/ppermute | solution.py:29
  17.0 2.6 %collective-permute-start.4 = (bf16[72,512]{1,0:T(8,128)(2,1)S(1)}, bf16[72,512]{1,0:T(8,128)(2,1)S(1)}, u32[]{:S(2)}, u32[]{:S(2)}) collective-permute-start(bf16[72,512]{1,0:T(8,128)(2,1)S(1)} %get-tuple-element.30), channel_id=1, source_target_pairs={{0,16},{1,17},{2,18},{3,19},{4,20},{5,21},{6,22},{7,23},{8,24},{9,... | collective-permute-start | bytes 221192 | tf_op jit(solution)/shard_map/ppermute | solution.py:29
  19.6 2.0 %collective-permute-done.3.one = bf16[72,512]{1,0:T(8,128)(2,1)S(1)} collective-permute-done((bf16[72,512]{1,0:T(8,128)(2,1)S(1)}, bf16[72,512]{1,0:T(8,128)(2,1)S(1)}, u32[]{:S(2)}, u32[]{:S(2)}) %collective-permute-start.3) | collective-permute-done | bytes 73760 | tf_op jit(solution)/shard_map/ppermute | solution.py:29
  21.6 0.9 %collective-permute-done.4.two = bf16[72,512]{1,0:T(8,128)(2,1)S(1)} collective-permute-done((bf16[72,512]{1,0:T(8,128)(2,1)S(1)}, bf16[72,512]{1,0:T(8,128)(2,1)S(1)}, u32[]{:S(2)}, u32[]{:S(2)}) %collective-permute-start.4) | collective-permute-done | bytes 73760 | tf_op jit(solution)/shard_map/ppermute | solution.py:29
  22.5 0.2 shard_map.60
  22.7 1.4 %collective-permute-start.5 = (bf16[72,512]{1,0:T(8,128)(2,1)S(1)}, bf16[72,512]{1,0:T(8,128)(2,1)S(1)}, u32[]{:S(2)}, u32[]{:S(2)}) collective-permute-start(bf16[72,512]{1,0:T(8,128)(2,1)S(1)} %get-tuple-element.31.own), channel_id=1, source_target_pairs={{0,8},{1,9},{2,10},{3,11},{4,12},{5,13},{6,14},{7,15},{8,0},{9,1},... | collective-permute-start | bytes 221192 | tf_op jit(solution)/shard_map/ppermute | solution.py:29
  24.1 2.4 %collective-permute-start.10 = (bf16[64,512]{1,0:T(8,128)(2,1)S(1)}, bf16[64,512]{1,0:T(8,128)(2,1)S(1)}, u32[]{:S(2)}, u32[]{:S(2)}) collective-permute-start(bf16[64,512]{1,0:T(8,128)(2,1)S(1)} %get-tuple-element.33.mean), channel_id=1, source_target_pairs={{0,24},{1,25},{2,26},{3,27},{4,28},{5,29},{6,30},{7,31},{8,16},{9,... | collective-permute-start | bytes 196616 | tf_op jit(solution)/shard_map/ppermute | solution.py:29
  26.5 1.3 %collective-permute-done.5.got = bf16[72,512]{1,0:T(8,128)(2,1)S(1)} collective-permute-done((bf16[72,512]{1,0:T(8,128)(2,1)S(1)}, bf16[72,512]{1,0:T(8,128)(2,1)S(1)}, u32[]{:S(2)}, u32[]{:S(2)}) %collective-permute-start.5) | collective-permute-done | bytes 73760 | tf_op jit(solution)/shard_map/ppermute | solution.py:29
  28.0 2.5 %collective-permute-start.6 = (bf16[128,512]{1,0:T(8,128)(2,1)S(1)}, bf16[128,512]{1,0:T(8,128)(2,1)S(1)}, u32[]{:S(2)}, u32[]{:S(2)}) collective-permute-start(bf16[128,512]{1,0:T(8,128)(2,1)S(1)} %get-tuple-element.34.refs_0_), channel_id=1, source_target_pairs={{0,2},{1,5},{2,0},{3,7},{4,6},{5,1},{6,4},{7,3},{8,10},{9,13},{10,... | collective-permute-start | bytes 393224 | tf_op jit(solution)/shard_map/ppermute | solution.py:29
  30.4 1.5 %collective-permute-start.8 = (bf16[128,512]{1,0:T(8,128)(2,1)S(1)}, bf16[128,512]{1,0:T(8,128)(2,1)S(1)}, u32[]{:S(2)}, u32[]{:S(2)}) collective-permute-start(bf16[128,512]{1,0:T(8,128)(2,1)S(1)} %get-tuple-element.34.refs_0_), channel_id=1, source_target_pairs={{0,6},{1,7},{2,4},{3,5},{4,2},{5,3},{6,0},{7,1},{8,14},{9,15},{10,... | collective-permute-start | bytes 393224 | tf_op jit(solution)/shard_map/ppermute | solution.py:29
  32.0 2.0 %collective-permute-start.11 = (bf16[128,512]{1,0:T(8,128)(2,1)S(1)}, bf16[128,512]{1,0:T(8,128)(2,1)S(1)}, u32[]{:S(2)}, u32[]{:S(2)}) collective-permute-start(bf16[128,512]{1,0:T(8,128)(2,1)S(1)} %shard_map.63.refs_0_), channel_id=1, source_target_pairs={{0,2},{1,5},{2,0},{3,7},{4,6},{5,1},{6,4},{7,3},{8,10},{9,13},{10,... | collective-permute-start | bytes 393224 | tf_op jit(solution)/shard_map/ppermute | solution.py:29
  34.0 0.7 %collective-permute-done.6.refs_1_ = bf16[128,512]{1,0:T(8,128)(2,1)S(1)} collective-permute-done((bf16[128,512]{1,0:T(8,128)(2,1)S(1)}, bf16[128,512]{1,0:T(8,128)(2,1)S(1)}, u32[]{:S(2)}, u32[]{:S(2)}) %collective-permute-start.6) | collective-permute-done | bytes 131104 | tf_op jit(solution)/shard_map/ppermute | solution.py:29
  34.7 1.1 %collective-permute-start.13 = (bf16[128,512]{1,0:T(8,128)(2,1)S(1)}, bf16[128,512]{1,0:T(8,128)(2,1)S(1)}, u32[]{:S(2)}, u32[]{:S(2)}) collective-permute-start(bf16[128,512]{1,0:T(8,128)(2,1)S(1)} %shard_map.63.refs_0_), channel_id=1, source_target_pairs={{0,6},{1,7},{2,4},{3,5},{4,2},{5,3},{6,0},{7,1},{8,14},{9,15},{10,... | collective-permute-start | bytes 393224 | tf_op jit(solution)/shard_map/ppermute | solution.py:29
  35.9 2.3 %collective-permute-done.7.refs_2_ = bf16[128,512]{1,0:T(8,128)(2,1)S(1)} collective-permute-done((bf16[128,512]{1,0:T(8,128)(2,1)S(1)}, bf16[128,512]{1,0:T(8,128)(2,1)S(1)}, u32[]{:S(2)}, u32[]{:S(2)}) %collective-permute-start.7) | collective-permute-done | bytes 131104 | tf_op jit(solution)/shard_map/ppermute | solution.py:29
  38.2 0.7 %shard_map.62 = (f32[1024,512]{1,0:T(8,128)S(1)}, bf16[1024,128]{1,0:T(8,128)(2,1)S(1)}) custom-call(s32[8,128]{1,0:T(8,128)S(1)} %get-tuple-element.32.ids, bf16[128,512]{1,0:T(8,128)(2,1)S(1)} %get-tuple-element.34.refs_0_, bf16[128,512]{1,0:T(8,128)(2,1)S(1)} %collective-permute-done.6.refs_1_, bf16[128,512]{1,0:T(8,128)(2,1)S(1)} %collective-permute-done.7.refs_2_, ...), custom_call_target="tpu_custom_call" | custom-call | tf_op jit(solution)/shard_map/pallas_call | solution.py:312
  39.0 2.0 %collective-permute-done.12.refs_2_ = bf16[128,512]{1,0:T(8,128)(2,1)S(1)} collective-permute-done((bf16[128,512]{1,0:T(8,128)(2,1)S(1)}, bf16[128,512]{1,0:T(8,128)(2,1)S(1)}, u32[]{:S(2)}, u32[]{:S(2)}) %collective-permute-start.12) | collective-permute-done | bytes 131104 | tf_op jit(solution)/shard_map/ppermute | solution.py:29
  41.0 1.5 %shard_map.64 = (bf16[64,512]{1,0:T(8,128)(2,1)}, bf16[64,512]{1,0:T(8,128)(2,1)}, f32[64,512]{1,0:T(8,128)S(1)}, bf16[64,512]{1,0:T(8,128)(2,1)S(1)}) custom-call(s32[8,128]{1,0:T(8,128)S(1)} %get-tuple-element.32.ids, bf16[64,512]{1,0:T(8,128)(2,1)S(1)} %get-tuple-element.33.mean, f32[1024,512]{1,0:T(8,128)S(1)} %get-tuple-element.35.sums, ...), custom_call_target="tpu_custom_call" | custom-call | tf_op jit(solution)/shard_map/pallas_call | solution.py:357
  42.6 1.2 %collective-permute-done.14 = bf16[64,512]{1,0:T(8,128)(2,1)S(1)} collective-permute-done((bf16[64,512]{1,0:T(8,128)(2,1)S(1)}, bf16[64,512]{1,0:T(8,128)(2,1)S(1)}, u32[]{:S(2)}, u32[]{:S(2)}) %collective-permute-start.14) | collective-permute-done | bytes 65568 | tf_op jit(solution)/shard_map/ppermute | solution.py:29
  43.8 0.7 %convert_add_fusion = f32[64,512]{1,0:T(8,128)} fusion(f32[64,512]{1,0:T(8,128)S(1)} %get-tuple-element.39, bf16[64,512]{1,0:T(8,128)(2,1)S(1)} %collective-permute-done.14), kind=kLoop, calls=%fused_computation | loop fusion | flops 65536 | bytes 327680 | tf_op jit(solution)/shard_map/add | solution.py:435
  (14 shorter events, 0.4 us)
Async XLA Ops:
  4.1 7.1 %collective-permute-start = (bf16[136,512]{1,0:T(8,128)(2,1)S(1)}, bf16[136,512]{1,0:T(8,128)(2,1)S(1)}, u32[]{:S(2)}, u32[]{:S(2)}) collective-permute-start(bf16[136,512]{1,0:T(8,128)(2,1)S(1)} %get-tuple-element.24), channel_id=1, source_target_pairs={{0,2},{1,3},{2,0},{3,1},{4,6},{5,7},{6,4},{7,5},{8,10},{9,11},{10,... | collective-permute-start | bytes 417800 | tf_op jit(solution)/shard_map/ppermute | solution.py:29
  7.1 8.1 %collective-permute-start.1 = (bf16[136,512]{1,0:T(8,128)(2,1)S(1)}, bf16[136,512]{1,0:T(8,128)(2,1)S(1)}, u32[]{:S(2)}, u32[]{:S(2)}) collective-permute-start(bf16[136,512]{1,0:T(8,128)(2,1)S(1)} %get-tuple-element.25), channel_id=1, source_target_pairs={{0,4},{1,5},{2,6},{3,7},{4,0},{5,1},{6,2},{7,3},{8,12},{9,13},{10,... | collective-permute-start | bytes 417800 | tf_op jit(solution)/shard_map/ppermute | solution.py:29
  8.6 6.6 %collective-permute-start.2 = (bf16[136,512]{1,0:T(8,128)(2,1)S(1)}, bf16[136,512]{1,0:T(8,128)(2,1)S(1)}, u32[]{:S(2)}, u32[]{:S(2)}) collective-permute-start(bf16[136,512]{1,0:T(8,128)(2,1)S(1)} %get-tuple-element.26), channel_id=1, source_target_pairs={{0,6},{1,7},{2,4},{3,5},{4,2},{5,3},{6,0},{7,1},{8,14},{9,15},{10,... | collective-permute-start | bytes 417800 | tf_op jit(solution)/shard_map/ppermute | solution.py:29
  15.3 6.3 %collective-permute-start.3 = (bf16[72,512]{1,0:T(8,128)(2,1)S(1)}, bf16[72,512]{1,0:T(8,128)(2,1)S(1)}, u32[]{:S(2)}, u32[]{:S(2)}) collective-permute-start(bf16[72,512]{1,0:T(8,128)(2,1)S(1)} %get-tuple-element.29), channel_id=1, source_target_pairs={{0,8},{1,9},{2,10},{3,11},{4,12},{5,13},{6,14},{7,15},{8,16},{9,17... | collective-permute-start | bytes 221192 | tf_op jit(solution)/shard_map/ppermute | solution.py:29
  17.0 5.6 %collective-permute-start.4 = (bf16[72,512]{1,0:T(8,128)(2,1)S(1)}, bf16[72,512]{1,0:T(8,128)(2,1)S(1)}, u32[]{:S(2)}, u32[]{:S(2)}) collective-permute-start(bf16[72,512]{1,0:T(8,128)(2,1)S(1)} %get-tuple-element.30), channel_id=1, source_target_pairs={{0,16},{1,17},{2,18},{3,19},{4,20},{5,21},{6,22},{7,23},{8,24},{9,... | collective-permute-start | bytes 221192 | tf_op jit(solution)/shard_map/ppermute | solution.py:29
  22.7 5.1 %collective-permute-start.5 = (bf16[72,512]{1,0:T(8,128)(2,1)S(1)}, bf16[72,512]{1,0:T(8,128)(2,1)S(1)}, u32[]{:S(2)}, u32[]{:S(2)}) collective-permute-start(bf16[72,512]{1,0:T(8,128)(2,1)S(1)} %get-tuple-element.31.own), channel_id=1, source_target_pairs={{0,8},{1,9},{2,10},{3,11},{4,12},{5,13},{6,14},{7,15},{8,0},{9,1},... | collective-permute-start | bytes 221192 | tf_op jit(solution)/shard_map/ppermute | solution.py:29
  24.1 7.8 %collective-permute-start.10 = (bf16[64,512]{1,0:T(8,128)(2,1)S(1)}, bf16[64,512]{1,0:T(8,128)(2,1)S(1)}, u32[]{:S(2)}, u32[]{:S(2)}) collective-permute-start(bf16[64,512]{1,0:T(8,128)(2,1)S(1)} %get-tuple-element.33.mean), channel_id=1, source_target_pairs={{0,24},{1,25},{2,26},{3,27},{4,28},{5,29},{6,30},{7,31},{8,16},{9,... | collective-permute-start | bytes 196616 | tf_op jit(solution)/shard_map/ppermute | solution.py:29
  26.5 5.4 %collective-permute-start.9 = (bf16[64,512]{1,0:T(8,128)(2,1)S(1)}, bf16[64,512]{1,0:T(8,128)(2,1)S(1)}, u32[]{:S(2)}, u32[]{:S(2)}) collective-permute-start(bf16[64,512]{1,0:T(8,128)(2,1)S(1)} %get-tuple-element.33.mean), channel_id=1, source_target_pairs={{0,16},{1,17},{2,18},{3,19},{4,20},{5,21},{6,22},{7,23},{8,24},{9,... | collective-permute-start | bytes 196616 | tf_op jit(solution)/shard_map/ppermute | solution.py:29
  28.0 6.8 %collective-permute-start.6 = (bf16[128,512]{1,0:T(8,128)(2,1)S(1)}, bf16[128,512]{1,0:T(8,128)(2,1)S(1)}, u32[]{:S(2)}, u32[]{:S(2)}) collective-permute-start(bf16[128,512]{1,0:T(8,128)(2,1)S(1)} %get-tuple-element.34.refs_0_), channel_id=1, source_target_pairs={{0,2},{1,5},{2,0},{3,7},{4,6},{5,1},{6,4},{7,3},{8,10},{9,13},{10,... | collective-permute-start | bytes 393224 | tf_op jit(solution)/shard_map/ppermute | solution.py:29
  30.4 7.8 %collective-permute-start.7 = (bf16[128,512]{1,0:T(8,128)(2,1)S(1)}, bf16[128,512]{1,0:T(8,128)(2,1)S(1)}, u32[]{:S(2)}, u32[]{:S(2)}) collective-permute-start(bf16[128,512]{1,0:T(8,128)(2,1)S(1)} %get-tuple-element.34.refs_0_), channel_id=1, source_target_pairs={{0,4},{1,3},{2,6},{3,1},{4,0},{5,7},{6,2},{7,5},{8,12},{9,11},{10,... | collective-permute-start | bytes 393224 | tf_op jit(solution)/shard_map/ppermute | solution.py:29
  30.4 7.8 %collective-permute-start.8 = (bf16[128,512]{1,0:T(8,128)(2,1)S(1)}, bf16[128,512]{1,0:T(8,128)(2,1)S(1)}, u32[]{:S(2)}, u32[]{:S(2)}) collective-permute-start(bf16[128,512]{1,0:T(8,128)(2,1)S(1)} %get-tuple-element.34.refs_0_), channel_id=1, source_target_pairs={{0,6},{1,7},{2,4},{3,5},{4,2},{5,3},{6,0},{7,1},{8,14},{9,15},{10,... | collective-permute-start | bytes 393224 | tf_op jit(solution)/shard_map/ppermute | solution.py:29
  32.0 7.0 %collective-permute-start.11 = (bf16[128,512]{1,0:T(8,128)(2,1)S(1)}, bf16[128,512]{1,0:T(8,128)(2,1)S(1)}, u32[]{:S(2)}, u32[]{:S(2)}) collective-permute-start(bf16[128,512]{1,0:T(8,128)(2,1)S(1)} %shard_map.63.refs_0_), channel_id=1, source_target_pairs={{0,2},{1,5},{2,0},{3,7},{4,6},{5,1},{6,4},{7,3},{8,10},{9,13},{10,... | collective-permute-start | bytes 393224 | tf_op jit(solution)/shard_map/ppermute | solution.py:29
  34.0 7.0 %collective-permute-start.12 = (bf16[128,512]{1,0:T(8,128)(2,1)S(1)}, bf16[128,512]{1,0:T(8,128)(2,1)S(1)}, u32[]{:S(2)}, u32[]{:S(2)}) collective-permute-start(bf16[128,512]{1,0:T(8,128)(2,1)S(1)} %shard_map.63.refs_0_), channel_id=1, source_target_pairs={{0,4},{1,3},{2,6},{3,1},{4,0},{5,7},{6,2},{7,5},{8,12},{9,11},{10,... | collective-permute-start | bytes 393224 | tf_op jit(solution)/shard_map/ppermute | solution.py:29
  34.7 6.3 %collective-permute-start.13 = (bf16[128,512]{1,0:T(8,128)(2,1)S(1)}, bf16[128,512]{1,0:T(8,128)(2,1)S(1)}, u32[]{:S(2)}, u32[]{:S(2)}) collective-permute-start(bf16[128,512]{1,0:T(8,128)(2,1)S(1)} %shard_map.63.refs_0_), channel_id=1, source_target_pairs={{0,6},{1,7},{2,4},{3,5},{4,2},{5,3},{6,0},{7,1},{8,14},{9,15},{10,... | collective-permute-start | bytes 393224 | tf_op jit(solution)/shard_map/ppermute | solution.py:29
  42.5 1.3 %collective-permute-start.14 = (bf16[64,512]{1,0:T(8,128)(2,1)S(1)}, bf16[64,512]{1,0:T(8,128)(2,1)S(1)}, u32[]{:S(2)}, u32[]{:S(2)}) collective-permute-start(bf16[64,512]{1,0:T(8,128)(2,1)S(1)} %get-tuple-element.40), channel_id=1, source_target_pairs={{0,1},{1,0},{2,3},{3,2},{4,5},{5,4},{6,7},{7,6},{8,9},{9,8},{10,11... | collective-permute-start | bytes 196616 | tf_op jit(solution)/shard_map/ppermute | solution.py:29

commit v4 on v3

--- a/solution.py
+++ b/solution.py
@@ -31,6 +31,10 @@
 
 def iota(shape, dim):
     return lax.broadcasted_iota(jnp.int32, shape, dim)
+
+
+def even_line():
+    return lax.axis_index("dp") // GROUP % 2 == 0
 
 
 def split_digits(row):
@@ -143,7 +147,7 @@
     )
 
 
-def group_kernel(cent, own, own_meta, one, two, three, base_ref, base_meta_ref, next_ref, far_ref):
+def group_kernel(cent, four, own, own_meta, one, two, three, base_ref, base_meta_ref, next_ref, far_ref):
     mate = lax.axis_index("dp") % GROUP
     pair = 2 * cent
     lane = iota((1, LANES), 1)
@@ -172,6 +176,13 @@
         digits = jnp.concatenate([high, low, jnp.zeros((META - 2, LANES), F32)], axis=0)
         return jnp.concatenate([digits, id_digits], axis=1)
 
+    if four:
+        even = even_line()
+        near, far = jnp.where(even, far, near), jnp.where(even, near, far)
+        counts, far_counts = (
+            jnp.where(even & (lane < cent), far_counts, counts),
+            jnp.where(even, counts, far_counts),
+        )
     base_ref[...] = near
     base_meta_ref[...] = meta_of(counts)
     for send, sums, row in ((next_ref, middle, counts), (far_ref, far, far_counts)):
@@ -180,11 +191,11 @@
         send[cent:, 2 * LANES :] = jnp.zeros((META, send.shape[1] - 2 * LANES), BF16)
 
 
-def group_sums(cent, own, own_meta, got):
+def group_sums(cent, four, own, own_meta, got):
     width = own.shape[1]
     send = jax.ShapeDtypeStruct((cent + META, width), BF16)
     return pl.pallas_call(
-        functools.partial(group_kernel, cent),
+        functools.partial(group_kernel, cent, four),
         in_specs=[whole()] * 5,
         out_specs=[whole()] * 4,
         out_shape=[
@@ -227,7 +238,7 @@
 def near_kernel(cent, own, got, near_ref, ids_ref):
     near_ref[:cent] = own[:cent]
     near_ref[cent:] = got[:cent]
-    odd = lax.axis_index("dp") // GROUP % 2 == 1
+    even = even_line()
     lane = iota((1, LANES), 1)
 
     def ids_of(block, steps, index):
@@ -237,9 +248,10 @@
 
     near_rows, far_rows = [], []
     for index in range(GROUP):
-        near_rows.append((ids_of(own, 0, index), ids_of(got, 0, index)))
-        last = jnp.where(odd, ids_of(got, 2, index), ids_of(own, 1, index))
-        far_rows.append((ids_of(own, 2, index), last))
+        here, one, two = (ids_of(own, steps, index) for steps in range(3))
+        three = ids_of(got, 2, index)
+        near_rows.append((jnp.where(even, two, here), jnp.where(even, one, three)))
+        far_rows.append((jnp.where(even, here, two), jnp.where(even, three, one)))
     rows = [
         jnp.where(lane < cent, left, pltpu.roll(right, cent, 1))
         for left, right in near_rows + far_rows
@@ -322,9 +334,12 @@
 
 
 def score_kernel(owned, ids, mean, sums, tally, *refs):
-    blocks, refs = refs[:-7], refs[-7:]
-    mean_hbm, second_hbm, keep_ref, send_ref, values_ref, second_ref, sent = refs
-    mean_copy = pltpu.make_async_copy(mean, mean_hbm, sent.at[0])
+    blocks, refs = refs[:-8], refs[-8:]
+    mean_hbm, second_hbm, keep_ref, send_ref, values_ref, mean_ref, second_ref, sent = refs
+    cent = mean.shape[0]
+    first = jnp.where(even_line(), blocks[0][:cent], mean[...])
+    mean_ref[...] = first
+    mean_copy = pltpu.make_async_copy(mean_ref, mean_hbm, sent.at[0])
     mean_copy.start()
     total, tally_here = gathered(ids, GROUP, blocks)
     count = jnp.sum((tally[...] + tally_here).astype(F32), axis=1, keepdims=True)
@@ -340,7 +355,7 @@
         [as_row(norms[at : at + LANES]) for at in range(0, K2, LANES)], axis=1
     )
     products = lax.dot_general(
-        mean[...], second, (((1,), (1,)), ((), ())), preferred_element_type=F32
+        first, second, (((1,), (1,)), ((), ())), preferred_element_type=F32
     )
     scores = products - row
     half = K2 // 2
@@ -366,6 +381,7 @@
         ],
         scratch_shapes=[
             pltpu.VMEM((K2, width), F32),
+            pltpu.VMEM((cent, width), BF16),
             pltpu.VMEM((owned, width), BF16),
             pltpu.SemaphoreType.DMA((2,)),
         ],
@@ -407,10 +423,14 @@
 
     own, own_meta, *sends = band_sums(devices, cent, first_level, embeddings, second_level)
     got = [partner(send, index + 1) for index, send in enumerate(sends)]
-    base, base_meta, following, far = group_sums(cent, own, own_meta, got)
-    got = [ahead(following, GROUP), ahead(far, 2 * GROUP)]
+    four = devices == GROUP * GROUP and cores == 2 and devices * cent <= K2
+    base, base_meta, following, far = group_sums(cent, four, own, own_meta, got)
+    if four:
+        got = [partner(following, GROUP), partner(far, 2 * GROUP)]
+    else:
+        got = [ahead(following, GROUP), ahead(far, 2 * GROUP)]
     mean, send = means(cent, base, base_meta, got)
-    if devices != GROUP * GROUP or cores != 2 or devices * cent > K2:
+    if not four:
         return (mean, *summed_scores(devices, second_level, mean))
 
     def sideways(value, steps):

time: 44.7 us -> 44.1 us (0.987)
  waiting for transfers between devices: 17.3 us -> 16.4 us
    ppermute x15, waiting for transfers between devices: 17.3 us -> 16.4 us  [exchanged(): return lax.ppermute(value, ('dp', 'mp'), pairs)]
where the time goes in v4:
time: 44.1 us; the launch traced here: 43.9 us
  starting transfers between devices  20.1 us (46%)
  waiting for transfers between devices  16.4 us (37%)
  Pallas kernels  6.06 us (14%)
  between operations  0.7 us (2%)
  other arithmetic  0.67 us (2%)
    ppermute x15, starting transfers between devices, exchanged(): return lax.ppermute(value, ('dp', 'mp'), pairs)  20.1 us
    ppermute x15, waiting for transfers between devices, exchanged(): return lax.ppermute(value, ('dp', 'mp'), pairs)  16.4 us
    pallas_call x1, Pallas kernels, band_sums(): pl.pallas_call(functools.partial(sum_kernel, devices, cent), in_specs=[pl...  3.44 us
    pallas_call x1, Pallas kernels, second_level_scores(): pl.pallas_call(functools.partial(score_kernel, owned), in_specs=[whole()]...  1.5 us
  transfers between devices with their start and end apart: 15, of which 10 were waited for; matrix products, arithmetic and copies ran while one was open for 0% of the time, Pallas kernels for 2%

profile of v4, /device:TPU:0, one launch (start us, length us, event | category | flops | bytes accessed | tf_op | source)
XLA Modules:
  0.0 43.9 jit_solution(5385718640761195878)
XLA Ops:
  0.6 3.4 %shard_map.58 = (f32[128,512]{1,0:T(8,128)S(1)}, f32[8,256]{1,0:T(8,128)S(1)}, bf16[136,512]{1,0:T(8,128)(2,1)S(1)}, bf16[136,512]{1,0:T(8,128)(2,1)S(1)}, bf16[136,512]{1,0:T(8,128)(2,1)S(1)}) custom-call(s32[1,3072]{1,0:T(1,128)} %bitcast.2, bf16[3072,512]{1,0:T(8,128)(2,1)} %rows_hbm.1, s32[1,64]{1,0:T(1,128)} %bitcast.3), custom_call_target="tpu_custom_call" | custom-call | tf_op jit(solution)/shard_map/pallas_call | solution.py:126
  4.1 3.0 %collective-permute-start = (bf16[136,512]{1,0:T(8,128)(2,1)S(1)}, bf16[136,512]{1,0:T(8,128)(2,1)S(1)}, u32[]{:S(2)}, u32[]{:S(2)}) collective-permute-start(bf16[136,512]{1,0:T(8,128)(2,1)S(1)} %get-tuple-element.24), channel_id=1, source_target_pairs={{0,2},{1,3},{2,0},{3,1},{4,6},{5,7},{6,4},{7,5},{8,10},{9,11},{10,... | collective-permute-start | bytes 417800 | tf_op jit(solution)/shard_map/ppermute | solution.py:29
  7.1 1.5 %collective-permute-start.1 = (bf16[136,512]{1,0:T(8,128)(2,1)S(1)}, bf16[136,512]{1,0:T(8,128)(2,1)S(1)}, u32[]{:S(2)}, u32[]{:S(2)}) collective-permute-start(bf16[136,512]{1,0:T(8,128)(2,1)S(1)} %get-tuple-element.25), channel_id=1, source_target_pairs={{0,4},{1,5},{2,6},{3,7},{4,0},{5,1},{6,2},{7,3},{8,12},{9,13},{10,... | collective-permute-start | bytes 417800 | tf_op jit(solution)/shard_map/ppermute | solution.py:29
  8.6 2.5 %collective-permute-done.one = bf16[136,512]{1,0:T(8,128)(2,1)S(1)} collective-permute-done((bf16[136,512]{1,0:T(8,128)(2,1)S(1)}, bf16[136,512]{1,0:T(8,128)(2,1)S(1)}, u32[]{:S(2)}, u32[]{:S(2)}) %collective-permute-start) | collective-permute-done | bytes 139296 | tf_op jit(solution)/shard_map/ppermute | solution.py:29
  11.2 4.0 %collective-permute-done.1.two = bf16[136,512]{1,0:T(8,128)(2,1)S(1)} collective-permute-done((bf16[136,512]{1,0:T(8,128)(2,1)S(1)}, bf16[136,512]{1,0:T(8,128)(2,1)S(1)}, u32[]{:S(2)}, u32[]{:S(2)}) %collective-permute-start.1) | collective-permute-done | bytes 139296 | tf_op jit(solution)/shard_map/ppermute | solution.py:29
  15.3 1.6 %collective-permute-start.3 = (bf16[72,512]{1,0:T(8,128)(2,1)S(1)}, bf16[72,512]{1,0:T(8,128)(2,1)S(1)}, u32[]{:S(2)}, u32[]{:S(2)}) collective-permute-start(bf16[72,512]{1,0:T(8,128)(2,1)S(1)} %get-tuple-element.29), channel_id=1, source_target_pairs={{0,8},{1,9},{2,10},{3,11},{4,12},{5,13},{6,14},{7,15},{8,0},{9,1},... | collective-permute-start | bytes 221192 | tf_op jit(solution)/shard_map/ppermute | solution.py:29
  17.0 2.6 %collective-permute-start.4 = (bf16[72,512]{1,0:T(8,128)(2,1)S(1)}, bf16[72,512]{1,0:T(8,128)(2,1)S(1)}, u32[]{:S(2)}, u32[]{:S(2)}) collective-permute-start(bf16[72,512]{1,0:T(8,128)(2,1)S(1)} %get-tuple-element.30), channel_id=1, source_target_pairs={{0,16},{1,17},{2,18},{3,19},{4,20},{5,21},{6,22},{7,23},{8,24},{9,... | collective-permute-start | bytes 221192 | tf_op jit(solution)/shard_map/ppermute | solution.py:29
  19.6 0.9 %collective-permute-done.3.one = bf16[72,512]{1,0:T(8,128)(2,1)S(1)} collective-permute-done((bf16[72,512]{1,0:T(8,128)(2,1)S(1)}, bf16[72,512]{1,0:T(8,128)(2,1)S(1)}, u32[]{:S(2)}, u32[]{:S(2)}) %collective-permute-start.3) | collective-permute-done | bytes 73760 | tf_op jit(solution)/shard_map/ppermute | solution.py:29
  20.5 2.6 %collective-permute-done.4.two = bf16[72,512]{1,0:T(8,128)(2,1)S(1)} collective-permute-done((bf16[72,512]{1,0:T(8,128)(2,1)S(1)}, bf16[72,512]{1,0:T(8,128)(2,1)S(1)}, u32[]{:S(2)}, u32[]{:S(2)}) %collective-permute-start.4) | collective-permute-done | bytes 73760 | tf_op jit(solution)/shard_map/ppermute | solution.py:29
  23.5 3.4 %collective-permute-start.10 = (bf16[64,512]{1,0:T(8,128)(2,1)S(1)}, bf16[64,512]{1,0:T(8,128)(2,1)S(1)}, u32[]{:S(2)}, u32[]{:S(2)}) collective-permute-start(bf16[64,512]{1,0:T(8,128)(2,1)S(1)} %get-tuple-element.33.mean), channel_id=1, source_target_pairs={{0,24},{1,25},{2,26},{3,27},{4,28},{5,29},{6,30},{7,31},{8,16},{9,... | collective-permute-start | bytes 196616 | tf_op jit(solution)/shard_map/ppermute | solution.py:29
  26.9 1.5 %collective-permute-done.5.got = bf16[72,512]{1,0:T(8,128)(2,1)S(1)} collective-permute-done((bf16[72,512]{1,0:T(8,128)(2,1)S(1)}, bf16[72,512]{1,0:T(8,128)(2,1)S(1)}, u32[]{:S(2)}, u32[]{:S(2)}) %collective-permute-start.5) | collective-permute-done | bytes 73760 | tf_op jit(solution)/shard_map/ppermute | solution.py:29
  28.4 1.3 %collective-permute-start.6 = (bf16[128,512]{1,0:T(8,128)(2,1)S(1)}, bf16[128,512]{1,0:T(8,128)(2,1)S(1)}, u32[]{:S(2)}, u32[]{:S(2)}) collective-permute-start(bf16[128,512]{1,0:T(8,128)(2,1)S(1)} %get-tuple-element.34.refs_0_), channel_id=1, source_target_pairs={{0,2},{1,5},{2,0},{3,7},{4,6},{5,1},{6,4},{7,3},{8,10},{9,13},{10,... | collective-permute-start | bytes 393224 | tf_op jit(solution)/shard_map/ppermute | solution.py:29
  29.7 0.8 %collective-permute-start.7 = (bf16[128,512]{1,0:T(8,128)(2,1)S(1)}, bf16[128,512]{1,0:T(8,128)(2,1)S(1)}, u32[]{:S(2)}, u32[]{:S(2)}) collective-permute-start(bf16[128,512]{1,0:T(8,128)(2,1)S(1)} %get-tuple-element.34.refs_0_), channel_id=1, source_target_pairs={{0,4},{1,3},{2,6},{3,1},{4,0},{5,7},{6,2},{7,5},{8,12},{9,11},{10,... | collective-permute-start | bytes 393224 | tf_op jit(solution)/shard_map/ppermute | solution.py:29
  30.6 1.4 %collective-permute-start.8 = (bf16[128,512]{1,0:T(8,128)(2,1)S(1)}, bf16[128,512]{1,0:T(8,128)(2,1)S(1)}, u32[]{:S(2)}, u32[]{:S(2)}) collective-permute-start(bf16[128,512]{1,0:T(8,128)(2,1)S(1)} %get-tuple-element.34.refs_0_), channel_id=1, source_target_pairs={{0,6},{1,7},{2,4},{3,5},{4,2},{5,3},{6,0},{7,1},{8,14},{9,15},{10,... | collective-permute-start | bytes 393224 | tf_op jit(solution)/shard_map/ppermute | solution.py:29
  32.1 1.3 %collective-permute-start.11 = (bf16[128,512]{1,0:T(8,128)(2,1)S(1)}, bf16[128,512]{1,0:T(8,128)(2,1)S(1)}, u32[]{:S(2)}, u32[]{:S(2)}) collective-permute-start(bf16[128,512]{1,0:T(8,128)(2,1)S(1)} %shard_map.63.refs_0_), channel_id=1, source_target_pairs={{0,2},{1,5},{2,0},{3,7},{4,6},{5,1},{6,4},{7,3},{8,10},{9,13},{10,... | collective-permute-start | bytes 393224 | tf_op jit(solution)/shard_map/ppermute | solution.py:29
  33.3 1.0 %collective-permute-start.12 = (bf16[128,512]{1,0:T(8,128)(2,1)S(1)}, bf16[128,512]{1,0:T(8,128)(2,1)S(1)}, u32[]{:S(2)}, u32[]{:S(2)}) collective-permute-start(bf16[128,512]{1,0:T(8,128)(2,1)S(1)} %shard_map.63.refs_0_), channel_id=1, source_target_pairs={{0,4},{1,3},{2,6},{3,1},{4,0},{5,7},{6,2},{7,5},{8,12},{9,11},{10,... | collective-permute-start | bytes 393224 | tf_op jit(solution)/shard_map/ppermute | solution.py:29
  34.4 1.8 %collective-permute-start.13 = (bf16[128,512]{1,0:T(8,128)(2,1)S(1)}, bf16[128,512]{1,0:T(8,128)(2,1)S(1)}, u32[]{:S(2)}, u32[]{:S(2)}) collective-permute-start(bf16[128,512]{1,0:T(8,128)(2,1)S(1)} %shard_map.63.refs_0_), channel_id=1, source_target_pairs={{0,6},{1,7},{2,4},{3,5},{4,2},{5,3},{6,0},{7,1},{8,14},{9,15},{10,... | collective-permute-start | bytes 393224 | tf_op jit(solution)/shard_map/ppermute | solution.py:29
  36.3 1.4 %collective-permute-done.8.refs_3_ = bf16[128,512]{1,0:T(8,128)(2,1)S(1)} collective-permute-done((bf16[128,512]{1,0:T(8,128)(2,1)S(1)}, bf16[128,512]{1,0:T(8,128)(2,1)S(1)}, u32[]{:S(2)}, u32[]{:S(2)}) %collective-permute-start.8) | collective-permute-done | bytes 131104 | tf_op jit(solution)/shard_map/ppermute | solution.py:29
  37.7 0.7 %shard_map.62 = (f32[1024,512]{1,0:T(8,128)S(1)}, bf16[1024,128]{1,0:T(8,128)(2,1)S(1)}) custom-call(s32[8,128]{1,0:T(8,128)S(1)} %get-tuple-element.32.ids, bf16[128,512]{1,0:T(8,128)(2,1)S(1)} %get-tuple-element.34.refs_0_, bf16[128,512]{1,0:T(8,128)(2,1)S(1)} %collective-permute-done.6.refs_1_, bf16[128,512]{1,0:T(8,128)(2,1)S(1)} %collective-permute-done.7.refs_2_, ...), custom_call_target="tpu_custom_call" | custom-call | tf_op jit(solution)/shard_map/pallas_call | solution.py:324
  38.4 0.6 %collective-permute-done.12.refs_2_ = bf16[128,512]{1,0:T(8,128)(2,1)S(1)} collective-permute-done((bf16[128,512]{1,0:T(8,128)(2,1)S(1)}, bf16[128,512]{1,0:T(8,128)(2,1)S(1)}, u32[]{:S(2)}, u32[]{:S(2)}) %collective-permute-start.12) | collective-permute-done | bytes 131104 | tf_op jit(solution)/shard_map/ppermute | solution.py:29
  39.0 1.4 %collective-permute-done.13.refs_3_ = bf16[128,512]{1,0:T(8,128)(2,1)S(1)} collective-permute-done((bf16[128,512]{1,0:T(8,128)(2,1)S(1)}, bf16[128,512]{1,0:T(8,128)(2,1)S(1)}, u32[]{:S(2)}, u32[]{:S(2)}) %collective-permute-start.13) | collective-permute-done | bytes 131104 | tf_op jit(solution)/shard_map/ppermute | solution.py:29
  40.4 1.5 %shard_map.64 = (bf16[64,512]{1,0:T(8,128)(2,1)}, bf16[64,512]{1,0:T(8,128)(2,1)}, f32[64,512]{1,0:T(8,128)S(1)}, bf16[64,512]{1,0:T(8,128)(2,1)S(1)}) custom-call(s32[8,128]{1,0:T(8,128)S(1)} %get-tuple-element.32.ids, bf16[64,512]{1,0:T(8,128)(2,1)S(1)} %get-tuple-element.33.mean, f32[1024,512]{1,0:T(8,128)S(1)} %get-tuple-element.35.sums, ...), custom_call_target="tpu_custom_call" | custom-call | tf_op jit(solution)/shard_map/pallas_call | solution.py:372
  42.0 1.2 %collective-permute-done.14 = bf16[64,512]{1,0:T(8,128)(2,1)S(1)} collective-permute-done((bf16[64,512]{1,0:T(8,128)(2,1)S(1)}, bf16[64,512]{1,0:T(8,128)(2,1)S(1)}, u32[]{:S(2)}, u32[]{:S(2)}) %collective-permute-start.14) | collective-permute-done | bytes 65568 | tf_op jit(solution)/shard_map/ppermute | solution.py:29
  43.2 0.7 %convert_add_fusion = f32[64,512]{1,0:T(8,128)} fusion(f32[64,512]{1,0:T(8,128)S(1)} %get-tuple-element.39, bf16[64,512]{1,0:T(8,128)(2,1)S(1)} %collective-permute-done.14), kind=kLoop, calls=%fused_computation | loop fusion | flops 65536 | bytes 327680 | tf_op jit(solution)/shard_map/add | solution.py:455
  (14 shorter events, 1.0 us)
Async XLA Ops:
  4.1 7.1 %collective-permute-start = (bf16[136,512]{1,0:T(8,128)(2,1)S(1)}, bf16[136,512]{1,0:T(8,128)(2,1)S(1)}, u32[]{:S(2)}, u32[]{:S(2)}) collective-permute-start(bf16[136,512]{1,0:T(8,128)(2,1)S(1)} %get-tuple-element.24), channel_id=1, source_target_pairs={{0,2},{1,3},{2,0},{3,1},{4,6},{5,7},{6,4},{7,5},{8,10},{9,11},{10,... | collective-permute-start | bytes 417800 | tf_op jit(solution)/shard_map/ppermute | solution.py:29
  7.1 8.1 %collective-permute-start.1 = (bf16[136,512]{1,0:T(8,128)(2,1)S(1)}, bf16[136,512]{1,0:T(8,128)(2,1)S(1)}, u32[]{:S(2)}, u32[]{:S(2)}) collective-permute-start(bf16[136,512]{1,0:T(8,128)(2,1)S(1)} %get-tuple-element.25), channel_id=1, source_target_pairs={{0,4},{1,5},{2,6},{3,7},{4,0},{5,1},{6,2},{7,3},{8,12},{9,13},{10,... | collective-permute-start | bytes 417800 | tf_op jit(solution)/shard_map/ppermute | solution.py:29
  8.6 6.6 %collective-permute-start.2 = (bf16[136,512]{1,0:T(8,128)(2,1)S(1)}, bf16[136,512]{1,0:T(8,128)(2,1)S(1)}, u32[]{:S(2)}, u32[]{:S(2)}) collective-permute-start(bf16[136,512]{1,0:T(8,128)(2,1)S(1)} %get-tuple-element.26), channel_id=1, source_target_pairs={{0,6},{1,7},{2,4},{3,5},{4,2},{5,3},{6,0},{7,1},{8,14},{9,15},{10,... | collective-permute-start | bytes 417800 | tf_op jit(solution)/shard_map/ppermute | solution.py:29
  15.3 5.1 %collective-permute-start.3 = (bf16[72,512]{1,0:T(8,128)(2,1)S(1)}, bf16[72,512]{1,0:T(8,128)(2,1)S(1)}, u32[]{:S(2)}, u32[]{:S(2)}) collective-permute-start(bf16[72,512]{1,0:T(8,128)(2,1)S(1)} %get-tuple-element.29), channel_id=1, source_target_pairs={{0,8},{1,9},{2,10},{3,11},{4,12},{5,13},{6,14},{7,15},{8,0},{9,1},... | collective-permute-start | bytes 221192 | tf_op jit(solution)/shard_map/ppermute | solution.py:29
  17.0 6.0 %collective-permute-start.4 = (bf16[72,512]{1,0:T(8,128)(2,1)S(1)}, bf16[72,512]{1,0:T(8,128)(2,1)S(1)}, u32[]{:S(2)}, u32[]{:S(2)}) collective-permute-start(bf16[72,512]{1,0:T(8,128)(2,1)S(1)} %get-tuple-element.30), channel_id=1, source_target_pairs={{0,16},{1,17},{2,18},{3,19},{4,20},{5,21},{6,22},{7,23},{8,24},{9,... | collective-permute-start | bytes 221192 | tf_op jit(solution)/shard_map/ppermute | solution.py:29
  23.2 5.1 %collective-permute-start.5 = (bf16[72,512]{1,0:T(8,128)(2,1)S(1)}, bf16[72,512]{1,0:T(8,128)(2,1)S(1)}, u32[]{:S(2)}, u32[]{:S(2)}) collective-permute-start(bf16[72,512]{1,0:T(8,128)(2,1)S(1)} %get-tuple-element.31.own), channel_id=1, source_target_pairs={{0,8},{1,9},{2,10},{3,11},{4,12},{5,13},{6,14},{7,15},{8,0},{9,1},... | collective-permute-start | bytes 221192 | tf_op jit(solution)/shard_map/ppermute | solution.py:29
  23.5 8.5 %collective-permute-start.10 = (bf16[64,512]{1,0:T(8,128)(2,1)S(1)}, bf16[64,512]{1,0:T(8,128)(2,1)S(1)}, u32[]{:S(2)}, u32[]{:S(2)}) collective-permute-start(bf16[64,512]{1,0:T(8,128)(2,1)S(1)} %get-tuple-element.33.mean), channel_id=1, source_target_pairs={{0,24},{1,25},{2,26},{3,27},{4,28},{5,29},{6,30},{7,31},{8,16},{9,... | collective-permute-start | bytes 196616 | tf_op jit(solution)/shard_map/ppermute | solution.py:29
  26.9 5.2 %collective-permute-start.9 = (bf16[64,512]{1,0:T(8,128)(2,1)S(1)}, bf16[64,512]{1,0:T(8,128)(2,1)S(1)}, u32[]{:S(2)}, u32[]{:S(2)}) collective-permute-start(bf16[64,512]{1,0:T(8,128)(2,1)S(1)} %get-tuple-element.33.mean), channel_id=1, source_target_pairs={{0,16},{1,17},{2,18},{3,19},{4,20},{5,21},{6,22},{7,23},{8,24},{9,... | collective-permute-start | bytes 196616 | tf_op jit(solution)/shard_map/ppermute | solution.py:29
  28.4 6.0 %collective-permute-start.6 = (bf16[128,512]{1,0:T(8,128)(2,1)S(1)}, bf16[128,512]{1,0:T(8,128)(2,1)S(1)}, u32[]{:S(2)}, u32[]{:S(2)}) collective-permute-start(bf16[128,512]{1,0:T(8,128)(2,1)S(1)} %get-tuple-element.34.refs_0_), channel_id=1, source_target_pairs={{0,2},{1,5},{2,0},{3,7},{4,6},{5,1},{6,4},{7,3},{8,10},{9,13},{10,... | collective-permute-start | bytes 393224 | tf_op jit(solution)/shard_map/ppermute | solution.py:29
  29.7 6.5 %collective-permute-start.7 = (bf16[128,512]{1,0:T(8,128)(2,1)S(1)}, bf16[128,512]{1,0:T(8,128)(2,1)S(1)}, u32[]{:S(2)}, u32[]{:S(2)}) collective-permute-start(bf16[128,512]{1,0:T(8,128)(2,1)S(1)} %get-tuple-element.34.refs_0_), channel_id=1, source_target_pairs={{0,4},{1,3},{2,6},{3,1},{4,0},{5,7},{6,2},{7,5},{8,12},{9,11},{10,... | collective-permute-start | bytes 393224 | tf_op jit(solution)/shard_map/ppermute | solution.py:29
  30.6 7.1 %collective-permute-start.8 = (bf16[128,512]{1,0:T(8,128)(2,1)S(1)}, bf16[128,512]{1,0:T(8,128)(2,1)S(1)}, u32[]{:S(2)}, u32[]{:S(2)}) collective-permute-start(bf16[128,512]{1,0:T(8,128)(2,1)S(1)} %get-tuple-element.34.refs_0_), channel_id=1, source_target_pairs={{0,6},{1,7},{2,4},{3,5},{4,2},{5,3},{6,0},{7,1},{8,14},{9,15},{10,... | collective-permute-start | bytes 393224 | tf_op jit(solution)/shard_map/ppermute | solution.py:29
  32.1 6.3 %collective-permute-start.11 = (bf16[128,512]{1,0:T(8,128)(2,1)S(1)}, bf16[128,512]{1,0:T(8,128)(2,1)S(1)}, u32[]{:S(2)}, u32[]{:S(2)}) collective-permute-start(bf16[128,512]{1,0:T(8,128)(2,1)S(1)} %shard_map.63.refs_0_), channel_id=1, source_target_pairs={{0,2},{1,5},{2,0},{3,7},{4,6},{5,1},{6,4},{7,3},{8,10},{9,13},{10,... | collective-permute-start | bytes 393224 | tf_op jit(solution)/shard_map/ppermute | solution.py:29
  33.3 5.7 %collective-permute-start.12 = (bf16[128,512]{1,0:T(8,128)(2,1)S(1)}, bf16[128,512]{1,0:T(8,128)(2,1)S(1)}, u32[]{:S(2)}, u32[]{:S(2)}) collective-permute-start(bf16[128,512]{1,0:T(8,128)(2,1)S(1)} %shard_map.63.refs_0_), channel_id=1, source_target_pairs={{0,4},{1,3},{2,6},{3,1},{4,0},{5,7},{6,2},{7,5},{8,12},{9,11},{10,... | collective-permute-start | bytes 393224 | tf_op jit(solution)/shard_map/ppermute | solution.py:29
  34.4 6.0 %collective-permute-start.13 = (bf16[128,512]{1,0:T(8,128)(2,1)S(1)}, bf16[128,512]{1,0:T(8,128)(2,1)S(1)}, u32[]{:S(2)}, u32[]{:S(2)}) collective-permute-start(bf16[128,512]{1,0:T(8,128)(2,1)S(1)} %shard_map.63.refs_0_), channel_id=1, source_target_pairs={{0,6},{1,7},{2,4},{3,5},{4,2},{5,3},{6,0},{7,1},{8,14},{9,15},{10,... | collective-permute-start | bytes 393224 | tf_op jit(solution)/shard_map/ppermute | solution.py:29
  41.9 1.3 %collective-permute-start.14 = (bf16[64,512]{1,0:T(8,128)(2,1)S(1)}, bf16[64,512]{1,0:T(8,128)(2,1)S(1)}, u32[]{:S(2)}, u32[]{:S(2)}) collective-permute-start(bf16[64,512]{1,0:T(8,128)(2,1)S(1)} %get-tuple-element.40), channel_id=1, source_target_pairs={{0,1},{1,0},{2,3},{3,2},{4,5},{5,4},{6,7},{7,6},{8,9},{9,8},{10,11... | collective-permute-start | bytes 196616 | tf_op jit(solution)/shard_map/ppermute | solution.py:29

commit v5 on v4

--- a/solution.py
+++ b/solution.py
@@ -58,86 +58,111 @@
     return jnp.where(hit, jnp.ones((), BF16), jnp.zeros((), BF16))
 
 
-def sum_kernel(devices, cent, ids_hbm, rows_hbm, group_hbm, own_ref, own_meta_ref, *rest):
-    sends, (ids_ref, rows_ref, group_ref, totals, arrived) = rest[:-5], rest[-5:]
-    steps, block = rows_ref.shape[:2]
+ORDER = (3, 1, 2, 0)
+
+
+def labelled_sums(start, labels, chunks, label_ref, rows_ref, totals, copies=None):
+    tallies = jnp.zeros((labels, LANES), BF16)
+    for step, (low, high) in enumerate(chunks):
+        one_hot = one_hot_of(labels, label_ref[:, low:high] - start)
+        for at in range(0, high - low, LANES):
+            tallies = tallies + one_hot[:, at : at + LANES]
+        if copies:
+            copies[step].wait()
+        part = jnp.dot(one_hot, rows_ref[low:high], preferred_element_type=F32)
+        if step == 0:
+            totals[...] = part
+        else:
+            totals[...] += part
+    counts = lax.dot_general(
+        jnp.ones((8, LANES), BF16), tallies, (((1,), (1,)), ((), ())), preferred_element_type=F32
+    )
+    return counts[:1]
+
+
+def fill_send(send, sums, counts, id_digits):
+    pair = sums.shape[0]
+    cent = id_digits.shape[1]
+    high, low = split_digits(counts)
+    meta = jnp.concatenate([high, low, jnp.zeros((META - 2, LANES), F32)], axis=0)
+    send[:pair] = sums.astype(BF16)
+    send[pair:, :LANES] = meta.astype(BF16)
+    send[pair:, LANES:] = jnp.zeros((META, send.shape[1] - LANES), BF16)
+    send[pair : pair + 2, LANES : LANES + cent] = id_digits.astype(BF16)
+
+
+def first_kernel(devices, cent, chunks, ids_hbm, rows_hbm, group_hbm, *refs):
+    sends, (rows_ref, label_ref, digits_ref, ids_ref, group_ref, totals, arrived) = refs[:2], refs[2:]
+    steps = len(chunks)
     ids_copy = pltpu.make_async_copy(ids_hbm, ids_ref, arrived.at[steps])
-    ids_copy.start()
     group_copy = pltpu.make_async_copy(group_hbm, group_ref, arrived.at[steps + 1])
     copies = [
-        pltpu.make_async_copy(
-            rows_hbm.at[step * block : (step + 1) * block], rows_ref.at[step], arrived.at[step]
-        )
-        for step in range(steps)
+        pltpu.make_async_copy(rows_hbm.at[low:high], rows_ref.at[low:high], arrived.at[step])
+        for step, (low, high) in enumerate(chunks)
     ]
+    ids_copy.start()
     for copy in copies:
         copy.start()
     group_copy.start()
     position = lax.axis_index("dp")
     mate = position % GROUP
-    labels = 2 * GROUP * cent
+    pair = 2 * cent
     ids_copy.wait()
-    tallies = jnp.zeros((labels, LANES), BF16)
-    for step in range(steps):
-        offset = ids_ref[:, step * block : (step + 1) * block] - position * cent
-        offset = jnp.where(offset < 0, offset + devices * cent, offset)
-        ahead = offset // cent + mate
-        partner = (ahead % GROUP) ^ mate
-        slot = jnp.where(ahead // GROUP == 1, 1, 0)
-        label = partner * (2 * cent) + slot * cent + offset % cent
-        one_hot = one_hot_of(labels, label)
-        for start in range(0, block, LANES):
-            tallies = tallies + one_hot[:, start : start + LANES]
-        copies[step].wait()
-        part = jnp.dot(one_hot, rows_ref[step], preferred_element_type=F32)
-        if step == 0:
-            totals[...] = part
-        else:
-            totals[...] += part
+    offset = ids_ref[...] - position * cent
+    offset = jnp.where(offset < 0, offset + devices * cent, offset)
+    ahead = offset // cent + mate
+    partner = (ahead % GROUP) ^ mate
+    place = jnp.zeros_like(partner)
+    for index, who in enumerate(ORDER):
+        place = jnp.where(partner == who, index, place)
+    slot = jnp.where(ahead // GROUP == 1, 1, 0)
+    label_ref[...] = place * pair + slot * cent + offset % cent
+    counts = labelled_sums(0, 2 * pair, chunks, label_ref, rows_ref, totals, copies)
     group_copy.wait()
-    id_high, id_low = split_digits(group_ref[...].astype(F32))
-    id_digits = jnp.concatenate([id_high, id_low], axis=0)
-    counts = lax.dot_general(
-        jnp.ones((8, LANES), BF16), tallies, (((1,), (1,)), ((), ())), preferred_element_type=F32
-    )
+    digits = jnp.concatenate(split_digits(group_ref[...].astype(F32)), axis=0)
+    digits_ref[...] = digits
+    for index, send in enumerate(sends):
+        at = index * pair
+        fill_send(send, totals[at : at + pair], counts[:, at : at + pair], digits)
+
+
+def second_kernel(cent, chunks, label_ref, rows_ref, digits_ref, send, own_ref, own_meta_ref, totals):
     pair = 2 * cent
-    own_ref[...] = totals[:pair]
-    for index in range(GROUP):
-        high, low = split_digits(counts[:1, index * pair : (index + 1) * pair])
-        meta = jnp.concatenate([high, low, jnp.zeros((META - 2, LANES), F32)], axis=0)
-        if index == 0:
-            own_meta_ref[:, :LANES] = meta
-            own_meta_ref[:, LANES:] = jnp.zeros((META, LANES), F32)
-            own_meta_ref[:2, LANES : LANES + cent] = id_digits
-        else:
-            send = sends[index - 1]
-            send[:pair] = totals[index * pair : (index + 1) * pair].astype(BF16)
-            send[pair:, :LANES] = meta.astype(BF16)
-            send[pair:, LANES:] = jnp.zeros((META, send.shape[1] - LANES), BF16)
-            send[pair : pair + 2, LANES : LANES + cent] = id_digits.astype(BF16)
+    counts = labelled_sums(2 * pair, 2 * pair, chunks, label_ref, rows_ref, totals)
+    digits = digits_ref[...]
+    fill_send(send, totals[:pair], counts[:, :pair], digits)
+    own_ref[...] = totals[pair:]
+    high, low = split_digits(counts[:, pair:])
+    meta = jnp.concatenate([high, low, jnp.zeros((META - 2, LANES), F32)], axis=0)
+    own_meta_ref[:, :LANES] = meta
+    own_meta_ref[:, LANES:] = jnp.zeros((META, LANES), F32)
+    own_meta_ref[:2, LANES : LANES + cent] = digits
 
 
 def band_sums(devices, cent, ids, rows, group):
     count, width = rows.shape
-    steps = 4
-    block = count // steps
     pair = 2 * cent
     send = jax.ShapeDtypeStruct((pair + META, width), BF16)
-    return pl.pallas_call(
-        functools.partial(sum_kernel, devices, cent),
-        in_specs=[pl.BlockSpec(memory_space=pltpu.HBM)] * 3,
-        out_specs=[whole()] * (GROUP + 1),
+    edges = [count * part // 12 for part in (0, 3, 6, 9, 12)]
+    chunks = list(zip(edges[:-1], edges[1:]))
+    half = count // 2
+    hbm = pl.BlockSpec(memory_space=pltpu.HBM)
+    one, two, rows, label, digits = pl.pallas_call(
+        functools.partial(first_kernel, devices, cent, chunks),
+        in_specs=[hbm] * 3,
+        out_specs=[whole()] * 5,
         out_shape=[
-            jax.ShapeDtypeStruct((pair, width), F32),
-            jax.ShapeDtypeStruct((META, 2 * LANES), F32),
-        ]
-        + [send] * (GROUP - 1),
+            send,
+            send,
+            jax.ShapeDtypeStruct((count, width), BF16),
+            jax.ShapeDtypeStruct((1, count), jnp.int32),
+            jax.ShapeDtypeStruct((2, cent), F32),
+        ],
         scratch_shapes=[
             pltpu.VMEM((1, count), jnp.int32),
-            pltpu.VMEM((steps, block, width), BF16),
             pltpu.VMEM((1, cent), jnp.int32),
-            pltpu.VMEM((GROUP * pair, width), F32),
-            pltpu.SemaphoreType.DMA((steps + 2,)),
+            pltpu.VMEM((2 * pair, width), F32),
+            pltpu.SemaphoreType.DMA((len(chunks) + 2,)),
         ],
         compiler_params=small(),
     )(
@@ -145,9 +170,26 @@
         pltpu.with_memory_space_constraint(rows, pltpu.HBM),
         pltpu.with_memory_space_constraint(group.reshape(1, cent), pltpu.HBM),
     )
-
-
-def group_kernel(cent, four, own, own_meta, one, two, three, base_ref, base_meta_ref, next_ref, far_ref):
+    three, own, own_meta = pl.pallas_call(
+        functools.partial(second_kernel, cent, [(0, half), (half, count)]),
+        in_specs=[whole()] * 3,
+        out_specs=[whole()] * 3,
+        out_shape=[
+            send,
+            jax.ShapeDtypeStruct((pair, width), F32),
+            jax.ShapeDtypeStruct((META, 2 * LANES), F32),
+        ],
+        cost_estimate=pl.CostEstimate(flops=100000000000, bytes_accessed=300000000, transcendentals=0),
+        scratch_shapes=[pltpu.VMEM((2 * pair, width), F32)],
+        compiler_params=small(),
+    )(label, rows, digits)
+    sends = [None] * GROUP
+    for index, send in zip(ORDER, (one, two, three)):
+        sends[index] = send
+    return own, own_meta, *sends[1:]
+
+
+def group_kernel(cent, four, three, one, two, own, own_meta, base_ref, base_meta_ref, next_ref, far_ref):
     mate = lax.axis_index("dp") % GROUP
     pair = 2 * cent
     lane = iota((1, LANES), 1)
@@ -205,10 +247,10 @@
             send,
         ],
         compiler_params=small(),
-    )(own, own_meta, *got)
-
-
-def mean_kernel(cent, base, base_meta, one, two, mean_ref, send_ref):
+    )(got[2], got[0], got[1], own, own_meta)
+
+
+def mean_kernel(cent, two, one, base, base_meta, mean_ref, send_ref):
     sums = base[...] + one[:cent].astype(F32) + two[:cent].astype(F32)
     metas = [meta[...].astype(F32) for meta in (base_meta, one.at[cent:], two.at[cent:])]
     rows = [meta[0:1, :LANES] * BASE + meta[1:2, :LANES] for meta in metas]
@@ -232,7 +274,7 @@
         out_specs=[whole()] * 2,
         out_shape=[mean, jax.ShapeDtypeStruct((cent + META, width), BF16)],
         compiler_params=small(),
-    )(base, base_meta, *got)
+    )(got[1], got[0], base, base_meta)
 
 
 def near_kernel(cent, own, got, near_ref, ids_ref):
@@ -273,7 +315,7 @@
     )(own, got)
 
 
-def join_kernel(first, second, out_ref):
+def join_kernel(second, first, out_ref):
     rows = first.shape[0]
     out_ref[:rows] = first[...]
     out_ref[rows:] = second[...]
@@ -288,7 +330,7 @@
         out_shape=jax.ShapeDtypeStruct((2 * rows, width), BF16),
         cost_estimate=pl.CostEstimate(flops=100000000000, bytes_accessed=300000000, transcendentals=0),
         compiler_params=small(),
-    )(first, second)
+    )(second, first)
 
 
 def ids_row(ids, base, order):
@@ -422,7 +464,10 @@
         )
 
     own, own_meta, *sends = band_sums(devices, cent, first_level, embeddings, second_level)
-    got = [partner(send, index + 1) for index, send in enumerate(sends)]
+    got = [None] * GROUP
+    for index in ORDER[:-1]:
+        got[index] = partner(sends[index - 1], index)
+    got = got[1:]
     four = devices == GROUP * GROUP and cores == 2 and devices * cent <= K2
     base, base_meta, following, far = group_sums(cent, four, own, own_meta, got)
     if four:

time: 44.1 us -> 43 us (0.975)
  waiting for transfers between devices: 16.4 us -> 13.6 us
  starting transfers between devices: 20.1 us -> 21.8 us
    ppermute x15, waiting for transfers between devices: 16.4 us -> 13.6 us  [exchanged(): return lax.ppermute(value, ('dp', 'mp'), pairs)]
    ppermute x15, starting transfers between devices: 20.1 us -> 21.8 us  [exchanged(): return lax.ppermute(value, ('dp', 'mp'), pairs)]
    pallas_call x1 -> x2, Pallas kernels: 3.44 us -> 3.43 us  [the longest x1 2.43 us: band_sums(): pl.pallas_call(functools.partial(first_kernel, devices, cent, chunks), in...]
  transfers between devices with their start and end apart: 15 -> 15, of which waited for: 10 -> 11; matrix products, arithmetic and copies ran while one was open for 0% -> 0% of each run, Pallas kernels for 2% -> 4%
where the time goes in v5:
time: 43 us; the launch traced here: 42.8 us
  starting transfers between devices  21.8 us (51%)
  waiting for transfers between devices  13.6 us (32%)
  Pallas kernels  6.07 us (14%)
  between operations  0.7 us (2%)
  other arithmetic  0.67 us (2%)
    ppermute x15, starting transfers between devices, exchanged(): return lax.ppermute(value, ('dp', 'mp'), pairs)  21.8 us
    ppermute x15, waiting for transfers between devices, exchanged(): return lax.ppermute(value, ('dp', 'mp'), pairs)  13.6 us
    pallas_call x1, Pallas kernels, band_sums(): pl.pallas_call(functools.partial(first_kernel, devices, cent, chunks), in...  2.43 us
    pallas_call x1, Pallas kernels, second_level_scores(): pl.pallas_call(functools.partial(score_kernel, owned), in_specs=[whole()]...  1.51 us
    pallas_call x1, Pallas kernels, band_sums(): pl.pallas_call(functools.partial(second_kernel, cent, [(0, half), (half,...  1.01 us
  transfers between devices with their start and end apart: 15, of which 11 were waited for; matrix products, arithmetic and copies ran while one was open for 0% of the time, Pallas kernels for 4%

profile of v5, /device:TPU:0, one launch (start us, length us, event | category | flops | bytes accessed | tf_op | source)
XLA Modules:
  0.0 42.8 jit_solution(814828810517516699)
XLA Ops:
  0.6 2.4 %shard_map.58 = (bf16[136,512]{1,0:T(8,128)(2,1)S(1)}, bf16[136,512]{1,0:T(8,128)(2,1)S(1)}, bf16[3072,512]{1,0:T(8,128)(2,1)S(1)}, s32[1,3072]{1,0:T(1,128)S(1)}, f32[2,64]{1,0:T(2,128)S(1)}) custom-call(s32[1,3072]{1,0:T(1,128)} %bitcast.2, bf16[3072,512]{1,0:T(8,128)(2,1)} %rows_hbm.1, s32[1,64]{1,0:T(1,128)} %bitcast.3), custom_call_target="tpu_custom_call" | custom-call | tf_op jit(solution)/shard_map/pallas_call | solution.py:150
  3.1 4.0 %collective-permute-start = (bf16[136,512]{1,0:T(8,128)(2,1)S(1)}, bf16[136,512]{1,0:T(8,128)(2,1)S(1)}, u32[]{:S(2)}, u32[]{:S(2)}) collective-permute-start(bf16[136,512]{1,0:T(8,128)(2,1)S(1)} %get-tuple-element.25), channel_id=1, source_target_pairs={{0,6},{1,7},{2,4},{3,5},{4,2},{5,3},{6,0},{7,1},{8,14},{9,15},{10,... | collective-permute-start | bytes 417800 | tf_op jit(solution)/shard_map/ppermute | solution.py:29
  7.6 1.0 %shard_map.59 = (bf16[136,512]{1,0:T(8,128)(2,1)S(1)}, f32[128,512]{1,0:T(8,128)S(1)}, f32[8,256]{1,0:T(8,128)S(1)}) custom-call(s32[1,3072]{1,0:T(1,128)S(1)} %get-tuple-element.27.label_ref, bf16[3072,512]{1,0:T(8,128)(2,1)S(1)} %get-tuple-element.28.rows_ref, f32[2,64]{1,0:T(2,128)S(1)} %get-tuple-element.29.digits_ref), custom_call_target="tpu_custom_call" | custom-call | flops 99999997952 | bytes 300000000 | tf_op jit(solution)/shard_map/pallas_call | solution.py:173
  8.7 2.8 %collective-permute-done.three = bf16[136,512]{1,0:T(8,128)(2,1)S(1)} collective-permute-done((bf16[136,512]{1,0:T(8,128)(2,1)S(1)}, bf16[136,512]{1,0:T(8,128)(2,1)S(1)}, u32[]{:S(2)}, u32[]{:S(2)}) %collective-permute-start) | collective-permute-done | bytes 139296 | tf_op jit(solution)/shard_map/ppermute | solution.py:29
  11.5 2.4 %collective-permute-done.1.one = bf16[136,512]{1,0:T(8,128)(2,1)S(1)} collective-permute-done((bf16[136,512]{1,0:T(8,128)(2,1)S(1)}, bf16[136,512]{1,0:T(8,128)(2,1)S(1)}, u32[]{:S(2)}, u32[]{:S(2)}) %collective-permute-start.1) | collective-permute-done | bytes 139296 | tf_op jit(solution)/shard_map/ppermute | solution.py:29
  14.2 2.9 %collective-permute-start.3 = (bf16[72,512]{1,0:T(8,128)(2,1)S(1)}, bf16[72,512]{1,0:T(8,128)(2,1)S(1)}, u32[]{:S(2)}, u32[]{:S(2)}) collective-permute-start(bf16[72,512]{1,0:T(8,128)(2,1)S(1)} %get-tuple-element.33), channel_id=1, source_target_pairs={{0,16},{1,17},{2,18},{3,19},{4,20},{5,21},{6,22},{7,23},{8,24},{9,... | collective-permute-start | bytes 221192 | tf_op jit(solution)/shard_map/ppermute | solution.py:29
  17.1 1.6 %collective-permute-start.4 = (bf16[72,512]{1,0:T(8,128)(2,1)S(1)}, bf16[72,512]{1,0:T(8,128)(2,1)S(1)}, u32[]{:S(2)}, u32[]{:S(2)}) collective-permute-start(bf16[72,512]{1,0:T(8,128)(2,1)S(1)} %get-tuple-element.34), channel_id=1, source_target_pairs={{0,8},{1,9},{2,10},{3,11},{4,12},{5,13},{6,14},{7,15},{8,0},{9,1},... | collective-permute-start | bytes 221192 | tf_op jit(solution)/shard_map/ppermute | solution.py:29
  18.6 1.1 %collective-permute-done.3.two = bf16[72,512]{1,0:T(8,128)(2,1)S(1)} collective-permute-done((bf16[72,512]{1,0:T(8,128)(2,1)S(1)}, bf16[72,512]{1,0:T(8,128)(2,1)S(1)}, u32[]{:S(2)}, u32[]{:S(2)}) %collective-permute-start.3) | collective-permute-done | bytes 73760 | tf_op jit(solution)/shard_map/ppermute | solution.py:29
  19.8 1.6 %collective-permute-done.4.one = bf16[72,512]{1,0:T(8,128)(2,1)S(1)} collective-permute-done((bf16[72,512]{1,0:T(8,128)(2,1)S(1)}, bf16[72,512]{1,0:T(8,128)(2,1)S(1)}, u32[]{:S(2)}, u32[]{:S(2)}) %collective-permute-start.4) | collective-permute-done | bytes 73760 | tf_op jit(solution)/shard_map/ppermute | solution.py:29
  21.6 1.6 %collective-permute-start.5 = (bf16[72,512]{1,0:T(8,128)(2,1)S(1)}, bf16[72,512]{1,0:T(8,128)(2,1)S(1)}, u32[]{:S(2)}, u32[]{:S(2)}) collective-permute-start(bf16[72,512]{1,0:T(8,128)(2,1)S(1)} %get-tuple-element.37.own), channel_id=1, source_target_pairs={{0,8},{1,9},{2,10},{3,11},{4,12},{5,13},{6,14},{7,15},{8,0},{9,1},... | collective-permute-start | bytes 221192 | tf_op jit(solution)/shard_map/ppermute | solution.py:29
  23.2 1.6 %collective-permute-start.10 = (bf16[64,512]{1,0:T(8,128)(2,1)S(1)}, bf16[64,512]{1,0:T(8,128)(2,1)S(1)}, u32[]{:S(2)}, u32[]{:S(2)}) collective-permute-start(bf16[64,512]{1,0:T(8,128)(2,1)S(1)} %get-tuple-element.39.mean), channel_id=1, source_target_pairs={{0,16},{1,17},{2,18},{3,19},{4,20},{5,21},{6,22},{7,23},{8,24},{9,... | collective-permute-start | bytes 196616 | tf_op jit(solution)/shard_map/ppermute | solution.py:29
  24.8 1.2 %collective-permute-start.9 = (bf16[64,512]{1,0:T(8,128)(2,1)S(1)}, bf16[64,512]{1,0:T(8,128)(2,1)S(1)}, u32[]{:S(2)}, u32[]{:S(2)}) collective-permute-start(bf16[64,512]{1,0:T(8,128)(2,1)S(1)} %get-tuple-element.39.mean), channel_id=1, source_target_pairs={{0,24},{1,25},{2,26},{3,27},{4,28},{5,29},{6,30},{7,31},{8,16},{9,... | collective-permute-start | bytes 196616 | tf_op jit(solution)/shard_map/ppermute | solution.py:29
  26.6 2.1 %collective-permute-start.8 = (bf16[128,512]{1,0:T(8,128)(2,1)S(1)}, bf16[128,512]{1,0:T(8,128)(2,1)S(1)}, u32[]{:S(2)}, u32[]{:S(2)}) collective-permute-start(bf16[128,512]{1,0:T(8,128)(2,1)S(1)} %get-tuple-element.40.refs_0_), channel_id=1, source_target_pairs={{0,6},{1,7},{2,4},{3,5},{4,2},{5,3},{6,0},{7,1},{8,14},{9,15},{10,... | collective-permute-start | bytes 393224 | tf_op jit(solution)/shard_map/ppermute | solution.py:29
  28.7 1.0 %collective-permute-start.7 = (bf16[128,512]{1,0:T(8,128)(2,1)S(1)}, bf16[128,512]{1,0:T(8,128)(2,1)S(1)}, u32[]{:S(2)}, u32[]{:S(2)}) collective-permute-start(bf16[128,512]{1,0:T(8,128)(2,1)S(1)} %get-tuple-element.40.refs_0_), channel_id=1, source_target_pairs={{0,4},{1,3},{2,6},{3,1},{4,0},{5,7},{6,2},{7,5},{8,12},{9,11},{10,... | collective-permute-start | bytes 393224 | tf_op jit(solution)/shard_map/ppermute | solution.py:29
  30.2 0.7 %collective-permute-done.9.second = bf16[64,512]{1,0:T(8,128)(2,1)S(1)} collective-permute-done((bf16[64,512]{1,0:T(8,128)(2,1)S(1)}, bf16[64,512]{1,0:T(8,128)(2,1)S(1)}, u32[]{:S(2)}, u32[]{:S(2)}) %collective-permute-start.9) | collective-permute-done | bytes 65568 | tf_op jit(solution)/shard_map/ppermute | solution.py:29
  30.9 2.2 %collective-permute-start.13 = (bf16[128,512]{1,0:T(8,128)(2,1)S(1)}, bf16[128,512]{1,0:T(8,128)(2,1)S(1)}, u32[]{:S(2)}, u32[]{:S(2)}) collective-permute-start(bf16[128,512]{1,0:T(8,128)(2,1)S(1)} %shard_map.64.refs_0_), channel_id=1, source_target_pairs={{0,6},{1,7},{2,4},{3,5},{4,2},{5,3},{6,0},{7,1},{8,14},{9,15},{10,... | collective-permute-start | bytes 393224 | tf_op jit(solution)/shard_map/ppermute | solution.py:29
  33.1 0.9 %collective-permute-start.12 = (bf16[128,512]{1,0:T(8,128)(2,1)S(1)}, bf16[128,512]{1,0:T(8,128)(2,1)S(1)}, u32[]{:S(2)}, u32[]{:S(2)}) collective-permute-start(bf16[128,512]{1,0:T(8,128)(2,1)S(1)} %shard_map.64.refs_0_), channel_id=1, source_target_pairs={{0,4},{1,3},{2,6},{3,1},{4,0},{5,7},{6,2},{7,5},{8,12},{9,11},{10,... | collective-permute-start | bytes 393224 | tf_op jit(solution)/shard_map/ppermute | solution.py:29
  34.0 1.5 %collective-permute-start.11 = (bf16[128,512]{1,0:T(8,128)(2,1)S(1)}, bf16[128,512]{1,0:T(8,128)(2,1)S(1)}, u32[]{:S(2)}, u32[]{:S(2)}) collective-permute-start(bf16[128,512]{1,0:T(8,128)(2,1)S(1)} %shard_map.64.refs_0_), channel_id=1, source_target_pairs={{0,2},{1,5},{2,0},{3,7},{4,6},{5,1},{6,4},{7,3},{8,10},{9,13},{10,... | collective-permute-start | bytes 393224 | tf_op jit(solution)/shard_map/ppermute | solution.py:29
  35.5 0.9 %collective-permute-done.7.refs_2_ = bf16[128,512]{1,0:T(8,128)(2,1)S(1)} collective-permute-done((bf16[128,512]{1,0:T(8,128)(2,1)S(1)}, bf16[128,512]{1,0:T(8,128)(2,1)S(1)}, u32[]{:S(2)}, u32[]{:S(2)}) %collective-permute-start.7) | collective-permute-done | bytes 131104 | tf_op jit(solution)/shard_map/ppermute | solution.py:29
  36.5 0.7 %shard_map.63 = (f32[1024,512]{1,0:T(8,128)S(1)}, bf16[1024,128]{1,0:T(8,128)(2,1)S(1)}) custom-call(s32[8,128]{1,0:T(8,128)S(1)} %get-tuple-element.38.ids, bf16[128,512]{1,0:T(8,128)(2,1)S(1)} %get-tuple-element.40.refs_0_, bf16[128,512]{1,0:T(8,128)(2,1)S(1)} %collective-permute-done.6.refs_1_, bf16[128,512]{1,0:T(8,128)(2,1)S(1)} %collective-permute-done.7.refs_2_, ...), custom_call_target="tpu_custom_call" | custom-call | tf_op jit(solution)/shard_map/pallas_call | solution.py:366
  37.2 0.8 %collective-permute-done.13.refs_3_ = bf16[128,512]{1,0:T(8,128)(2,1)S(1)} collective-permute-done((bf16[128,512]{1,0:T(8,128)(2,1)S(1)}, bf16[128,512]{1,0:T(8,128)(2,1)S(1)}, u32[]{:S(2)}, u32[]{:S(2)}) %collective-permute-start.13) | collective-permute-done | bytes 131104 | tf_op jit(solution)/shard_map/ppermute | solution.py:29
  38.0 1.3 %collective-permute-done.12.refs_2_ = bf16[128,512]{1,0:T(8,128)(2,1)S(1)} collective-permute-done((bf16[128,512]{1,0:T(8,128)(2,1)S(1)}, bf16[128,512]{1,0:T(8,128)(2,1)S(1)}, u32[]{:S(2)}, u32[]{:S(2)}) %collective-permute-start.12) | collective-permute-done | bytes 131104 | tf_op jit(solution)/shard_map/ppermute | solution.py:29
  39.3 1.5 %shard_map.65 = (bf16[64,512]{1,0:T(8,128)(2,1)}, bf16[64,512]{1,0:T(8,128)(2,1)}, f32[64,512]{1,0:T(8,128)S(1)}, bf16[64,512]{1,0:T(8,128)(2,1)S(1)}) custom-call(s32[8,128]{1,0:T(8,128)S(1)} %get-tuple-element.38.ids, bf16[64,512]{1,0:T(8,128)(2,1)S(1)} %get-tuple-element.39.mean, f32[1024,512]{1,0:T(8,128)S(1)} %get-tuple-element.41.sums, ...), custom_call_target="tpu_custom_call" | custom-call | tf_op jit(solution)/shard_map/pallas_call | solution.py:414
  40.9 1.2 %collective-permute-done.14 = bf16[64,512]{1,0:T(8,128)(2,1)S(1)} collective-permute-done((bf16[64,512]{1,0:T(8,128)(2,1)S(1)}, bf16[64,512]{1,0:T(8,128)(2,1)S(1)}, u32[]{:S(2)}, u32[]{:S(2)}) %collective-permute-start.14) | collective-permute-done | bytes 65568 | tf_op jit(solution)/shard_map/ppermute | solution.py:29
  (15 shorter events, 3.0 us)
Async XLA Ops:
  3.1 8.5 %collective-permute-start = (bf16[136,512]{1,0:T(8,128)(2,1)S(1)}, bf16[136,512]{1,0:T(8,128)(2,1)S(1)}, u32[]{:S(2)}, u32[]{:S(2)}) collective-permute-start(bf16[136,512]{1,0:T(8,128)(2,1)S(1)} %get-tuple-element.25), channel_id=1, source_target_pairs={{0,6},{1,7},{2,4},{3,5},{4,2},{5,3},{6,0},{7,1},{8,14},{9,15},{10,... | collective-permute-start | bytes 417800 | tf_op jit(solution)/shard_map/ppermute | solution.py:29
  7.0 6.9 %collective-permute-start.1 = (bf16[136,512]{1,0:T(8,128)(2,1)S(1)}, bf16[136,512]{1,0:T(8,128)(2,1)S(1)}, u32[]{:S(2)}, u32[]{:S(2)}) collective-permute-start(bf16[136,512]{1,0:T(8,128)(2,1)S(1)} %get-tuple-element.26), channel_id=1, source_target_pairs={{0,2},{1,3},{2,0},{3,1},{4,6},{5,7},{6,4},{7,5},{8,10},{9,11},{10,... | collective-permute-start | bytes 417800 | tf_op jit(solution)/shard_map/ppermute | solution.py:29
  8.6 5.4 %collective-permute-start.2 = (bf16[136,512]{1,0:T(8,128)(2,1)S(1)}, bf16[136,512]{1,0:T(8,128)(2,1)S(1)}, u32[]{:S(2)}, u32[]{:S(2)}) collective-permute-start(bf16[136,512]{1,0:T(8,128)(2,1)S(1)} %get-tuple-element.30), channel_id=1, source_target_pairs={{0,4},{1,5},{2,6},{3,7},{4,0},{5,1},{6,2},{7,3},{8,12},{9,13},{10,... | collective-permute-start | bytes 417800 | tf_op jit(solution)/shard_map/ppermute | solution.py:29
  14.2 5.6 %collective-permute-start.3 = (bf16[72,512]{1,0:T(8,128)(2,1)S(1)}, bf16[72,512]{1,0:T(8,128)(2,1)S(1)}, u32[]{:S(2)}, u32[]{:S(2)}) collective-permute-start(bf16[72,512]{1,0:T(8,128)(2,1)S(1)} %get-tuple-element.33), channel_id=1, source_target_pairs={{0,16},{1,17},{2,18},{3,19},{4,20},{5,21},{6,22},{7,23},{8,24},{9,... | collective-permute-start | bytes 221192 | tf_op jit(solution)/shard_map/ppermute | solution.py:29
  17.1 4.4 %collective-permute-start.4 = (bf16[72,512]{1,0:T(8,128)(2,1)S(1)}, bf16[72,512]{1,0:T(8,128)(2,1)S(1)}, u32[]{:S(2)}, u32[]{:S(2)}) collective-permute-start(bf16[72,512]{1,0:T(8,128)(2,1)S(1)} %get-tuple-element.34), channel_id=1, source_target_pairs={{0,8},{1,9},{2,10},{3,11},{4,12},{5,13},{6,14},{7,15},{8,0},{9,1},... | collective-permute-start | bytes 221192 | tf_op jit(solution)/shard_map/ppermute | solution.py:29
  21.6 4.9 %collective-permute-start.5 = (bf16[72,512]{1,0:T(8,128)(2,1)S(1)}, bf16[72,512]{1,0:T(8,128)(2,1)S(1)}, u32[]{:S(2)}, u32[]{:S(2)}) collective-permute-start(bf16[72,512]{1,0:T(8,128)(2,1)S(1)} %get-tuple-element.37.own), channel_id=1, source_target_pairs={{0,8},{1,9},{2,10},{3,11},{4,12},{5,13},{6,14},{7,15},{8,0},{9,1},... | collective-permute-start | bytes 221192 | tf_op jit(solution)/shard_map/ppermute | solution.py:29
  23.2 7.0 %collective-permute-start.10 = (bf16[64,512]{1,0:T(8,128)(2,1)S(1)}, bf16[64,512]{1,0:T(8,128)(2,1)S(1)}, u32[]{:S(2)}, u32[]{:S(2)}) collective-permute-start(bf16[64,512]{1,0:T(8,128)(2,1)S(1)} %get-tuple-element.39.mean), channel_id=1, source_target_pairs={{0,16},{1,17},{2,18},{3,19},{4,20},{5,21},{6,22},{7,23},{8,24},{9,... | collective-permute-start | bytes 196616 | tf_op jit(solution)/shard_map/ppermute | solution.py:29
  24.8 6.1 %collective-permute-start.9 = (bf16[64,512]{1,0:T(8,128)(2,1)S(1)}, bf16[64,512]{1,0:T(8,128)(2,1)S(1)}, u32[]{:S(2)}, u32[]{:S(2)}) collective-permute-start(bf16[64,512]{1,0:T(8,128)(2,1)S(1)} %get-tuple-element.39.mean), channel_id=1, source_target_pairs={{0,24},{1,25},{2,26},{3,27},{4,28},{5,29},{6,30},{7,31},{8,16},{9,... | collective-permute-start | bytes 196616 | tf_op jit(solution)/shard_map/ppermute | solution.py:29
  26.6 7.3 %collective-permute-start.8 = (bf16[128,512]{1,0:T(8,128)(2,1)S(1)}, bf16[128,512]{1,0:T(8,128)(2,1)S(1)}, u32[]{:S(2)}, u32[]{:S(2)}) collective-permute-start(bf16[128,512]{1,0:T(8,128)(2,1)S(1)} %get-tuple-element.40.refs_0_), channel_id=1, source_target_pairs={{0,6},{1,7},{2,4},{3,5},{4,2},{5,3},{6,0},{7,1},{8,14},{9,15},{10,... | collective-permute-start | bytes 393224 | tf_op jit(solution)/shard_map/ppermute | solution.py:29
  28.7 7.8 %collective-permute-start.7 = (bf16[128,512]{1,0:T(8,128)(2,1)S(1)}, bf16[128,512]{1,0:T(8,128)(2,1)S(1)}, u32[]{:S(2)}, u32[]{:S(2)}) collective-permute-start(bf16[128,512]{1,0:T(8,128)(2,1)S(1)} %get-tuple-element.40.refs_0_), channel_id=1, source_target_pairs={{0,4},{1,3},{2,6},{3,1},{4,0},{5,7},{6,2},{7,5},{8,12},{9,11},{10,... | collective-permute-start | bytes 393224 | tf_op jit(solution)/shard_map/ppermute | solution.py:29
  29.7 6.8 %collective-permute-start.6 = (bf16[128,512]{1,0:T(8,128)(2,1)S(1)}, bf16[128,512]{1,0:T(8,128)(2,1)S(1)}, u32[]{:S(2)}, u32[]{:S(2)}) collective-permute-start(bf16[128,512]{1,0:T(8,128)(2,1)S(1)} %get-tuple-element.40.refs_0_), channel_id=1, source_target_pairs={{0,2},{1,5},{2,0},{3,7},{4,6},{5,1},{6,4},{7,3},{8,10},{9,13},{10,... | collective-permute-start | bytes 393224 | tf_op jit(solution)/shard_map/ppermute | solution.py:29
  30.9 7.0 %collective-permute-start.13 = (bf16[128,512]{1,0:T(8,128)(2,1)S(1)}, bf16[128,512]{1,0:T(8,128)(2,1)S(1)}, u32[]{:S(2)}, u32[]{:S(2)}) collective-permute-start(bf16[128,512]{1,0:T(8,128)(2,1)S(1)} %shard_map.64.refs_0_), channel_id=1, source_target_pairs={{0,6},{1,7},{2,4},{3,5},{4,2},{5,3},{6,0},{7,1},{8,14},{9,15},{10,... | collective-permute-start | bytes 393224 | tf_op jit(solution)/shard_map/ppermute | solution.py:29
  33.1 6.2 %collective-permute-start.12 = (bf16[128,512]{1,0:T(8,128)(2,1)S(1)}, bf16[128,512]{1,0:T(8,128)(2,1)S(1)}, u32[]{:S(2)}, u32[]{:S(2)}) collective-permute-start(bf16[128,512]{1,0:T(8,128)(2,1)S(1)} %shard_map.64.refs_0_), channel_id=1, source_target_pairs={{0,4},{1,3},{2,6},{3,1},{4,0},{5,7},{6,2},{7,5},{8,12},{9,11},{10,... | collective-permute-start | bytes 393224 | tf_op jit(solution)/shard_map/ppermute | solution.py:29
  34.0 5.3 %collective-permute-start.11 = (bf16[128,512]{1,0:T(8,128)(2,1)S(1)}, bf16[128,512]{1,0:T(8,128)(2,1)S(1)}, u32[]{:S(2)}, u32[]{:S(2)}) collective-permute-start(bf16[128,512]{1,0:T(8,128)(2,1)S(1)} %shard_map.64.refs_0_), channel_id=1, source_target_pairs={{0,2},{1,5},{2,0},{3,7},{4,6},{5,1},{6,4},{7,3},{8,10},{9,13},{10,... | collective-permute-start | bytes 393224 | tf_op jit(solution)/shard_map/ppermute | solution.py:29
  40.8 1.3 %collective-permute-start.14 = (bf16[64,512]{1,0:T(8,128)(2,1)S(1)}, bf16[64,512]{1,0:T(8,128)(2,1)S(1)}, u32[]{:S(2)}, u32[]{:S(2)}) collective-permute-start(bf16[64,512]{1,0:T(8,128)(2,1)S(1)} %get-tuple-element.46), channel_id=1, source_target_pairs={{0,1},{1,0},{2,3},{3,2},{4,5},{5,4},{6,7},{7,6},{8,9},{9,8},{10,11... | collective-permute-start | bytes 196616 | tf_op jit(solution)/shard_map/ppermute | solution.py:29

commit v6 on v5

--- a/solution.py
+++ b/solution.py
@@ -59,6 +59,12 @@
 
 
 ORDER = (3, 1, 2, 0)
+
+
+def divided(value, by):
+    if by & (by - 1):
+        return value // by
+    return lax.shift_right_logical(value, jnp.full_like(value, by.bit_length() - 1))
 
 
 def labelled_sums(start, labels, chunks, label_ref, rows_ref, totals, copies=None):
@@ -110,13 +116,13 @@
     ids_copy.wait()
     offset = ids_ref[...] - position * cent
     offset = jnp.where(offset < 0, offset + devices * cent, offset)
-    ahead = offset // cent + mate
-    partner = (ahead % GROUP) ^ mate
+    ahead = divided(offset, cent) + mate
+    partner = (ahead & (GROUP - 1)) ^ mate
     place = jnp.zeros_like(partner)
     for index, who in enumerate(ORDER):
         place = jnp.where(partner == who, index, place)
-    slot = jnp.where(ahead // GROUP == 1, 1, 0)
-    label_ref[...] = place * pair + slot * cent + offset % cent
+    slot = jnp.where(divided(ahead, GROUP) == 1, cent, 0)
+    label_ref[...] = place * pair + slot + offset - divided(offset, cent) * cent
     counts = labelled_sums(0, 2 * pair, chunks, label_ref, rows_ref, totals, copies)
     group_copy.wait()
     digits = jnp.concatenate(split_digits(group_ref[...].astype(F32)), axis=0)
@@ -342,93 +348,132 @@
     return jnp.where(low, first, other)
 
 
-def gathered(ids, base, blocks):
-    one_hots = [one_hot_of(K2, ids_row(ids, base, order)) for order in range(GROUP)]
-    rows = [block[...] for block in blocks]
-    if len(rows) == GROUP:
-        rows[2:] = [jnp.concatenate(rows[2:], axis=0)]
-    rows[:2] = [jnp.concatenate(rows[:2], axis=0)]
+def picked_ids(ids, pick):
+    return ids_row(ids, pick // GROUP * GROUP, pick % GROUP)
+
+
+def gathered(ids, picks, blocks, start, count):
+    one_hots = [one_hot_of(count, picked_ids(ids, pick) - start) for pick in picks]
     total = None
-    for index, row in enumerate(rows):
-        one_hot = jnp.concatenate(one_hots[2 * index : 2 * index + 2], axis=1)
-        part = jnp.dot(one_hot, row, preferred_element_type=F32)
+    for at in range(0, len(picks), 2):
+        one_hot = jnp.concatenate(one_hots[at : at + 2], axis=1)
+        rows = jnp.concatenate([block[...] for block in blocks[at : at + 2]], axis=0)
+        part = jnp.dot(one_hot, rows, preferred_element_type=F32)
         total = part if total is None else total + part
-    return total, sum(one_hots[1:], one_hots[0])
-
-
-def gather_kernel(ids, *refs):
-    blocks, (sums_ref, tally_ref) = refs[:-2], refs[-2:]
-    sums_ref[...], tally_ref[...] = gathered(ids, 0, blocks)
-
-
-def gathered_sums(ids, blocks):
-    width = blocks[0].shape[1]
-    return pl.pallas_call(
-        gather_kernel,
-        in_specs=[whole()] * (1 + len(blocks)),
-        out_specs=[whole()] * 2,
+    return total
+
+
+def gather_kernel(picks, *refs):
+    blocks, (ids, mean, far, sums_ref, tally_ref, first_ref) = refs[:-6], refs[-6:]
+    first_ref[...] = jnp.where(even_line(), far[: mean.shape[0]], mean[...])
+    sums_ref[...] = gathered(ids, picks, blocks, 0, K2)
+    tally = one_hot_of(K2, picked_ids(ids, picks[0]))
+    for pick in picks[1:]:
+        tally = tally + one_hot_of(K2, picked_ids(ids, pick))
+    tally_ref[...] = tally
+
+
+def gathered_sums(ids, mean, far, picks, blocks):
+    cent, width = mean.shape
+    return pl.pallas_call(
+        functools.partial(gather_kernel, picks),
+        in_specs=[whole()] * (3 + len(picks)),
+        out_specs=[whole()] * 3,
         out_shape=[
             jax.ShapeDtypeStruct((K2, width), F32),
             jax.ShapeDtypeStruct((K2, LANES), BF16),
-        ],
-        compiler_params=small(),
-    )(ids, *blocks)
-
-
-def score_kernel(owned, ids, mean, sums, tally, *refs):
-    blocks, refs = refs[:-8], refs[-8:]
-    mean_hbm, second_hbm, keep_ref, send_ref, values_ref, mean_ref, second_ref, sent = refs
-    cent = mean.shape[0]
-    first = jnp.where(even_line(), blocks[0][:cent], mean[...])
-    mean_ref[...] = first
-    mean_copy = pltpu.make_async_copy(mean_ref, mean_hbm, sent.at[0])
-    mean_copy.start()
-    total, tally_here = gathered(ids, GROUP, blocks)
-    count = jnp.sum((tally[...] + tally_here).astype(F32), axis=1, keepdims=True)
-    second = ((sums[...] + total) * (1.0 / count)).astype(BF16)
+            jax.ShapeDtypeStruct((cent, width), BF16),
+        ],
+        compiler_params=small(),
+    )(*[blocks[pick] for pick in picks], ids, mean, far)
+
+
+def half_centroids(ids, picks, blocks, sums, tally, start):
+    half = K2 // 2
+    rows = pl.ds(pl.multiple_of(start, half), half)
+    total = sums[rows] + gathered(ids, picks, blocks, start, half)
+    count = tally[rows]
+    for pick in picks:
+        count = count + one_hot_of(half, picked_ids(ids, pick) - start)
+    count = jnp.sum(count.astype(F32), axis=1, keepdims=True)
+    return (total * (1.0 / count)).astype(BF16)
+
+
+def scores_of(first, second):
     values = second.astype(F32)
-    values_ref[...] = values
-    start = pl.multiple_of(lax.axis_index("dp") * owned, owned)
-    second_ref[...] = values_ref[pl.ds(start, owned)].astype(BF16)
-    second_copy = pltpu.make_async_copy(second_ref, second_hbm, sent.at[1])
-    second_copy.start()
     norms = 0.5 * jnp.sum(values * values, axis=1, keepdims=True)
     row = jnp.concatenate(
-        [as_row(norms[at : at + LANES]) for at in range(0, K2, LANES)], axis=1
+        [as_row(norms[at : at + LANES]) for at in range(0, second.shape[0], LANES)], axis=1
     )
     products = lax.dot_general(
         first, second, (((1,), (1,)), ((), ())), preferred_element_type=F32
     )
-    scores = products - row
+    return products - row
+
+
+def send_kernel(picks, *refs):
+    blocks, refs = refs[:-8], refs[-8:]
+    ids, first, sums, tally, first_hbm, other_ref, send_ref, sent = refs
+    first_copy = pltpu.make_async_copy(first, first_hbm, sent.at[0])
+    first_copy.start()
+    start = (1 - lax.axis_index("mp")) * (K2 // 2)
+    second = half_centroids(ids, picks, blocks, sums, tally, start)
+    other_ref[...] = second
+    send_ref[...] = scores_of(first[...], second).astype(BF16)
+    first_copy.wait()
+
+
+def sent_scores(ids, first, sums, tally, picks, blocks):
+    cent, width = first.shape
     half = K2 // 2
-    low = lax.axis_index("mp") == 0
-    keep_ref[...] = jnp.where(low, scores[:, :half], scores[:, half:])
-    send_ref[...] = jnp.where(low, scores[:, half:], scores[:, :half]).astype(BF16)
-    mean_copy.wait()
+    return pl.pallas_call(
+        functools.partial(send_kernel, picks),
+        in_specs=[whole()] * (4 + len(picks)),
+        out_specs=[pl.BlockSpec(memory_space=pltpu.HBM), whole(), whole()],
+        out_shape=[
+            jax.ShapeDtypeStruct((cent, width), BF16),
+            jax.ShapeDtypeStruct((half, width), BF16),
+            jax.ShapeDtypeStruct((cent, half), BF16),
+        ],
+        scratch_shapes=[pltpu.SemaphoreType.DMA((1,))],
+        compiler_params=small(),
+    )(*[blocks[pick] for pick in picks], ids, first, sums, tally)
+
+
+def keep_kernel(owned, picks, *refs):
+    blocks, refs = refs[:-10], refs[-10:]
+    ids, first, sums, tally, other, second_hbm, keep_ref, every, second_ref, sent = refs
+    half = K2 // 2
+    core = lax.axis_index("mp")
+    second = half_centroids(ids, picks, blocks, sums, tally, core * half)
+    every[...] = second
+    at = lax.axis_index("dp") * owned
+    rows = pl.ds(pl.multiple_of(at % half, owned), owned)
+    second_ref[...] = jnp.where(at // half == core, every[rows], other[rows])
+    second_copy = pltpu.make_async_copy(second_ref, second_hbm, sent.at[0])
+    second_copy.start()
+    keep_ref[...] = scores_of(first[...], second)
     second_copy.wait()
 
 
-def second_level_scores(owned, ids, mean, sums, tally, blocks):
-    cent, width = mean.shape
-    hbm = pl.BlockSpec(memory_space=pltpu.HBM)
-    return pl.pallas_call(
-        functools.partial(score_kernel, owned),
-        in_specs=[whole()] * (4 + len(blocks)),
-        out_specs=[hbm, hbm, whole(), whole()],
-        out_shape=[
-            jax.ShapeDtypeStruct((cent, width), BF16),
+def kept_scores(owned, ids, first, sums, tally, other, picks, blocks):
+    cent, width = first.shape
+    half = K2 // 2
+    return pl.pallas_call(
+        functools.partial(keep_kernel, owned, picks),
+        in_specs=[whole()] * (5 + len(picks)),
+        out_specs=[pl.BlockSpec(memory_space=pltpu.HBM), whole()],
+        out_shape=[
             jax.ShapeDtypeStruct((owned, width), BF16),
-            jax.ShapeDtypeStruct((cent, K2 // 2), F32),
-            jax.ShapeDtypeStruct((cent, K2 // 2), BF16),
+            jax.ShapeDtypeStruct((cent, half), F32),
         ],
         scratch_shapes=[
-            pltpu.VMEM((K2, width), F32),
-            pltpu.VMEM((cent, width), BF16),
+            pltpu.VMEM((half, width), BF16),
             pltpu.VMEM((owned, width), BF16),
-            pltpu.SemaphoreType.DMA((2,)),
-        ],
-        compiler_params=small(),
-    )(ids, mean, sums, tally, *blocks)
+            pltpu.SemaphoreType.DMA((1,)),
+        ],
+        compiler_params=small(),
+    )(*[blocks[pick] for pick in picks], ids, first, sums, tally, other)
 
 
 def summed_scores(devices, second_level, first_centroids):
@@ -492,12 +537,12 @@
 
     near, ids = near_rows(cent, send, partner(send, GROUP))
     far = joined(partner(mean, 2 * GROUP), partner(mean, 3 * GROUP))
-    sums, tally = gathered_sums(ids, plane_rows(near))
-    mean, second, keep, send = second_level_scores(
-        K2 // devices, ids, mean, sums, tally, plane_rows(far)
-    )
+    blocks = plane_rows(near) + plane_rows(far)
+    sums, tally, first = gathered_sums(ids, mean, far, (0, 1, 2, 3, 4), blocks)
+    first_out, other, send = sent_scores(ids, first, sums, tally, (5, 6, 7), blocks)
     got = exchanged(send, [(d * cores + c, d * cores + (c ^ 1)) for d, c in everyone])
-    return mean, second, keep + got.astype(F32)
+    second, keep = kept_scores(K2 // devices, ids, first, sums, tally, other, (5, 6, 7), blocks)
+    return first_out, second, keep + got.astype(F32)
 
 
 def solution(mesh):

time: 43 us -> 42.2 us (0.981)
  waiting for transfers between devices: 13.6 us -> 12.2 us
  Pallas kernels: 6.07 us -> 6.62 us
    ppermute x15, waiting for transfers between devices: 13.6 us -> 12.2 us  [exchanged(): return lax.ppermute(value, ('dp', 'mp'), pairs)]
    pallas_call x2 -> x3, Pallas kernels: 2.21 us -> 2.76 us  [the longest x1 1.11 us: kept_scores(): pl.pallas_call(functools.partial(keep_kernel, owned, picks), in_specs=[wh...]
  transfers between devices with their start and end apart: 15 -> 15, of which waited for: 11 -> 11; matrix products, arithmetic and copies ran while one was open for 0% -> 0% of each run, Pallas kernels for 4% -> 8%
where the time goes in v6:
time: 42.2 us; the launch traced here: 41.9 us
  starting transfers between devices  21.8 us (52%)
  waiting for transfers between devices  12.2 us (29%)
  Pallas kernels  6.62 us (16%)
  between operations  0.7 us (2%)
  other arithmetic  0.67 us (2%)
    ppermute x15, starting transfers between devices, exchanged(): return lax.ppermute(value, ('dp', 'mp'), pairs)  21.8 us
    ppermute x15, waiting for transfers between devices, exchanged(): return lax.ppermute(value, ('dp', 'mp'), pairs)  12.2 us
    pallas_call x1, Pallas kernels, band_sums(): pl.pallas_call(functools.partial(first_kernel, devices, cent, chunks), in...  2.43 us
    pallas_call x1, Pallas kernels, kept_scores(): pl.pallas_call(functools.partial(keep_kernel, owned, picks), in_specs=[wh...  1.11 us
    pallas_call x1, Pallas kernels, band_sums(): pl.pallas_call(functools.partial(second_kernel, cent, [(0, half), (half,...  1.01 us
    pallas_call x1, Pallas kernels, gathered_sums(): pl.pallas_call(functools.partial(gather_kernel, picks), in_specs=[whole()...  0.99 us
  transfers between devices with their start and end apart: 15, of which 11 were waited for; matrix products, arithmetic and copies ran while one was open for 0% of the time, Pallas kernels for 8%

profile of v6, /device:TPU:0, one launch (start us, length us, event | category | flops | bytes accessed | tf_op | source)
XLA Modules:
  0.0 41.9 jit_solution(2437812698043032920)
XLA Ops:
  0.6 2.4 %shard_map.58 = (bf16[136,512]{1,0:T(8,128)(2,1)S(1)}, bf16[136,512]{1,0:T(8,128)(2,1)S(1)}, bf16[3072,512]{1,0:T(8,128)(2,1)S(1)}, s32[1,3072]{1,0:T(1,128)S(1)}, f32[2,64]{1,0:T(2,128)S(1)}) custom-call(s32[1,3072]{1,0:T(1,128)} %bitcast.2, bf16[3072,512]{1,0:T(8,128)(2,1)} %rows_hbm.1, s32[1,64]{1,0:T(1,128)} %bitcast.3), custom_call_target="tpu_custom_call" | custom-call | tf_op jit(solution)/shard_map/pallas_call | solution.py:156
  3.1 4.0 %collective-permute-start = (bf16[136,512]{1,0:T(8,128)(2,1)S(1)}, bf16[136,512]{1,0:T(8,128)(2,1)S(1)}, u32[]{:S(2)}, u32[]{:S(2)}) collective-permute-start(bf16[136,512]{1,0:T(8,128)(2,1)S(1)} %get-tuple-element.27), channel_id=1, source_target_pairs={{0,6},{1,7},{2,4},{3,5},{4,2},{5,3},{6,0},{7,1},{8,14},{9,15},{10,... | collective-permute-start | bytes 417800 | tf_op jit(solution)/shard_map/ppermute | solution.py:29
  7.6 1.0 %shard_map.59 = (bf16[136,512]{1,0:T(8,128)(2,1)S(1)}, f32[128,512]{1,0:T(8,128)S(1)}, f32[8,256]{1,0:T(8,128)S(1)}) custom-call(s32[1,3072]{1,0:T(1,128)S(1)} %get-tuple-element.29.label_ref, bf16[3072,512]{1,0:T(8,128)(2,1)S(1)} %get-tuple-element.30.rows_ref, f32[2,64]{1,0:T(2,128)S(1)} %get-tuple-element.31.digits_ref), custom_call_target="tpu_custom_call" | custom-call | flops 99999997952 | bytes 300000000 | tf_op jit(solution)/shard_map/pallas_call | solution.py:179
  8.7 2.8 %collective-permute-done.three = bf16[136,512]{1,0:T(8,128)(2,1)S(1)} collective-permute-done((bf16[136,512]{1,0:T(8,128)(2,1)S(1)}, bf16[136,512]{1,0:T(8,128)(2,1)S(1)}, u32[]{:S(2)}, u32[]{:S(2)}) %collective-permute-start) | collective-permute-done | bytes 139296 | tf_op jit(solution)/shard_map/ppermute | solution.py:29
  11.5 2.4 %collective-permute-done.1.one = bf16[136,512]{1,0:T(8,128)(2,1)S(1)} collective-permute-done((bf16[136,512]{1,0:T(8,128)(2,1)S(1)}, bf16[136,512]{1,0:T(8,128)(2,1)S(1)}, u32[]{:S(2)}, u32[]{:S(2)}) %collective-permute-start.1) | collective-permute-done | bytes 139296 | tf_op jit(solution)/shard_map/ppermute | solution.py:29
  14.2 2.9 %collective-permute-start.3 = (bf16[72,512]{1,0:T(8,128)(2,1)S(1)}, bf16[72,512]{1,0:T(8,128)(2,1)S(1)}, u32[]{:S(2)}, u32[]{:S(2)}) collective-permute-start(bf16[72,512]{1,0:T(8,128)(2,1)S(1)} %get-tuple-element.35), channel_id=1, source_target_pairs={{0,16},{1,17},{2,18},{3,19},{4,20},{5,21},{6,22},{7,23},{8,24},{9,... | collective-permute-start | bytes 221192 | tf_op jit(solution)/shard_map/ppermute | solution.py:29
  17.1 1.6 %collective-permute-start.4 = (bf16[72,512]{1,0:T(8,128)(2,1)S(1)}, bf16[72,512]{1,0:T(8,128)(2,1)S(1)}, u32[]{:S(2)}, u32[]{:S(2)}) collective-permute-start(bf16[72,512]{1,0:T(8,128)(2,1)S(1)} %get-tuple-element.36), channel_id=1, source_target_pairs={{0,8},{1,9},{2,10},{3,11},{4,12},{5,13},{6,14},{7,15},{8,0},{9,1},... | collective-permute-start | bytes 221192 | tf_op jit(solution)/shard_map/ppermute | solution.py:29
  18.6 1.1 %collective-permute-done.3.two = bf16[72,512]{1,0:T(8,128)(2,1)S(1)} collective-permute-done((bf16[72,512]{1,0:T(8,128)(2,1)S(1)}, bf16[72,512]{1,0:T(8,128)(2,1)S(1)}, u32[]{:S(2)}, u32[]{:S(2)}) %collective-permute-start.3) | collective-permute-done | bytes 73760 | tf_op jit(solution)/shard_map/ppermute | solution.py:29
  19.8 1.6 %collective-permute-done.4.one = bf16[72,512]{1,0:T(8,128)(2,1)S(1)} collective-permute-done((bf16[72,512]{1,0:T(8,128)(2,1)S(1)}, bf16[72,512]{1,0:T(8,128)(2,1)S(1)}, u32[]{:S(2)}, u32[]{:S(2)}) %collective-permute-start.4) | collective-permute-done | bytes 73760 | tf_op jit(solution)/shard_map/ppermute | solution.py:29
  21.6 1.6 %collective-permute-start.10 = (bf16[72,512]{1,0:T(8,128)(2,1)S(1)}, bf16[72,512]{1,0:T(8,128)(2,1)S(1)}, u32[]{:S(2)}, u32[]{:S(2)}) collective-permute-start(bf16[72,512]{1,0:T(8,128)(2,1)S(1)} %get-tuple-element.40.own), channel_id=1, source_target_pairs={{0,8},{1,9},{2,10},{3,11},{4,12},{5,13},{6,14},{7,15},{8,0},{9,1},... | collective-permute-start | bytes 221192 | tf_op jit(solution)/shard_map/ppermute | solution.py:29
  23.2 1.6 %collective-permute-start.6 = (bf16[64,512]{1,0:T(8,128)(2,1)S(1)}, bf16[64,512]{1,0:T(8,128)(2,1)S(1)}, u32[]{:S(2)}, u32[]{:S(2)}) collective-permute-start(bf16[64,512]{1,0:T(8,128)(2,1)S(1)} %get-tuple-element.39.refs_6_), channel_id=1, source_target_pairs={{0,16},{1,17},{2,18},{3,19},{4,20},{5,21},{6,22},{7,23},{8,24},{9,... | collective-permute-start | bytes 196616 | tf_op jit(solution)/shard_map/ppermute | solution.py:29
  24.8 1.2 %collective-permute-start.5 = (bf16[64,512]{1,0:T(8,128)(2,1)S(1)}, bf16[64,512]{1,0:T(8,128)(2,1)S(1)}, u32[]{:S(2)}, u32[]{:S(2)}) collective-permute-start(bf16[64,512]{1,0:T(8,128)(2,1)S(1)} %get-tuple-element.39.refs_6_), channel_id=1, source_target_pairs={{0,24},{1,25},{2,26},{3,27},{4,28},{5,29},{6,30},{7,31},{8,16},{9,... | collective-permute-start | bytes 196616 | tf_op jit(solution)/shard_map/ppermute | solution.py:29
  26.6 2.1 %collective-permute-start.13 = (bf16[128,512]{1,0:T(8,128)(2,1)S(1)}, bf16[128,512]{1,0:T(8,128)(2,1)S(1)}, u32[]{:S(2)}, u32[]{:S(2)}) collective-permute-start(bf16[128,512]{1,0:T(8,128)(2,1)S(1)} %get-tuple-element.42.refs_0_), channel_id=1, source_target_pairs={{0,6},{1,7},{2,4},{3,5},{4,2},{5,3},{6,0},{7,1},{8,14},{9,15},{10,... | collective-permute-start | bytes 393224 | tf_op jit(solution)/shard_map/ppermute | solution.py:29
  28.7 1.0 %collective-permute-start.12 = (bf16[128,512]{1,0:T(8,128)(2,1)S(1)}, bf16[128,512]{1,0:T(8,128)(2,1)S(1)}, u32[]{:S(2)}, u32[]{:S(2)}) collective-permute-start(bf16[128,512]{1,0:T(8,128)(2,1)S(1)} %get-tuple-element.42.refs_0_), channel_id=1, source_target_pairs={{0,4},{1,3},{2,6},{3,1},{4,0},{5,7},{6,2},{7,5},{8,12},{9,11},{10,... | collective-permute-start | bytes 393224 | tf_op jit(solution)/shard_map/ppermute | solution.py:29
  30.2 0.7 %collective-permute-done.5.second = bf16[64,512]{1,0:T(8,128)(2,1)S(1)} collective-permute-done((bf16[64,512]{1,0:T(8,128)(2,1)S(1)}, bf16[64,512]{1,0:T(8,128)(2,1)S(1)}, u32[]{:S(2)}, u32[]{:S(2)}) %collective-permute-start.5) | collective-permute-done | bytes 65568 | tf_op jit(solution)/shard_map/ppermute | solution.py:29
  30.9 2.2 %collective-permute-start.9 = (bf16[128,512]{1,0:T(8,128)(2,1)S(1)}, bf16[128,512]{1,0:T(8,128)(2,1)S(1)}, u32[]{:S(2)}, u32[]{:S(2)}) collective-permute-start(bf16[128,512]{1,0:T(8,128)(2,1)S(1)} %shard_map.62.refs_4_.refs_7_), channel_id=1, source_target_pairs={{0,6},{1,7},{2,4},{3,5},{4,2},{5,3},{6,0},{7,1},{8,14},{9,15},{10,... | collective-permute-start | bytes 393224 | tf_op jit(solution)/shard_map/ppermute | solution.py:29
  33.1 0.9 %collective-permute-start.8 = (bf16[128,512]{1,0:T(8,128)(2,1)S(1)}, bf16[128,512]{1,0:T(8,128)(2,1)S(1)}, u32[]{:S(2)}, u32[]{:S(2)}) collective-permute-start(bf16[128,512]{1,0:T(8,128)(2,1)S(1)} %shard_map.62.refs_4_.refs_7_), channel_id=1, source_target_pairs={{0,4},{1,3},{2,6},{3,1},{4,0},{5,7},{6,2},{7,5},{8,12},{9,11},{10,... | collective-permute-start | bytes 393224 | tf_op jit(solution)/shard_map/ppermute | solution.py:29
  34.0 1.5 %collective-permute-start.7 = (bf16[128,512]{1,0:T(8,128)(2,1)S(1)}, bf16[128,512]{1,0:T(8,128)(2,1)S(1)}, u32[]{:S(2)}, u32[]{:S(2)}) collective-permute-start(bf16[128,512]{1,0:T(8,128)(2,1)S(1)} %shard_map.62.refs_4_.refs_7_), channel_id=1, source_target_pairs={{0,2},{1,5},{2,0},{3,7},{4,6},{5,1},{6,4},{7,3},{8,10},{9,13},{10,... | collective-permute-start | bytes 393224 | tf_op jit(solution)/shard_map/ppermute | solution.py:29
  35.5 0.9 %collective-permute-done.12.refs_2_ = bf16[128,512]{1,0:T(8,128)(2,1)S(1)} collective-permute-done((bf16[128,512]{1,0:T(8,128)(2,1)S(1)}, bf16[128,512]{1,0:T(8,128)(2,1)S(1)}, u32[]{:S(2)}, u32[]{:S(2)}) %collective-permute-start.12) | collective-permute-done | bytes 131104 | tf_op jit(solution)/shard_map/ppermute | solution.py:29
  36.5 1.0 %shard_map.64 = (f32[1024,512]{1,0:T(8,128)S(1)}, bf16[1024,128]{1,0:T(8,128)(2,1)S(1)}, bf16[64,512]{1,0:T(8,128)(2,1)S(1)}) custom-call(bf16[128,512]{1,0:T(8,128)(2,1)S(1)} %get-tuple-element.42.refs_0_, bf16[128,512]{1,0:T(8,128)(2,1)S(1)} %collective-permute-done.11.refs_1_, bf16[128,512]{1,0:T(8,128)(2,1)S(1)} %collective-permute-done.12.refs_2_, ...), custom_call_target="tpu_custom_call" | custom-call | tf_op jit(solution)/shard_map/pallas_call | solution.py:378
  38.0 1.3 %collective-permute-done.8.refs_1_ = bf16[128,512]{1,0:T(8,128)(2,1)S(1)} collective-permute-done((bf16[128,512]{1,0:T(8,128)(2,1)S(1)}, bf16[128,512]{1,0:T(8,128)(2,1)S(1)}, u32[]{:S(2)}, u32[]{:S(2)}) %collective-permute-start.8) | collective-permute-done | bytes 131104 | tf_op jit(solution)/shard_map/ppermute | solution.py:29
  39.3 0.7 %shard_map.65 = (bf16[64,512]{1,0:T(8,128)(2,1)}, bf16[512,512]{1,0:T(8,128)(2,1)S(1)}, bf16[64,512]{1,0:T(8,128)(2,1)S(1)}) custom-call(bf16[128,512]{1,0:T(8,128)(2,1)S(1)} %collective-permute-done.7.refs_0_, bf16[128,512]{1,0:T(8,128)(2,1)S(1)} %collective-permute-done.8.refs_1_, bf16[128,512]{1,0:T(8,128)(2,1)S(1)} %collective-permute-done.9.refs_2_, ...), custom_call_target="tpu_custom_call" | custom-call | tf_op jit(solution)/shard_map/pallas_call | solution.py:429
  40.0 1.1 %shard_map.66 = (bf16[64,512]{1,0:T(8,128)(2,1)}, f32[64,512]{1,0:T(8,128)S(1)}) custom-call(bf16[128,512]{1,0:T(8,128)(2,1)S(1)} %collective-permute-done.7.refs_0_, bf16[128,512]{1,0:T(8,128)(2,1)S(1)} %collective-permute-done.8.refs_1_, bf16[128,512]{1,0:T(8,128)(2,1)S(1)} %collective-permute-done.9.refs_2_, ...), custom_call_target="tpu_custom_call" | custom-call | tf_op jit(solution)/shard_map/pallas_call | solution.py:462
  41.3 0.7 %convert_add_fusion = f32[64,512]{1,0:T(8,128)} fusion(f32[64,512]{1,0:T(8,128)S(1)} %get-tuple-element.49, bf16[64,512]{1,0:T(8,128)(2,1)S(1)} %collective-permute-done.14), kind=kLoop, calls=%fused_computation | loop fusion | flops 65536 | bytes 327680 | tf_op jit(solution)/shard_map/add | solution.py:545
  (16 shorter events, 3.0 us)
Async XLA Ops:
  3.1 8.5 %collective-permute-start = (bf16[136,512]{1,0:T(8,128)(2,1)S(1)}, bf16[136,512]{1,0:T(8,128)(2,1)S(1)}, u32[]{:S(2)}, u32[]{:S(2)}) collective-permute-start(bf16[136,512]{1,0:T(8,128)(2,1)S(1)} %get-tuple-element.27), channel_id=1, source_target_pairs={{0,6},{1,7},{2,4},{3,5},{4,2},{5,3},{6,0},{7,1},{8,14},{9,15},{10,... | collective-permute-start | bytes 417800 | tf_op jit(solution)/shard_map/ppermute | solution.py:29
  7.0 6.9 %collective-permute-start.1 = (bf16[136,512]{1,0:T(8,128)(2,1)S(1)}, bf16[136,512]{1,0:T(8,128)(2,1)S(1)}, u32[]{:S(2)}, u32[]{:S(2)}) collective-permute-start(bf16[136,512]{1,0:T(8,128)(2,1)S(1)} %get-tuple-element.28), channel_id=1, source_target_pairs={{0,2},{1,3},{2,0},{3,1},{4,6},{5,7},{6,4},{7,5},{8,10},{9,11},{10,... | collective-permute-start | bytes 417800 | tf_op jit(solution)/shard_map/ppermute | solution.py:29
  8.6 5.4 %collective-permute-start.2 = (bf16[136,512]{1,0:T(8,128)(2,1)S(1)}, bf16[136,512]{1,0:T(8,128)(2,1)S(1)}, u32[]{:S(2)}, u32[]{:S(2)}) collective-permute-start(bf16[136,512]{1,0:T(8,128)(2,1)S(1)} %get-tuple-element.32), channel_id=1, source_target_pairs={{0,4},{1,5},{2,6},{3,7},{4,0},{5,1},{6,2},{7,3},{8,12},{9,13},{10,... | collective-permute-start | bytes 417800 | tf_op jit(solution)/shard_map/ppermute | solution.py:29
  14.2 5.6 %collective-permute-start.3 = (bf16[72,512]{1,0:T(8,128)(2,1)S(1)}, bf16[72,512]{1,0:T(8,128)(2,1)S(1)}, u32[]{:S(2)}, u32[]{:S(2)}) collective-permute-start(bf16[72,512]{1,0:T(8,128)(2,1)S(1)} %get-tuple-element.35), channel_id=1, source_target_pairs={{0,16},{1,17},{2,18},{3,19},{4,20},{5,21},{6,22},{7,23},{8,24},{9,... | collective-permute-start | bytes 221192 | tf_op jit(solution)/shard_map/ppermute | solution.py:29
  17.1 4.4 %collective-permute-start.4 = (bf16[72,512]{1,0:T(8,128)(2,1)S(1)}, bf16[72,512]{1,0:T(8,128)(2,1)S(1)}, u32[]{:S(2)}, u32[]{:S(2)}) collective-permute-start(bf16[72,512]{1,0:T(8,128)(2,1)S(1)} %get-tuple-element.36), channel_id=1, source_target_pairs={{0,8},{1,9},{2,10},{3,11},{4,12},{5,13},{6,14},{7,15},{8,0},{9,1},... | collective-permute-start | bytes 221192 | tf_op jit(solution)/shard_map/ppermute | solution.py:29
  21.6 4.9 %collective-permute-start.10 = (bf16[72,512]{1,0:T(8,128)(2,1)S(1)}, bf16[72,512]{1,0:T(8,128)(2,1)S(1)}, u32[]{:S(2)}, u32[]{:S(2)}) collective-permute-start(bf16[72,512]{1,0:T(8,128)(2,1)S(1)} %get-tuple-element.40.own), channel_id=1, source_target_pairs={{0,8},{1,9},{2,10},{3,11},{4,12},{5,13},{6,14},{7,15},{8,0},{9,1},... | collective-permute-start | bytes 221192 | tf_op jit(solution)/shard_map/ppermute | solution.py:29
  23.2 7.0 %collective-permute-start.6 = (bf16[64,512]{1,0:T(8,128)(2,1)S(1)}, bf16[64,512]{1,0:T(8,128)(2,1)S(1)}, u32[]{:S(2)}, u32[]{:S(2)}) collective-permute-start(bf16[64,512]{1,0:T(8,128)(2,1)S(1)} %get-tuple-element.39.refs_6_), channel_id=1, source_target_pairs={{0,16},{1,17},{2,18},{3,19},{4,20},{5,21},{6,22},{7,23},{8,24},{9,... | collective-permute-start | bytes 196616 | tf_op jit(solution)/shard_map/ppermute | solution.py:29
  24.8 6.1 %collective-permute-start.5 = (bf16[64,512]{1,0:T(8,128)(2,1)S(1)}, bf16[64,512]{1,0:T(8,128)(2,1)S(1)}, u32[]{:S(2)}, u32[]{:S(2)}) collective-permute-start(bf16[64,512]{1,0:T(8,128)(2,1)S(1)} %get-tuple-element.39.refs_6_), channel_id=1, source_target_pairs={{0,24},{1,25},{2,26},{3,27},{4,28},{5,29},{6,30},{7,31},{8,16},{9,... | collective-permute-start | bytes 196616 | tf_op jit(solution)/shard_map/ppermute | solution.py:29
  26.6 7.3 %collective-permute-start.13 = (bf16[128,512]{1,0:T(8,128)(2,1)S(1)}, bf16[128,512]{1,0:T(8,128)(2,1)S(1)}, u32[]{:S(2)}, u32[]{:S(2)}) collective-permute-start(bf16[128,512]{1,0:T(8,128)(2,1)S(1)} %get-tuple-element.42.refs_0_), channel_id=1, source_target_pairs={{0,6},{1,7},{2,4},{3,5},{4,2},{5,3},{6,0},{7,1},{8,14},{9,15},{10,... | collective-permute-start | bytes 393224 | tf_op jit(solution)/shard_map/ppermute | solution.py:29
  28.7 7.8 %collective-permute-start.12 = (bf16[128,512]{1,0:T(8,128)(2,1)S(1)}, bf16[128,512]{1,0:T(8,128)(2,1)S(1)}, u32[]{:S(2)}, u32[]{:S(2)}) collective-permute-start(bf16[128,512]{1,0:T(8,128)(2,1)S(1)} %get-tuple-element.42.refs_0_), channel_id=1, source_target_pairs={{0,4},{1,3},{2,6},{3,1},{4,0},{5,7},{6,2},{7,5},{8,12},{9,11},{10,... | collective-permute-start | bytes 393224 | tf_op jit(solution)/shard_map/ppermute | solution.py:29
  29.7 6.8 %collective-permute-start.11 = (bf16[128,512]{1,0:T(8,128)(2,1)S(1)}, bf16[128,512]{1,0:T(8,128)(2,1)S(1)}, u32[]{:S(2)}, u32[]{:S(2)}) collective-permute-start(bf16[128,512]{1,0:T(8,128)(2,1)S(1)} %get-tuple-element.42.refs_0_), channel_id=1, source_target_pairs={{0,2},{1,5},{2,0},{3,7},{4,6},{5,1},{6,4},{7,3},{8,10},{9,13},{10,... | collective-permute-start | bytes 393224 | tf_op jit(solution)/shard_map/ppermute | solution.py:29
  30.9 7.0 %collective-permute-start.9 = (bf16[128,512]{1,0:T(8,128)(2,1)S(1)}, bf16[128,512]{1,0:T(8,128)(2,1)S(1)}, u32[]{:S(2)}, u32[]{:S(2)}) collective-permute-start(bf16[128,512]{1,0:T(8,128)(2,1)S(1)} %shard_map.62.refs_4_.refs_7_), channel_id=1, source_target_pairs={{0,6},{1,7},{2,4},{3,5},{4,2},{5,3},{6,0},{7,1},{8,14},{9,15},{10,... | collective-permute-start | bytes 393224 | tf_op jit(solution)/shard_map/ppermute | solution.py:29
  33.1 6.2 %collective-permute-start.8 = (bf16[128,512]{1,0:T(8,128)(2,1)S(1)}, bf16[128,512]{1,0:T(8,128)(2,1)S(1)}, u32[]{:S(2)}, u32[]{:S(2)}) collective-permute-start(bf16[128,512]{1,0:T(8,128)(2,1)S(1)} %shard_map.62.refs_4_.refs_7_), channel_id=1, source_target_pairs={{0,4},{1,3},{2,6},{3,1},{4,0},{5,7},{6,2},{7,5},{8,12},{9,11},{10,... | collective-permute-start | bytes 393224 | tf_op jit(solution)/shard_map/ppermute | solution.py:29
  34.0 5.3 %collective-permute-start.7 = (bf16[128,512]{1,0:T(8,128)(2,1)S(1)}, bf16[128,512]{1,0:T(8,128)(2,1)S(1)}, u32[]{:S(2)}, u32[]{:S(2)}) collective-permute-start(bf16[128,512]{1,0:T(8,128)(2,1)S(1)} %shard_map.62.refs_4_.refs_7_), channel_id=1, source_target_pairs={{0,2},{1,5},{2,0},{3,7},{4,6},{5,1},{6,4},{7,3},{8,10},{9,13},{10,... | collective-permute-start | bytes 393224 | tf_op jit(solution)/shard_map/ppermute | solution.py:29
  40.0 1.3 %collective-permute-start.14 = (bf16[64,512]{1,0:T(8,128)(2,1)S(1)}, bf16[64,512]{1,0:T(8,128)(2,1)S(1)}, u32[]{:S(2)}, u32[]{:S(2)}) collective-permute-start(bf16[64,512]{1,0:T(8,128)(2,1)S(1)} %get-tuple-element.50), channel_id=1, source_target_pairs={{0,1},{1,0},{2,3},{3,2},{4,5},{5,4},{6,7},{7,6},{8,9},{9,8},{10,11... | collective-permute-start | bytes 196616 | tf_op jit(solution)/shard_map/ppermute | solution.py:29

commit v7 on v6

--- a/solution.py
+++ b/solution.py
@@ -118,6 +118,8 @@
     offset = jnp.where(offset < 0, offset + devices * cent, offset)
     ahead = divided(offset, cent) + mate
     partner = (ahead & (GROUP - 1)) ^ mate
+    swapped = (partner > 0) & (partner < 3) & (lax.axis_index("mp") % 2 == 1)
+    partner = jnp.where(swapped, 3 - partner, partner)
     place = jnp.zeros_like(partner)
     for index, who in enumerate(ORDER):
         place = jnp.where(partner == who, index, place)
@@ -205,8 +207,10 @@
     counts = own_meta[0:1, :LANES] * BASE + own_meta[1:2, :LANES]
     far_counts = jnp.zeros_like(counts)
     id_digits = [own_meta[0:2, LANES:]]
+    swapped = lax.axis_index("mp") % 2 == 1
     for index, got in ((1, one), (2, two), (3, three)):
-        before = (mate ^ index) < mate
+        source = index if index == 3 else jnp.where(swapped, 3 - index, index)
+        before = (mate ^ source) < mate
         first = got[:cent].astype(F32)
         near = near + jnp.where(before, first, 0.0)
         far = far + jnp.where(before, 0.0, first)
@@ -217,6 +221,10 @@
         counts = counts + jnp.where(mask, row, 0.0)
         far_counts = far_counts + jnp.where(mask, 0.0, row)
         id_digits.append(meta[0:2, LANES:])
+    id_digits[1], id_digits[2] = (
+        jnp.where(swapped, id_digits[2], id_digits[1]),
+        jnp.where(swapped, id_digits[1], id_digits[2]),
+    )
     id_digits = jnp.concatenate(id_digits, axis=0)
 
     def meta_of(row):
@@ -364,13 +372,18 @@
 
 
 def gather_kernel(picks, *refs):
-    blocks, (ids, mean, far, sums_ref, tally_ref, first_ref) = refs[:-6], refs[-6:]
+    blocks, refs = refs[:-8], refs[-8:]
+    ids, mean, far, sums_ref, scale_ref, first_ref, first_hbm, sent = refs
     first_ref[...] = jnp.where(even_line(), far[: mean.shape[0]], mean[...])
+    first_copy = pltpu.make_async_copy(first_ref, first_hbm, sent.at[0])
+    first_copy.start()
     sums_ref[...] = gathered(ids, picks, blocks, 0, K2)
-    tally = one_hot_of(K2, picked_ids(ids, picks[0]))
-    for pick in picks[1:]:
-        tally = tally + one_hot_of(K2, picked_ids(ids, pick))
-    tally_ref[...] = tally
+    tally = one_hot_of(K2, ids[0:1])
+    for row in range(1, 2 * GROUP):
+        tally = tally + one_hot_of(K2, ids[row : row + 1])
+    count = jnp.sum(tally.astype(F32), axis=1, keepdims=True)
+    scale_ref[...] = jnp.broadcast_to(1.0 / count, scale_ref.shape)
+    first_copy.wait()
 
 
 def gathered_sums(ids, mean, far, picks, blocks):
@@ -378,25 +391,25 @@
     return pl.pallas_call(
         functools.partial(gather_kernel, picks),
         in_specs=[whole()] * (3 + len(picks)),
-        out_specs=[whole()] * 3,
+        out_specs=[whole()] * 3 + [pl.BlockSpec(memory_space=pltpu.HBM)],
         out_shape=[
             jax.ShapeDtypeStruct((K2, width), F32),
-            jax.ShapeDtypeStruct((K2, LANES), BF16),
+            jax.ShapeDtypeStruct((K2, LANES), F32),
             jax.ShapeDtypeStruct((cent, width), BF16),
-        ],
+            jax.ShapeDtypeStruct((cent, width), BF16),
+        ],
+        scratch_shapes=[pltpu.SemaphoreType.DMA((1,))],
         compiler_params=small(),
     )(*[blocks[pick] for pick in picks], ids, mean, far)
 
 
-def half_centroids(ids, picks, blocks, sums, tally, start):
+def half_centroids(ids, picks, blocks, sums, scale, start):
     half = K2 // 2
     rows = pl.ds(pl.multiple_of(start, half), half)
     total = sums[rows] + gathered(ids, picks, blocks, start, half)
-    count = tally[rows]
-    for pick in picks:
-        count = count + one_hot_of(half, picked_ids(ids, pick) - start)
-    count = jnp.sum(count.astype(F32), axis=1, keepdims=True)
-    return (total * (1.0 / count)).astype(BF16)
+    factor = scale[rows]
+    parts = [total[:, at : at + LANES] * factor for at in range(0, total.shape[1], LANES)]
+    return jnp.concatenate(parts, axis=1).astype(BF16)
 
 
 def scores_of(first, second):
@@ -412,40 +425,35 @@
 
 
 def send_kernel(picks, *refs):
-    blocks, refs = refs[:-8], refs[-8:]
-    ids, first, sums, tally, first_hbm, other_ref, send_ref, sent = refs
-    first_copy = pltpu.make_async_copy(first, first_hbm, sent.at[0])
-    first_copy.start()
+    blocks, refs = refs[:-6], refs[-6:]
+    ids, first, sums, scale, other_ref, send_ref = refs
     start = (1 - lax.axis_index("mp")) * (K2 // 2)
-    second = half_centroids(ids, picks, blocks, sums, tally, start)
+    second = half_centroids(ids, picks, blocks, sums, scale, start)
     other_ref[...] = second
     send_ref[...] = scores_of(first[...], second).astype(BF16)
-    first_copy.wait()
-
-
-def sent_scores(ids, first, sums, tally, picks, blocks):
+
+
+def sent_scores(ids, first, sums, scale, picks, blocks):
     cent, width = first.shape
     half = K2 // 2
     return pl.pallas_call(
         functools.partial(send_kernel, picks),
         in_specs=[whole()] * (4 + len(picks)),
-        out_specs=[pl.BlockSpec(memory_space=pltpu.HBM), whole(), whole()],
-        out_shape=[
-            jax.ShapeDtypeStruct((cent, width), BF16),
+        out_specs=[whole()] * 2,
+        out_shape=[
             jax.ShapeDtypeStruct((half, width), BF16),
             jax.ShapeDtypeStruct((cent, half), BF16),
         ],
-        scratch_shapes=[pltpu.SemaphoreType.DMA((1,))],
-        compiler_params=small(),
-    )(*[blocks[pick] for pick in picks], ids, first, sums, tally)
+        compiler_params=small(),
+    )(*[blocks[pick] for pick in picks], ids, first, sums, scale)
 
 
 def keep_kernel(owned, picks, *refs):
     blocks, refs = refs[:-10], refs[-10:]
-    ids, first, sums, tally, other, second_hbm, keep_ref, every, second_ref, sent = refs
+    ids, first, sums, scale, other, second_hbm, keep_ref, every, second_ref, sent = refs
     half = K2 // 2
     core = lax.axis_index("mp")
-    second = half_centroids(ids, picks, blocks, sums, tally, core * half)
+    second = half_centroids(ids, picks, blocks, sums, scale, core * half)
     every[...] = second
     at = lax.axis_index("dp") * owned
     rows = pl.ds(pl.multiple_of(at % half, owned), owned)
@@ -456,7 +464,7 @@
     second_copy.wait()
 
 
-def kept_scores(owned, ids, first, sums, tally, other, picks, blocks):
+def kept_scores(owned, ids, first, sums, scale, other, picks, blocks):
     cent, width = first.shape
     half = K2 // 2
     return pl.pallas_call(
@@ -473,7 +481,7 @@
             pltpu.SemaphoreType.DMA((1,)),
         ],
         compiler_params=small(),
-    )(*[blocks[pick] for pick in picks], ids, first, sums, tally, other)
+    )(*[blocks[pick] for pick in picks], ids, first, sums, scale, other)
 
 
 def summed_scores(devices, second_level, first_centroids):
@@ -503,15 +511,21 @@
     def partner(value, index):
         return exchanged(value, [(d * cores + c, (d ^ index) * cores + c) for d, c in everyone])
 
+    def sideways(value, steps):
+        return exchanged(
+            value, [(d * cores + c, (d ^ steps[c % 2]) * cores + c) for d, c in everyone]
+        )
+
     def ahead(value, steps):
         return exchanged(
             value, [(d * cores + c, (d + steps) % devices * cores + c) for d, c in everyone]
         )
 
     own, own_meta, *sends = band_sums(devices, cent, first_level, embeddings, second_level)
+    turns = ((1, 2), (2, 1), (3, 3))
     got = [None] * GROUP
     for index in ORDER[:-1]:
-        got[index] = partner(sends[index - 1], index)
+        got[index] = sideways(sends[index - 1], turns[index - 1])
     got = got[1:]
     four = devices == GROUP * GROUP and cores == 2 and devices * cent <= K2
     base, base_meta, following, far = group_sums(cent, four, own, own_meta, got)
@@ -523,11 +537,6 @@
     if not four:
         return (mean, *summed_scores(devices, second_level, mean))
 
-    def sideways(value, steps):
-        return exchanged(
-            value, [(d * cores + c, (d ^ steps[c]) * cores + c) for d, c in everyone]
-        )
-
     def plane_rows(value):
         return [value, sideways(value, (1, 2)), sideways(value, (2, 1)), partner(value, 3)]
 
@@ -538,10 +547,10 @@
     near, ids = near_rows(cent, send, partner(send, GROUP))
     far = joined(partner(mean, 2 * GROUP), partner(mean, 3 * GROUP))
     blocks = plane_rows(near) + plane_rows(far)
-    sums, tally, first = gathered_sums(ids, mean, far, (0, 1, 2, 3, 4), blocks)
-    first_out, other, send = sent_scores(ids, first, sums, tally, (5, 6, 7), blocks)
+    sums, scale, first, first_out = gathered_sums(ids, mean, far, (0, 1, 2, 3, 4), blocks)
+    other, send = sent_scores(ids, first, sums, scale, (5, 6, 7), blocks)
     got = exchanged(send, [(d * cores + c, d * cores + (c ^ 1)) for d, c in everyone])
-    second, keep = kept_scores(K2 // devices, ids, first, sums, tally, other, (5, 6, 7), blocks)
+    second, keep = kept_scores(K2 // devices, ids, first, sums, scale, other, (5, 6, 7), blocks)
     return first_out, second, keep + got.astype(F32)
 
 

time: 42.2 us -> 42.1 us (level)
  starting transfers between devices: 21.8 us -> 20.9 us
  Pallas kernels: 6.62 us -> 7.19 us
    ppermute x15, starting transfers between devices: 21.8 us -> 20.9 us  [exchanged(): return lax.ppermute(value, ('dp', 'mp'), pairs)]
    pallas_call x1, Pallas kernels: 0.99 us -> 1.58 us  [gathered_sums(): pl.pallas_call(functools.partial(gather_kernel, picks), in_specs=[whole()...]
  transfers between devices with their start and end apart: 15 -> 15, of which waited for: 11 -> 12; matrix products, arithmetic and copies ran while one was open for 0% -> 0% of each run, Pallas kernels for 8% -> 9%
where the time goes in v7:
time: 42.1 us; the launch traced here: 41.8 us
  starting transfers between devices  20.9 us (50%)
  waiting for transfers between devices  12.3 us (29%)
  Pallas kernels  7.19 us (17%)
  between operations  0.71 us (2%)
  other arithmetic  0.67 us (2%)
    ppermute x15, starting transfers between devices, exchanged(): return lax.ppermute(value, ('dp', 'mp'), pairs)  20.9 us
    ppermute x15, waiting for transfers between devices, exchanged(): return lax.ppermute(value, ('dp', 'mp'), pairs)  12.3 us
    pallas_call x1, Pallas kernels, band_sums(): pl.pallas_call(functools.partial(first_kernel, devices, cent, chunks), in...  2.43 us
    pallas_call x1, Pallas kernels, gathered_sums(): pl.pallas_call(functools.partial(gather_kernel, picks), in_specs=[whole()...  1.58 us
    pallas_call x1, Pallas kernels, kept_scores(): pl.pallas_call(functools.partial(keep_kernel, owned, picks), in_specs=[wh...  1.11 us
    pallas_call x1, Pallas kernels, band_sums(): pl.pallas_call(functools.partial(second_kernel, cent, [(0, half), (half,...  1.01 us
  transfers between devices with their start and end apart: 15, of which 12 were waited for; matrix products, arithmetic and copies ran while one was open for 0% of the time, Pallas kernels for 9%

profile of v7, /device:TPU:0, one launch (start us, length us, event | category | flops | bytes accessed | tf_op | source)
XLA Modules:
  0.0 41.8 jit_solution(11229496681371710899)
XLA Ops:
  0.6 2.4 %shard_map.58 = (bf16[136,512]{1,0:T(8,128)(2,1)S(1)}, bf16[136,512]{1,0:T(8,128)(2,1)S(1)}, bf16[3072,512]{1,0:T(8,128)(2,1)S(1)}, s32[1,3072]{1,0:T(1,128)S(1)}, f32[2,64]{1,0:T(2,128)S(1)}) custom-call(s32[1,3072]{1,0:T(1,128)} %bitcast.2, bf16[3072,512]{1,0:T(8,128)(2,1)} %rows_hbm.1, s32[1,64]{1,0:T(1,128)} %bitcast.3), custom_call_target="tpu_custom_call" | custom-call | tf_op jit(solution)/shard_map/pallas_call | solution.py:158
  3.1 4.0 %collective-permute-start = (bf16[136,512]{1,0:T(8,128)(2,1)S(1)}, bf16[136,512]{1,0:T(8,128)(2,1)S(1)}, u32[]{:S(2)}, u32[]{:S(2)}) collective-permute-start(bf16[136,512]{1,0:T(8,128)(2,1)S(1)} %get-tuple-element.27), channel_id=1, source_target_pairs={{0,6},{1,7},{2,4},{3,5},{4,2},{5,3},{6,0},{7,1},{8,14},{9,15},{10,... | collective-permute-start | bytes 417800 | tf_op jit(solution)/shard_map/ppermute | solution.py:29
  7.6 1.0 %shard_map.59 = (bf16[136,512]{1,0:T(8,128)(2,1)S(1)}, f32[128,512]{1,0:T(8,128)S(1)}, f32[8,256]{1,0:T(8,128)S(1)}) custom-call(s32[1,3072]{1,0:T(1,128)S(1)} %get-tuple-element.29.label_ref, bf16[3072,512]{1,0:T(8,128)(2,1)S(1)} %get-tuple-element.30.rows_ref, f32[2,64]{1,0:T(2,128)S(1)} %get-tuple-element.31.digits_ref), custom_call_target="tpu_custom_call" | custom-call | flops 99999997952 | bytes 300000000 | tf_op jit(solution)/shard_map/pallas_call | solution.py:181
  8.7 2.4 %collective-permute-done.three = bf16[136,512]{1,0:T(8,128)(2,1)S(1)} collective-permute-done((bf16[136,512]{1,0:T(8,128)(2,1)S(1)}, bf16[136,512]{1,0:T(8,128)(2,1)S(1)}, u32[]{:S(2)}, u32[]{:S(2)}) %collective-permute-start) | collective-permute-done | bytes 139296 | tf_op jit(solution)/shard_map/ppermute | solution.py:29
  11.1 2.9 %collective-permute-done.1.one = bf16[136,512]{1,0:T(8,128)(2,1)S(1)} collective-permute-done((bf16[136,512]{1,0:T(8,128)(2,1)S(1)}, bf16[136,512]{1,0:T(8,128)(2,1)S(1)}, u32[]{:S(2)}, u32[]{:S(2)}) %collective-permute-start.1) | collective-permute-done | bytes 139296 | tf_op jit(solution)/shard_map/ppermute | solution.py:29
  14.1 2.7 %collective-permute-start.3 = (bf16[72,512]{1,0:T(8,128)(2,1)S(1)}, bf16[72,512]{1,0:T(8,128)(2,1)S(1)}, u32[]{:S(2)}, u32[]{:S(2)}) collective-permute-start(bf16[72,512]{1,0:T(8,128)(2,1)S(1)} %get-tuple-element.35), channel_id=1, source_target_pairs={{0,16},{1,17},{2,18},{3,19},{4,20},{5,21},{6,22},{7,23},{8,24},{9,... | collective-permute-start | bytes 221192 | tf_op jit(solution)/shard_map/ppermute | solution.py:29
  16.8 1.6 %collective-permute-start.4 = (bf16[72,512]{1,0:T(8,128)(2,1)S(1)}, bf16[72,512]{1,0:T(8,128)(2,1)S(1)}, u32[]{:S(2)}, u32[]{:S(2)}) collective-permute-start(bf16[72,512]{1,0:T(8,128)(2,1)S(1)} %get-tuple-element.36), channel_id=1, source_target_pairs={{0,8},{1,9},{2,10},{3,11},{4,12},{5,13},{6,14},{7,15},{8,0},{9,1},... | collective-permute-start | bytes 221192 | tf_op jit(solution)/shard_map/ppermute | solution.py:29
  18.4 1.8 %collective-permute-done.3.two = bf16[72,512]{1,0:T(8,128)(2,1)S(1)} collective-permute-done((bf16[72,512]{1,0:T(8,128)(2,1)S(1)}, bf16[72,512]{1,0:T(8,128)(2,1)S(1)}, u32[]{:S(2)}, u32[]{:S(2)}) %collective-permute-start.3) | collective-permute-done | bytes 73760 | tf_op jit(solution)/shard_map/ppermute | solution.py:29
  20.1 1.0 %collective-permute-done.4.one = bf16[72,512]{1,0:T(8,128)(2,1)S(1)} collective-permute-done((bf16[72,512]{1,0:T(8,128)(2,1)S(1)}, bf16[72,512]{1,0:T(8,128)(2,1)S(1)}, u32[]{:S(2)}, u32[]{:S(2)}) %collective-permute-start.4) | collective-permute-done | bytes 73760 | tf_op jit(solution)/shard_map/ppermute | solution.py:29
  21.3 1.6 %collective-permute-start.5 = (bf16[72,512]{1,0:T(8,128)(2,1)S(1)}, bf16[72,512]{1,0:T(8,128)(2,1)S(1)}, u32[]{:S(2)}, u32[]{:S(2)}) collective-permute-start(bf16[72,512]{1,0:T(8,128)(2,1)S(1)} %get-tuple-element.39.own), channel_id=1, source_target_pairs={{0,8},{1,9},{2,10},{3,11},{4,12},{5,13},{6,14},{7,15},{8,0},{9,1},... | collective-permute-start | bytes 221192 | tf_op jit(solution)/shard_map/ppermute | solution.py:29
  23.0 1.8 %collective-permute-start.10 = (bf16[64,512]{1,0:T(8,128)(2,1)S(1)}, bf16[64,512]{1,0:T(8,128)(2,1)S(1)}, u32[]{:S(2)}, u32[]{:S(2)}) collective-permute-start(bf16[64,512]{1,0:T(8,128)(2,1)S(1)} %get-tuple-element.41.refs_6_), channel_id=1, source_target_pairs={{0,16},{1,17},{2,18},{3,19},{4,20},{5,21},{6,22},{7,23},{8,24},{9,... | collective-permute-start | bytes 196616 | tf_op jit(solution)/shard_map/ppermute | solution.py:29
  24.8 1.0 %collective-permute-start.9 = (bf16[64,512]{1,0:T(8,128)(2,1)S(1)}, bf16[64,512]{1,0:T(8,128)(2,1)S(1)}, u32[]{:S(2)}, u32[]{:S(2)}) collective-permute-start(bf16[64,512]{1,0:T(8,128)(2,1)S(1)} %get-tuple-element.41.refs_6_), channel_id=1, source_target_pairs={{0,24},{1,25},{2,26},{3,27},{4,28},{5,29},{6,30},{7,31},{8,16},{9,... | collective-permute-start | bytes 196616 | tf_op jit(solution)/shard_map/ppermute | solution.py:29
  26.0 1.7 %collective-permute-start.8 = (bf16[128,512]{1,0:T(8,128)(2,1)S(1)}, bf16[128,512]{1,0:T(8,128)(2,1)S(1)}, u32[]{:S(2)}, u32[]{:S(2)}) collective-permute-start(bf16[128,512]{1,0:T(8,128)(2,1)S(1)} %get-tuple-element.40.refs_0_), channel_id=1, source_target_pairs={{0,6},{1,7},{2,4},{3,5},{4,2},{5,3},{6,0},{7,1},{8,14},{9,15},{10,... | collective-permute-start | bytes 393224 | tf_op jit(solution)/shard_map/ppermute | solution.py:29
  27.6 1.5 %collective-permute-start.7 = (bf16[128,512]{1,0:T(8,128)(2,1)S(1)}, bf16[128,512]{1,0:T(8,128)(2,1)S(1)}, u32[]{:S(2)}, u32[]{:S(2)}) collective-permute-start(bf16[128,512]{1,0:T(8,128)(2,1)S(1)} %get-tuple-element.40.refs_0_), channel_id=1, source_target_pairs={{0,4},{1,3},{2,6},{3,1},{4,0},{5,7},{6,2},{7,5},{8,12},{9,11},{10,... | collective-permute-start | bytes 393224 | tf_op jit(solution)/shard_map/ppermute | solution.py:29
  29.5 1.3 %collective-permute-done.9.second = bf16[64,512]{1,0:T(8,128)(2,1)S(1)} collective-permute-done((bf16[64,512]{1,0:T(8,128)(2,1)S(1)}, bf16[64,512]{1,0:T(8,128)(2,1)S(1)}, u32[]{:S(2)}, u32[]{:S(2)}) %collective-permute-start.9) | collective-permute-done | bytes 65568 | tf_op jit(solution)/shard_map/ppermute | solution.py:29
  30.9 1.6 %collective-permute-start.13 = (bf16[128,512]{1,0:T(8,128)(2,1)S(1)}, bf16[128,512]{1,0:T(8,128)(2,1)S(1)}, u32[]{:S(2)}, u32[]{:S(2)}) collective-permute-start(bf16[128,512]{1,0:T(8,128)(2,1)S(1)} %shard_map.63.refs_4_.refs_7_), channel_id=1, source_target_pairs={{0,6},{1,7},{2,4},{3,5},{4,2},{5,3},{6,0},{7,1},{8,14},{9,15},{10,... | collective-permute-start | bytes 393224 | tf_op jit(solution)/shard_map/ppermute | solution.py:29
  32.4 1.2 %collective-permute-start.12 = (bf16[128,512]{1,0:T(8,128)(2,1)S(1)}, bf16[128,512]{1,0:T(8,128)(2,1)S(1)}, u32[]{:S(2)}, u32[]{:S(2)}) collective-permute-start(bf16[128,512]{1,0:T(8,128)(2,1)S(1)} %shard_map.63.refs_4_.refs_7_), channel_id=1, source_target_pairs={{0,4},{1,3},{2,6},{3,1},{4,0},{5,7},{6,2},{7,5},{8,12},{9,11},{10,... | collective-permute-start | bytes 393224 | tf_op jit(solution)/shard_map/ppermute | solution.py:29
  33.7 1.2 %collective-permute-start.11 = (bf16[128,512]{1,0:T(8,128)(2,1)S(1)}, bf16[128,512]{1,0:T(8,128)(2,1)S(1)}, u32[]{:S(2)}, u32[]{:S(2)}) collective-permute-start(bf16[128,512]{1,0:T(8,128)(2,1)S(1)} %shard_map.63.refs_4_.refs_7_), channel_id=1, source_target_pairs={{0,2},{1,5},{2,0},{3,7},{4,6},{5,1},{6,4},{7,3},{8,10},{9,13},{10,... | collective-permute-start | bytes 393224 | tf_op jit(solution)/shard_map/ppermute | solution.py:29
  35.5 1.6 %shard_map.64 = (f32[1024,512]{1,0:T(8,128)S(1)}, f32[1024,128]{1,0:T(8,128)S(1)}, bf16[64,512]{1,0:T(8,128)(2,1)S(1)}, bf16[64,512]{1,0:T(8,128)(2,1)}) custom-call(bf16[128,512]{1,0:T(8,128)(2,1)S(1)} %get-tuple-element.40.refs_0_, bf16[128,512]{1,0:T(8,128)(2,1)S(1)} %collective-permute-done.6.refs_1_, ...), custom_call_target="tpu_custom_call" | custom-call | tf_op jit(solution)/shard_map/pallas_call | solution.py:391
  37.1 0.8 %collective-permute-done.13.refs_2_ = bf16[128,512]{1,0:T(8,128)(2,1)S(1)} collective-permute-done((bf16[128,512]{1,0:T(8,128)(2,1)S(1)}, bf16[128,512]{1,0:T(8,128)(2,1)S(1)}, u32[]{:S(2)}, u32[]{:S(2)}) %collective-permute-start.13) | collective-permute-done | bytes 131104 | tf_op jit(solution)/shard_map/ppermute | solution.py:29
  37.9 1.1 %collective-permute-done.12.refs_1_ = bf16[128,512]{1,0:T(8,128)(2,1)S(1)} collective-permute-done((bf16[128,512]{1,0:T(8,128)(2,1)S(1)}, bf16[128,512]{1,0:T(8,128)(2,1)S(1)}, u32[]{:S(2)}, u32[]{:S(2)}) %collective-permute-start.12) | collective-permute-done | bytes 131104 | tf_op jit(solution)/shard_map/ppermute | solution.py:29
  39.2 0.6 %shard_map.65 = (bf16[512,512]{1,0:T(8,128)(2,1)S(1)}, bf16[64,512]{1,0:T(8,128)(2,1)S(1)}) custom-call(bf16[128,512]{1,0:T(8,128)(2,1)S(1)} %collective-permute-done.11.refs_0_, bf16[128,512]{1,0:T(8,128)(2,1)S(1)} %collective-permute-done.12.refs_1_, bf16[128,512]{1,0:T(8,128)(2,1)S(1)} %collective-permute-done.13.refs_2_, ...), custom_call_target="tpu_custom_call" | custom-call | tf_op jit(solution)/shard_map/pallas_call | solution.py:439
  39.9 1.1 %shard_map.66 = (bf16[64,512]{1,0:T(8,128)(2,1)}, f32[64,512]{1,0:T(8,128)S(1)}) custom-call(bf16[128,512]{1,0:T(8,128)(2,1)S(1)} %collective-permute-done.11.refs_0_, bf16[128,512]{1,0:T(8,128)(2,1)S(1)} %collective-permute-done.12.refs_1_, bf16[128,512]{1,0:T(8,128)(2,1)S(1)} %collective-permute-done.13.refs_2_, ...), custom_call_target="tpu_custom_call" | custom-call | tf_op jit(solution)/shard_map/pallas_call | solution.py:470
  41.1 0.7 %convert_add_fusion = f32[64,512]{1,0:T(8,128)} fusion(f32[64,512]{1,0:T(8,128)S(1)} %get-tuple-element.49, bf16[64,512]{1,0:T(8,128)(2,1)S(1)} %collective-permute-done.14), kind=kLoop, calls=%fused_computation | loop fusion | flops 65536 | bytes 327680 | tf_op jit(solution)/shard_map/add | solution.py:554
  (16 shorter events, 2.6 us)
Async XLA Ops:
  3.1 8.0 %collective-permute-start = (bf16[136,512]{1,0:T(8,128)(2,1)S(1)}, bf16[136,512]{1,0:T(8,128)(2,1)S(1)}, u32[]{:S(2)}, u32[]{:S(2)}) collective-permute-start(bf16[136,512]{1,0:T(8,128)(2,1)S(1)} %get-tuple-element.27), channel_id=1, source_target_pairs={{0,6},{1,7},{2,4},{3,5},{4,2},{5,3},{6,0},{7,1},{8,14},{9,15},{10,... | collective-permute-start | bytes 417800 | tf_op jit(solution)/shard_map/ppermute | solution.py:29
  7.0 7.0 %collective-permute-start.1 = (bf16[136,512]{1,0:T(8,128)(2,1)S(1)}, bf16[136,512]{1,0:T(8,128)(2,1)S(1)}, u32[]{:S(2)}, u32[]{:S(2)}) collective-permute-start(bf16[136,512]{1,0:T(8,128)(2,1)S(1)} %get-tuple-element.28), channel_id=1, source_target_pairs={{0,2},{1,5},{2,0},{3,7},{4,6},{5,1},{6,4},{7,3},{8,10},{9,13},{10,... | collective-permute-start | bytes 417800 | tf_op jit(solution)/shard_map/ppermute | solution.py:29
  8.6 5.4 %collective-permute-start.2 = (bf16[136,512]{1,0:T(8,128)(2,1)S(1)}, bf16[136,512]{1,0:T(8,128)(2,1)S(1)}, u32[]{:S(2)}, u32[]{:S(2)}) collective-permute-start(bf16[136,512]{1,0:T(8,128)(2,1)S(1)} %get-tuple-element.32), channel_id=1, source_target_pairs={{0,4},{1,3},{2,6},{3,1},{4,0},{5,7},{6,2},{7,5},{8,12},{9,11},{10,... | collective-permute-start | bytes 417800 | tf_op jit(solution)/shard_map/ppermute | solution.py:29
  14.1 6.0 %collective-permute-start.3 = (bf16[72,512]{1,0:T(8,128)(2,1)S(1)}, bf16[72,512]{1,0:T(8,128)(2,1)S(1)}, u32[]{:S(2)}, u32[]{:S(2)}) collective-permute-start(bf16[72,512]{1,0:T(8,128)(2,1)S(1)} %get-tuple-element.35), channel_id=1, source_target_pairs={{0,16},{1,17},{2,18},{3,19},{4,20},{5,21},{6,22},{7,23},{8,24},{9,... | collective-permute-start | bytes 221192 | tf_op jit(solution)/shard_map/ppermute | solution.py:29
  16.8 4.4 %collective-permute-start.4 = (bf16[72,512]{1,0:T(8,128)(2,1)S(1)}, bf16[72,512]{1,0:T(8,128)(2,1)S(1)}, u32[]{:S(2)}, u32[]{:S(2)}) collective-permute-start(bf16[72,512]{1,0:T(8,128)(2,1)S(1)} %get-tuple-element.36), channel_id=1, source_target_pairs={{0,8},{1,9},{2,10},{3,11},{4,12},{5,13},{6,14},{7,15},{8,0},{9,1},... | collective-permute-start | bytes 221192 | tf_op jit(solution)/shard_map/ppermute | solution.py:29
  21.3 4.5 %collective-permute-start.5 = (bf16[72,512]{1,0:T(8,128)(2,1)S(1)}, bf16[72,512]{1,0:T(8,128)(2,1)S(1)}, u32[]{:S(2)}, u32[]{:S(2)}) collective-permute-start(bf16[72,512]{1,0:T(8,128)(2,1)S(1)} %get-tuple-element.39.own), channel_id=1, source_target_pairs={{0,8},{1,9},{2,10},{3,11},{4,12},{5,13},{6,14},{7,15},{8,0},{9,1},... | collective-permute-start | bytes 221192 | tf_op jit(solution)/shard_map/ppermute | solution.py:29
  23.0 6.6 %collective-permute-start.10 = (bf16[64,512]{1,0:T(8,128)(2,1)S(1)}, bf16[64,512]{1,0:T(8,128)(2,1)S(1)}, u32[]{:S(2)}, u32[]{:S(2)}) collective-permute-start(bf16[64,512]{1,0:T(8,128)(2,1)S(1)} %get-tuple-element.41.refs_6_), channel_id=1, source_target_pairs={{0,16},{1,17},{2,18},{3,19},{4,20},{5,21},{6,22},{7,23},{8,24},{9,... | collective-permute-start | bytes 196616 | tf_op jit(solution)/shard_map/ppermute | solution.py:29
  24.8 6.1 %collective-permute-start.9 = (bf16[64,512]{1,0:T(8,128)(2,1)S(1)}, bf16[64,512]{1,0:T(8,128)(2,1)S(1)}, u32[]{:S(2)}, u32[]{:S(2)}) collective-permute-start(bf16[64,512]{1,0:T(8,128)(2,1)S(1)} %get-tuple-element.41.refs_6_), channel_id=1, source_target_pairs={{0,24},{1,25},{2,26},{3,27},{4,28},{5,29},{6,30},{7,31},{8,16},{9,... | collective-permute-start | bytes 196616 | tf_op jit(solution)/shard_map/ppermute | solution.py:29
  26.0 7.7 %collective-permute-start.8 = (bf16[128,512]{1,0:T(8,128)(2,1)S(1)}, bf16[128,512]{1,0:T(8,128)(2,1)S(1)}, u32[]{:S(2)}, u32[]{:S(2)}) collective-permute-start(bf16[128,512]{1,0:T(8,128)(2,1)S(1)} %get-tuple-element.40.refs_0_), channel_id=1, source_target_pairs={{0,6},{1,7},{2,4},{3,5},{4,2},{5,3},{6,0},{7,1},{8,14},{9,15},{10,... | collective-permute-start | bytes 393224 | tf_op jit(solution)/shard_map/ppermute | solution.py:29
  27.6 7.8 %collective-permute-start.7 = (bf16[128,512]{1,0:T(8,128)(2,1)S(1)}, bf16[128,512]{1,0:T(8,128)(2,1)S(1)}, u32[]{:S(2)}, u32[]{:S(2)}) collective-permute-start(bf16[128,512]{1,0:T(8,128)(2,1)S(1)} %get-tuple-element.40.refs_0_), channel_id=1, source_target_pairs={{0,4},{1,3},{2,6},{3,1},{4,0},{5,7},{6,2},{7,5},{8,12},{9,11},{10,... | collective-permute-start | bytes 393224 | tf_op jit(solution)/shard_map/ppermute | solution.py:29
  29.2 6.3 %collective-permute-start.6 = (bf16[128,512]{1,0:T(8,128)(2,1)S(1)}, bf16[128,512]{1,0:T(8,128)(2,1)S(1)}, u32[]{:S(2)}, u32[]{:S(2)}) collective-permute-start(bf16[128,512]{1,0:T(8,128)(2,1)S(1)} %get-tuple-element.40.refs_0_), channel_id=1, source_target_pairs={{0,2},{1,5},{2,0},{3,7},{4,6},{5,1},{6,4},{7,3},{8,10},{9,13},{10,... | collective-permute-start | bytes 393224 | tf_op jit(solution)/shard_map/ppermute | solution.py:29
  30.9 7.1 %collective-permute-start.13 = (bf16[128,512]{1,0:T(8,128)(2,1)S(1)}, bf16[128,512]{1,0:T(8,128)(2,1)S(1)}, u32[]{:S(2)}, u32[]{:S(2)}) collective-permute-start(bf16[128,512]{1,0:T(8,128)(2,1)S(1)} %shard_map.63.refs_4_.refs_7_), channel_id=1, source_target_pairs={{0,6},{1,7},{2,4},{3,5},{4,2},{5,3},{6,0},{7,1},{8,14},{9,15},{10,... | collective-permute-start | bytes 393224 | tf_op jit(solution)/shard_map/ppermute | solution.py:29
  32.4 6.6 %collective-permute-start.12 = (bf16[128,512]{1,0:T(8,128)(2,1)S(1)}, bf16[128,512]{1,0:T(8,128)(2,1)S(1)}, u32[]{:S(2)}, u32[]{:S(2)}) collective-permute-start(bf16[128,512]{1,0:T(8,128)(2,1)S(1)} %shard_map.63.refs_4_.refs_7_), channel_id=1, source_target_pairs={{0,4},{1,3},{2,6},{3,1},{4,0},{5,7},{6,2},{7,5},{8,12},{9,11},{10,... | collective-permute-start | bytes 393224 | tf_op jit(solution)/shard_map/ppermute | solution.py:29
  33.7 5.5 %collective-permute-start.11 = (bf16[128,512]{1,0:T(8,128)(2,1)S(1)}, bf16[128,512]{1,0:T(8,128)(2,1)S(1)}, u32[]{:S(2)}, u32[]{:S(2)}) collective-permute-start(bf16[128,512]{1,0:T(8,128)(2,1)S(1)} %shard_map.63.refs_4_.refs_7_), channel_id=1, source_target_pairs={{0,2},{1,5},{2,0},{3,7},{4,6},{5,1},{6,4},{7,3},{8,10},{9,13},{10,... | collective-permute-start | bytes 393224 | tf_op jit(solution)/shard_map/ppermute | solution.py:29
  39.8 1.3 %collective-permute-start.14 = (bf16[64,512]{1,0:T(8,128)(2,1)S(1)}, bf16[64,512]{1,0:T(8,128)(2,1)S(1)}, u32[]{:S(2)}, u32[]{:S(2)}) collective-permute-start(bf16[64,512]{1,0:T(8,128)(2,1)S(1)} %get-tuple-element.50), channel_id=1, source_target_pairs={{0,1},{1,0},{2,3},{3,2},{4,5},{5,4},{6,7},{7,6},{8,9},{9,8},{10,11... | collective-permute-start | bytes 196616 | tf_op jit(solution)/shard_map/ppermute | solution.py:29

commit v8 on v7

--- a/solution.py
+++ b/solution.py
@@ -10,7 +10,7 @@
 BAND = 8
 K2 = 1024
 GROUP = 4
-META = 8
+META = 16
 BASE = 256
 LANES = 128
 BF16 = jnp.bfloat16
@@ -225,6 +225,7 @@
         jnp.where(swapped, id_digits[2], id_digits[1]),
         jnp.where(swapped, id_digits[1], id_digits[2]),
     )
+    id_digits.append(jnp.zeros((META - 2 * GROUP, LANES), F32))
     id_digits = jnp.concatenate(id_digits, axis=0)
 
     def meta_of(row):

time: 42.1 us -> 43 us (1.021)
  waiting for transfers between devices: 12.3 us -> 13.2 us
    ppermute x15, waiting for transfers between devices: 12.3 us -> 13.2 us  [exchanged(): return lax.ppermute(value, ('dp', 'mp'), pairs)]
  transfers between devices with their start and end apart: 15 -> 15, of which waited for: 12 -> 10; matrix products, arithmetic and copies ran while one was open for 0% -> 0% of each run, Pallas kernels for 9% -> 9%
where the time goes in v8:
time: 43 us; the launch traced here: 42.7 us
  starting transfers between devices  20.9 us (49%)
  waiting for transfers between devices  13.2 us (31%)
  Pallas kernels  7.19 us (17%)
  between operations  0.72 us (2%)
  other arithmetic  0.67 us (2%)
    ppermute x15, starting transfers between devices, exchanged(): return lax.ppermute(value, ('dp', 'mp'), pairs)  20.9 us
    ppermute x15, waiting for transfers between devices, exchanged(): return lax.ppermute(value, ('dp', 'mp'), pairs)  13.2 us
    pallas_call x1, Pallas kernels, band_sums(): pl.pallas_call(functools.partial(first_kernel, devices, cent, chunks), in...  2.43 us
    pallas_call x1, Pallas kernels, gathered_sums(): pl.pallas_call(functools.partial(gather_kernel, picks), in_specs=[whole()...  1.58 us
    pallas_call x1, Pallas kernels, kept_scores(): pl.pallas_call(functools.partial(keep_kernel, owned, picks), in_specs=[wh...  1.1 us
    pallas_call x1, Pallas kernels, band_sums(): pl.pallas_call(functools.partial(second_kernel, cent, [(0, half), (half,...  1.01 us
  transfers between devices with their start and end apart: 15, of which 10 were waited for; matrix products, arithmetic and copies ran while one was open for 0% of the time, Pallas kernels for 9%

profile of v8, /device:TPU:0, one launch (start us, length us, event | category | flops | bytes accessed | tf_op | source)
XLA Modules:
  0.0 42.7 jit_solution(9962382370893868450)
XLA Ops:
  0.6 2.4 %shard_map.58 = (bf16[144,512]{1,0:T(8,128)(2,1)S(1)}, bf16[144,512]{1,0:T(8,128)(2,1)S(1)}, bf16[3072,512]{1,0:T(8,128)(2,1)S(1)}, s32[1,3072]{1,0:T(1,128)S(1)}, f32[2,64]{1,0:T(2,128)S(1)}) custom-call(s32[1,3072]{1,0:T(1,128)} %bitcast.2, bf16[3072,512]{1,0:T(8,128)(2,1)} %rows_hbm.1, s32[1,64]{1,0:T(1,128)} %bitcast.3), custom_call_target="tpu_custom_call" | custom-call | tf_op jit(solution)/shard_map/pallas_call | solution.py:158
  3.1 4.0 %collective-permute-start = (bf16[144,512]{1,0:T(8,128)(2,1)S(1)}, bf16[144,512]{1,0:T(8,128)(2,1)S(1)}, u32[]{:S(2)}, u32[]{:S(2)}) collective-permute-start(bf16[144,512]{1,0:T(8,128)(2,1)S(1)} %get-tuple-element.27), channel_id=1, source_target_pairs={{0,6},{1,7},{2,4},{3,5},{4,2},{5,3},{6,0},{7,1},{8,14},{9,15},{10,... | collective-permute-start | bytes 442376 | tf_op jit(solution)/shard_map/ppermute | solution.py:29
  7.6 1.0 %shard_map.59 = (bf16[144,512]{1,0:T(8,128)(2,1)S(1)}, f32[128,512]{1,0:T(8,128)S(1)}, f32[16,256]{1,0:T(8,128)S(1)}) custom-call(s32[1,3072]{1,0:T(1,128)S(1)} %get-tuple-element.29.label_ref, bf16[3072,512]{1,0:T(8,128)(2,1)S(1)} %get-tuple-element.30.rows_ref, f32[2,64]{1,0:T(2,128)S(1)} %get-tuple-element.31.digits_ref), custom_call_target="tpu_custom_call" | custom-call | flops 99999997952 | bytes 300000000 | tf_op jit(solution)/shard_map/pallas_call | solution.py:181
  8.7 2.5 %collective-permute-done.three = bf16[144,512]{1,0:T(8,128)(2,1)S(1)} collective-permute-done((bf16[144,512]{1,0:T(8,128)(2,1)S(1)}, bf16[144,512]{1,0:T(8,128)(2,1)S(1)}, u32[]{:S(2)}, u32[]{:S(2)}) %collective-permute-start) | collective-permute-done | bytes 147488 | tf_op jit(solution)/shard_map/ppermute | solution.py:29
  11.3 3.0 %collective-permute-done.1.one = bf16[144,512]{1,0:T(8,128)(2,1)S(1)} collective-permute-done((bf16[144,512]{1,0:T(8,128)(2,1)S(1)}, bf16[144,512]{1,0:T(8,128)(2,1)S(1)}, u32[]{:S(2)}, u32[]{:S(2)}) %collective-permute-start.1) | collective-permute-done | bytes 147488 | tf_op jit(solution)/shard_map/ppermute | solution.py:29
  14.5 2.7 %collective-permute-start.3 = (bf16[80,512]{1,0:T(8,128)(2,1)S(1)}, bf16[80,512]{1,0:T(8,128)(2,1)S(1)}, u32[]{:S(2)}, u32[]{:S(2)}) collective-permute-start(bf16[80,512]{1,0:T(8,128)(2,1)S(1)} %get-tuple-element.35), channel_id=1, source_target_pairs={{0,16},{1,17},{2,18},{3,19},{4,20},{5,21},{6,22},{7,23},{8,24},{9,... | collective-permute-start | bytes 245768 | tf_op jit(solution)/shard_map/ppermute | solution.py:29
  17.1 1.6 %collective-permute-start.4 = (bf16[80,512]{1,0:T(8,128)(2,1)S(1)}, bf16[80,512]{1,0:T(8,128)(2,1)S(1)}, u32[]{:S(2)}, u32[]{:S(2)}) collective-permute-start(bf16[80,512]{1,0:T(8,128)(2,1)S(1)} %get-tuple-element.36), channel_id=1, source_target_pairs={{0,8},{1,9},{2,10},{3,11},{4,12},{5,13},{6,14},{7,15},{8,0},{9,1},... | collective-permute-start | bytes 245768 | tf_op jit(solution)/shard_map/ppermute | solution.py:29
  18.7 1.7 %collective-permute-done.3.two = bf16[80,512]{1,0:T(8,128)(2,1)S(1)} collective-permute-done((bf16[80,512]{1,0:T(8,128)(2,1)S(1)}, bf16[80,512]{1,0:T(8,128)(2,1)S(1)}, u32[]{:S(2)}, u32[]{:S(2)}) %collective-permute-start.3) | collective-permute-done | bytes 81952 | tf_op jit(solution)/shard_map/ppermute | solution.py:29
  20.5 1.1 %collective-permute-done.4.one = bf16[80,512]{1,0:T(8,128)(2,1)S(1)} collective-permute-done((bf16[80,512]{1,0:T(8,128)(2,1)S(1)}, bf16[80,512]{1,0:T(8,128)(2,1)S(1)}, u32[]{:S(2)}, u32[]{:S(2)}) %collective-permute-start.4) | collective-permute-done | bytes 81952 | tf_op jit(solution)/shard_map/ppermute | solution.py:29
  21.7 1.6 %collective-permute-start.5 = (bf16[80,512]{1,0:T(8,128)(2,1)S(1)}, bf16[80,512]{1,0:T(8,128)(2,1)S(1)}, u32[]{:S(2)}, u32[]{:S(2)}) collective-permute-start(bf16[80,512]{1,0:T(8,128)(2,1)S(1)} %get-tuple-element.39.own), channel_id=1, source_target_pairs={{0,8},{1,9},{2,10},{3,11},{4,12},{5,13},{6,14},{7,15},{8,0},{9,1},... | collective-permute-start | bytes 245768 | tf_op jit(solution)/shard_map/ppermute | solution.py:29
  23.4 1.9 %collective-permute-start.10 = (bf16[64,512]{1,0:T(8,128)(2,1)S(1)}, bf16[64,512]{1,0:T(8,128)(2,1)S(1)}, u32[]{:S(2)}, u32[]{:S(2)}) collective-permute-start(bf16[64,512]{1,0:T(8,128)(2,1)S(1)} %get-tuple-element.41.refs_6_), channel_id=1, source_target_pairs={{0,16},{1,17},{2,18},{3,19},{4,20},{5,21},{6,22},{7,23},{8,24},{9,... | collective-permute-start | bytes 196616 | tf_op jit(solution)/shard_map/ppermute | solution.py:29
  25.3 0.9 %collective-permute-start.9 = (bf16[64,512]{1,0:T(8,128)(2,1)S(1)}, bf16[64,512]{1,0:T(8,128)(2,1)S(1)}, u32[]{:S(2)}, u32[]{:S(2)}) collective-permute-start(bf16[64,512]{1,0:T(8,128)(2,1)S(1)} %get-tuple-element.41.refs_6_), channel_id=1, source_target_pairs={{0,24},{1,25},{2,26},{3,27},{4,28},{5,29},{6,30},{7,31},{8,16},{9,... | collective-permute-start | bytes 196616 | tf_op jit(solution)/shard_map/ppermute | solution.py:29
  26.2 0.7 %collective-permute-done.5.got = bf16[80,512]{1,0:T(8,128)(2,1)S(1)} collective-permute-done((bf16[80,512]{1,0:T(8,128)(2,1)S(1)}, bf16[80,512]{1,0:T(8,128)(2,1)S(1)}, u32[]{:S(2)}, u32[]{:S(2)}) %collective-permute-start.5) | collective-permute-done | bytes 81952 | tf_op jit(solution)/shard_map/ppermute | solution.py:29
  27.0 1.5 %collective-permute-start.8 = (bf16[128,512]{1,0:T(8,128)(2,1)S(1)}, bf16[128,512]{1,0:T(8,128)(2,1)S(1)}, u32[]{:S(2)}, u32[]{:S(2)}) collective-permute-start(bf16[128,512]{1,0:T(8,128)(2,1)S(1)} %get-tuple-element.40.refs_0_), channel_id=1, source_target_pairs={{0,6},{1,7},{2,4},{3,5},{4,2},{5,3},{6,0},{7,1},{8,14},{9,15},{10,... | collective-permute-start | bytes 393224 | tf_op jit(solution)/shard_map/ppermute | solution.py:29
  28.6 1.2 %collective-permute-start.7 = (bf16[128,512]{1,0:T(8,128)(2,1)S(1)}, bf16[128,512]{1,0:T(8,128)(2,1)S(1)}, u32[]{:S(2)}, u32[]{:S(2)}) collective-permute-start(bf16[128,512]{1,0:T(8,128)(2,1)S(1)} %get-tuple-element.40.refs_0_), channel_id=1, source_target_pairs={{0,4},{1,3},{2,6},{3,1},{4,0},{5,7},{6,2},{7,5},{8,12},{9,11},{10,... | collective-permute-start | bytes 393224 | tf_op jit(solution)/shard_map/ppermute | solution.py:29
  29.8 0.8 %collective-permute-start.6 = (bf16[128,512]{1,0:T(8,128)(2,1)S(1)}, bf16[128,512]{1,0:T(8,128)(2,1)S(1)}, u32[]{:S(2)}, u32[]{:S(2)}) collective-permute-start(bf16[128,512]{1,0:T(8,128)(2,1)S(1)} %get-tuple-element.40.refs_0_), channel_id=1, source_target_pairs={{0,2},{1,5},{2,0},{3,7},{4,6},{5,1},{6,4},{7,3},{8,10},{9,13},{10,... | collective-permute-start | bytes 393224 | tf_op jit(solution)/shard_map/ppermute | solution.py:29
  30.6 0.8 %collective-permute-done.9.second = bf16[64,512]{1,0:T(8,128)(2,1)S(1)} collective-permute-done((bf16[64,512]{1,0:T(8,128)(2,1)S(1)}, bf16[64,512]{1,0:T(8,128)(2,1)S(1)}, u32[]{:S(2)}, u32[]{:S(2)}) %collective-permute-start.9) | collective-permute-done | bytes 65568 | tf_op jit(solution)/shard_map/ppermute | solution.py:29
  31.4 1.6 %collective-permute-start.13 = (bf16[128,512]{1,0:T(8,128)(2,1)S(1)}, bf16[128,512]{1,0:T(8,128)(2,1)S(1)}, u32[]{:S(2)}, u32[]{:S(2)}) collective-permute-start(bf16[128,512]{1,0:T(8,128)(2,1)S(1)} %shard_map.63.refs_4_.refs_7_), channel_id=1, source_target_pairs={{0,6},{1,7},{2,4},{3,5},{4,2},{5,3},{6,0},{7,1},{8,14},{9,15},{10,... | collective-permute-start | bytes 393224 | tf_op jit(solution)/shard_map/ppermute | solution.py:29
  33.0 1.2 %collective-permute-start.12 = (bf16[128,512]{1,0:T(8,128)(2,1)S(1)}, bf16[128,512]{1,0:T(8,128)(2,1)S(1)}, u32[]{:S(2)}, u32[]{:S(2)}) collective-permute-start(bf16[128,512]{1,0:T(8,128)(2,1)S(1)} %shard_map.63.refs_4_.refs_7_), channel_id=1, source_target_pairs={{0,4},{1,3},{2,6},{3,1},{4,0},{5,7},{6,2},{7,5},{8,12},{9,11},{10,... | collective-permute-start | bytes 393224 | tf_op jit(solution)/shard_map/ppermute | solution.py:29
  34.2 1.1 %collective-permute-start.11 = (bf16[128,512]{1,0:T(8,128)(2,1)S(1)}, bf16[128,512]{1,0:T(8,128)(2,1)S(1)}, u32[]{:S(2)}, u32[]{:S(2)}) collective-permute-start(bf16[128,512]{1,0:T(8,128)(2,1)S(1)} %shard_map.63.refs_4_.refs_7_), channel_id=1, source_target_pairs={{0,2},{1,5},{2,0},{3,7},{4,6},{5,1},{6,4},{7,3},{8,10},{9,13},{10,... | collective-permute-start | bytes 393224 | tf_op jit(solution)/shard_map/ppermute | solution.py:29
  35.3 1.7 %collective-permute-done.7.refs_2_ = bf16[128,512]{1,0:T(8,128)(2,1)S(1)} collective-permute-done((bf16[128,512]{1,0:T(8,128)(2,1)S(1)}, bf16[128,512]{1,0:T(8,128)(2,1)S(1)}, u32[]{:S(2)}, u32[]{:S(2)}) %collective-permute-start.7) | collective-permute-done | bytes 131104 | tf_op jit(solution)/shard_map/ppermute | solution.py:29
  37.1 1.6 %shard_map.64 = (f32[1024,512]{1,0:T(8,128)S(1)}, f32[1024,128]{1,0:T(8,128)S(1)}, bf16[64,512]{1,0:T(8,128)(2,1)S(1)}, bf16[64,512]{1,0:T(8,128)(2,1)}) custom-call(bf16[128,512]{1,0:T(8,128)(2,1)S(1)} %get-tuple-element.40.refs_0_, bf16[128,512]{1,0:T(8,128)(2,1)S(1)} %collective-permute-done.6.refs_1_, ...), custom_call_target="tpu_custom_call" | custom-call | tf_op jit(solution)/shard_map/pallas_call | solution.py:392
  38.7 1.3 %collective-permute-done.12.refs_1_ = bf16[128,512]{1,0:T(8,128)(2,1)S(1)} collective-permute-done((bf16[128,512]{1,0:T(8,128)(2,1)S(1)}, bf16[128,512]{1,0:T(8,128)(2,1)S(1)}, u32[]{:S(2)}, u32[]{:S(2)}) %collective-permute-start.12) | collective-permute-done | bytes 131104 | tf_op jit(solution)/shard_map/ppermute | solution.py:29
  40.8 1.1 %shard_map.66 = (bf16[64,512]{1,0:T(8,128)(2,1)}, f32[64,512]{1,0:T(8,128)S(1)}) custom-call(bf16[128,512]{1,0:T(8,128)(2,1)S(1)} %collective-permute-done.11.refs_0_, bf16[128,512]{1,0:T(8,128)(2,1)S(1)} %collective-permute-done.12.refs_1_, bf16[128,512]{1,0:T(8,128)(2,1)S(1)} %collective-permute-done.13.refs_2_, ...), custom_call_target="tpu_custom_call" | custom-call | tf_op jit(solution)/shard_map/pallas_call | solution.py:471
  (16 shorter events, 2.8 us)
Async XLA Ops:
  3.1 8.2 %collective-permute-start = (bf16[144,512]{1,0:T(8,128)(2,1)S(1)}, bf16[144,512]{1,0:T(8,128)(2,1)S(1)}, u32[]{:S(2)}, u32[]{:S(2)}) collective-permute-start(bf16[144,512]{1,0:T(8,128)(2,1)S(1)} %get-tuple-element.27), channel_id=1, source_target_pairs={{0,6},{1,7},{2,4},{3,5},{4,2},{5,3},{6,0},{7,1},{8,14},{9,15},{10,... | collective-permute-start | bytes 442376 | tf_op jit(solution)/shard_map/ppermute | solution.py:29
  7.0 7.3 %collective-permute-start.1 = (bf16[144,512]{1,0:T(8,128)(2,1)S(1)}, bf16[144,512]{1,0:T(8,128)(2,1)S(1)}, u32[]{:S(2)}, u32[]{:S(2)}) collective-permute-start(bf16[144,512]{1,0:T(8,128)(2,1)S(1)} %get-tuple-element.28), channel_id=1, source_target_pairs={{0,2},{1,5},{2,0},{3,7},{4,6},{5,1},{6,4},{7,3},{8,10},{9,13},{10,... | collective-permute-start | bytes 442376 | tf_op jit(solution)/shard_map/ppermute | solution.py:29
  8.6 5.8 %collective-permute-start.2 = (bf16[144,512]{1,0:T(8,128)(2,1)S(1)}, bf16[144,512]{1,0:T(8,128)(2,1)S(1)}, u32[]{:S(2)}, u32[]{:S(2)}) collective-permute-start(bf16[144,512]{1,0:T(8,128)(2,1)S(1)} %get-tuple-element.32), channel_id=1, source_target_pairs={{0,4},{1,3},{2,6},{3,1},{4,0},{5,7},{6,2},{7,5},{8,12},{9,11},{10,... | collective-permute-start | bytes 442376 | tf_op jit(solution)/shard_map/ppermute | solution.py:29
  14.5 6.0 %collective-permute-start.3 = (bf16[80,512]{1,0:T(8,128)(2,1)S(1)}, bf16[80,512]{1,0:T(8,128)(2,1)S(1)}, u32[]{:S(2)}, u32[]{:S(2)}) collective-permute-start(bf16[80,512]{1,0:T(8,128)(2,1)S(1)} %get-tuple-element.35), channel_id=1, source_target_pairs={{0,16},{1,17},{2,18},{3,19},{4,20},{5,21},{6,22},{7,23},{8,24},{9,... | collective-permute-start | bytes 245768 | tf_op jit(solution)/shard_map/ppermute | solution.py:29
  17.1 4.4 %collective-permute-start.4 = (bf16[80,512]{1,0:T(8,128)(2,1)S(1)}, bf16[80,512]{1,0:T(8,128)(2,1)S(1)}, u32[]{:S(2)}, u32[]{:S(2)}) collective-permute-start(bf16[80,512]{1,0:T(8,128)(2,1)S(1)} %get-tuple-element.36), channel_id=1, source_target_pairs={{0,8},{1,9},{2,10},{3,11},{4,12},{5,13},{6,14},{7,15},{8,0},{9,1},... | collective-permute-start | bytes 245768 | tf_op jit(solution)/shard_map/ppermute | solution.py:29
  21.7 5.2 %collective-permute-start.5 = (bf16[80,512]{1,0:T(8,128)(2,1)S(1)}, bf16[80,512]{1,0:T(8,128)(2,1)S(1)}, u32[]{:S(2)}, u32[]{:S(2)}) collective-permute-start(bf16[80,512]{1,0:T(8,128)(2,1)S(1)} %get-tuple-element.39.own), channel_id=1, source_target_pairs={{0,8},{1,9},{2,10},{3,11},{4,12},{5,13},{6,14},{7,15},{8,0},{9,1},... | collective-permute-start | bytes 245768 | tf_op jit(solution)/shard_map/ppermute | solution.py:29
  23.4 7.2 %collective-permute-start.10 = (bf16[64,512]{1,0:T(8,128)(2,1)S(1)}, bf16[64,512]{1,0:T(8,128)(2,1)S(1)}, u32[]{:S(2)}, u32[]{:S(2)}) collective-permute-start(bf16[64,512]{1,0:T(8,128)(2,1)S(1)} %get-tuple-element.41.refs_6_), channel_id=1, source_target_pairs={{0,16},{1,17},{2,18},{3,19},{4,20},{5,21},{6,22},{7,23},{8,24},{9,... | collective-permute-start | bytes 196616 | tf_op jit(solution)/shard_map/ppermute | solution.py:29
  25.3 6.1 %collective-permute-start.9 = (bf16[64,512]{1,0:T(8,128)(2,1)S(1)}, bf16[64,512]{1,0:T(8,128)(2,1)S(1)}, u32[]{:S(2)}, u32[]{:S(2)}) collective-permute-start(bf16[64,512]{1,0:T(8,128)(2,1)S(1)} %get-tuple-element.41.refs_6_), channel_id=1, source_target_pairs={{0,24},{1,25},{2,26},{3,27},{4,28},{5,29},{6,30},{7,31},{8,16},{9,... | collective-permute-start | bytes 196616 | tf_op jit(solution)/shard_map/ppermute | solution.py:29
  27.0 7.2 %collective-permute-start.8 = (bf16[128,512]{1,0:T(8,128)(2,1)S(1)}, bf16[128,512]{1,0:T(8,128)(2,1)S(1)}, u32[]{:S(2)}, u32[]{:S(2)}) collective-permute-start(bf16[128,512]{1,0:T(8,128)(2,1)S(1)} %get-tuple-element.40.refs_0_), channel_id=1, source_target_pairs={{0,6},{1,7},{2,4},{3,5},{4,2},{5,3},{6,0},{7,1},{8,14},{9,15},{10,... | collective-permute-start | bytes 393224 | tf_op jit(solution)/shard_map/ppermute | solution.py:29
  28.6 8.5 %collective-permute-start.7 = (bf16[128,512]{1,0:T(8,128)(2,1)S(1)}, bf16[128,512]{1,0:T(8,128)(2,1)S(1)}, u32[]{:S(2)}, u32[]{:S(2)}) collective-permute-start(bf16[128,512]{1,0:T(8,128)(2,1)S(1)} %get-tuple-element.40.refs_0_), channel_id=1, source_target_pairs={{0,4},{1,3},{2,6},{3,1},{4,0},{5,7},{6,2},{7,5},{8,12},{9,11},{10,... | collective-permute-start | bytes 393224 | tf_op jit(solution)/shard_map/ppermute | solution.py:29
  29.8 7.3 %collective-permute-start.6 = (bf16[128,512]{1,0:T(8,128)(2,1)S(1)}, bf16[128,512]{1,0:T(8,128)(2,1)S(1)}, u32[]{:S(2)}, u32[]{:S(2)}) collective-permute-start(bf16[128,512]{1,0:T(8,128)(2,1)S(1)} %get-tuple-element.40.refs_0_), channel_id=1, source_target_pairs={{0,2},{1,5},{2,0},{3,7},{4,6},{5,1},{6,4},{7,3},{8,10},{9,13},{10,... | collective-permute-start | bytes 393224 | tf_op jit(solution)/shard_map/ppermute | solution.py:29
  31.4 7.3 %collective-permute-start.13 = (bf16[128,512]{1,0:T(8,128)(2,1)S(1)}, bf16[128,512]{1,0:T(8,128)(2,1)S(1)}, u32[]{:S(2)}, u32[]{:S(2)}) collective-permute-start(bf16[128,512]{1,0:T(8,128)(2,1)S(1)} %shard_map.63.refs_4_.refs_7_), channel_id=1, source_target_pairs={{0,6},{1,7},{2,4},{3,5},{4,2},{5,3},{6,0},{7,1},{8,14},{9,15},{10,... | collective-permute-start | bytes 393224 | tf_op jit(solution)/shard_map/ppermute | solution.py:29
  33.0 7.0 %collective-permute-start.12 = (bf16[128,512]{1,0:T(8,128)(2,1)S(1)}, bf16[128,512]{1,0:T(8,128)(2,1)S(1)}, u32[]{:S(2)}, u32[]{:S(2)}) collective-permute-start(bf16[128,512]{1,0:T(8,128)(2,1)S(1)} %shard_map.63.refs_4_.refs_7_), channel_id=1, source_target_pairs={{0,4},{1,3},{2,6},{3,1},{4,0},{5,7},{6,2},{7,5},{8,12},{9,11},{10,... | collective-permute-start | bytes 393224 | tf_op jit(solution)/shard_map/ppermute | solution.py:29
  34.2 5.9 %collective-permute-start.11 = (bf16[128,512]{1,0:T(8,128)(2,1)S(1)}, bf16[128,512]{1,0:T(8,128)(2,1)S(1)}, u32[]{:S(2)}, u32[]{:S(2)}) collective-permute-start(bf16[128,512]{1,0:T(8,128)(2,1)S(1)} %shard_map.63.refs_4_.refs_7_), channel_id=1, source_target_pairs={{0,2},{1,5},{2,0},{3,7},{4,6},{5,1},{6,4},{7,3},{8,10},{9,13},{10,... | collective-permute-start | bytes 393224 | tf_op jit(solution)/shard_map/ppermute | solution.py:29
  40.7 1.3 %collective-permute-start.14 = (bf16[64,512]{1,0:T(8,128)(2,1)S(1)}, bf16[64,512]{1,0:T(8,128)(2,1)S(1)}, u32[]{:S(2)}, u32[]{:S(2)}) collective-permute-start(bf16[64,512]{1,0:T(8,128)(2,1)S(1)} %get-tuple-element.50), channel_id=1, source_target_pairs={{0,1},{1,0},{2,3},{3,2},{4,5},{5,4},{6,7},{7,6},{8,9},{9,8},{10,11... | collective-permute-start | bytes 196616 | tf_op jit(solution)/shard_map/ppermute | solution.py:29

commit v9 on v7

--- a/solution.py
+++ b/solution.py
@@ -241,7 +241,15 @@
         )
     base_ref[...] = near
     base_meta_ref[...] = meta_of(counts)
-    for send, sums, row in ((next_ref, middle, counts), (far_ref, far, far_counts)):
+    next_counts = counts
+    if four:
+        swapped = lax.axis_index("mp") % 2 == 0
+        middle, far = jnp.where(swapped, far, middle), jnp.where(swapped, middle, far)
+        next_counts, far_counts = (
+            jnp.where(swapped, far_counts, counts),
+            jnp.where(swapped, counts, far_counts),
+        )
+    for send, sums, row in ((next_ref, middle, next_counts), (far_ref, far, far_counts)):
         send[:cent] = sums.astype(BF16)
         send[cent:, : 2 * LANES] = meta_of(row).astype(BF16)
         send[cent:, 2 * LANES :] = jnp.zeros((META, send.shape[1] - 2 * LANES), BF16)
@@ -264,9 +272,15 @@
     )(got[2], got[0], got[1], own, own_meta)
 
 
-def mean_kernel(cent, two, one, base, base_meta, mean_ref, send_ref):
+def mean_kernel(cent, four, two, one, base, base_meta, mean_ref, send_ref):
     sums = base[...] + one[:cent].astype(F32) + two[:cent].astype(F32)
     metas = [meta[...].astype(F32) for meta in (base_meta, one.at[cent:], two.at[cent:])]
+    if four:
+        swapped = lax.axis_index("mp") % 2 == 0
+        metas[1:] = [
+            jnp.where(swapped, metas[2], metas[1]),
+            jnp.where(swapped, metas[1], metas[2]),
+        ]
     rows = [meta[0:1, :LANES] * BASE + meta[1:2, :LANES] for meta in metas]
     row = rows[0] + pltpu.roll(rows[1], LANES - cent, 1) + rows[2]
     mean = (sums / as_column(row, cent)).astype(BF16)
@@ -279,11 +293,11 @@
     send_ref[cent:, known:] = jnp.zeros((META, mean.shape[1] - known), BF16)
 
 
-def means(cent, base, base_meta, got):
+def means(cent, four, base, base_meta, got):
     width = base.shape[1]
     mean = jax.ShapeDtypeStruct((cent, width), BF16)
     return pl.pallas_call(
-        functools.partial(mean_kernel, cent),
+        functools.partial(mean_kernel, cent, four),
         in_specs=[whole()] * 4,
         out_specs=[whole()] * 2,
         out_shape=[mean, jax.ShapeDtypeStruct((cent + META, width), BF16)],
@@ -530,10 +544,11 @@
     four = devices == GROUP * GROUP and cores == 2 and devices * cent <= K2
     base, base_meta, following, far = group_sums(cent, four, own, own_meta, got)
     if four:
-        got = [partner(following, GROUP), partner(far, 2 * GROUP)]
+        turns = ((2 * GROUP, GROUP), (GROUP, 2 * GROUP))
+        got = [sideways(following, turns[0]), sideways(far, turns[1])]
     else:
         got = [ahead(following, GROUP), ahead(far, 2 * GROUP)]
-    mean, send = means(cent, base, base_meta, got)
+    mean, send = means(cent, four, base, base_meta, got)
     if not four:
         return (mean, *summed_scores(devices, second_level, mean))
 

time: 42.1 us -> 43 us (1.021)
  starting transfers between devices: 20.9 us -> 22.7 us
  waiting for transfers between devices: 12.3 us -> 11.4 us
    ppermute x15, starting transfers between devices: 20.9 us -> 22.7 us  [exchanged(): return lax.ppermute(value, ('dp', 'mp'), pairs)]
    ppermute x15, waiting for transfers between devices: 12.3 us -> 11.4 us  [exchanged(): return lax.ppermute(value, ('dp', 'mp'), pairs)]
  transfers between devices with their start and end apart: 15 -> 15, of which waited for: 12 -> 8; matrix products, arithmetic and copies ran while one was open for 0% -> 0% of each run, Pallas kernels for 9% -> 9%
where the time goes in v9:
time: 43 us; the launch traced here: 42.7 us
  starting transfers between devices  22.7 us (53%)
  waiting for transfers between devices  11.4 us (27%)
  Pallas kernels  7.2 us (17%)
  between operations  0.72 us (2%)
  other arithmetic  0.67 us (2%)
    ppermute x15, starting transfers between devices, exchanged(): return lax.ppermute(value, ('dp', 'mp'), pairs)  22.7 us
    ppermute x15, waiting for transfers between devices, exchanged(): return lax.ppermute(value, ('dp', 'mp'), pairs)  11.4 us
    pallas_call x1, Pallas kernels, band_sums(): pl.pallas_call(functools.partial(first_kernel, devices, cent, chunks), in...  2.43 us
    pallas_call x1, Pallas kernels, gathered_sums(): pl.pallas_call(functools.partial(gather_kernel, picks), in_specs=[whole()...  1.58 us
    pallas_call x1, Pallas kernels, kept_scores(): pl.pallas_call(functools.partial(keep_kernel, owned, picks), in_specs=[wh...  1.1 us
    pallas_call x1, Pallas kernels, band_sums(): pl.pallas_call(functools.partial(second_kernel, cent, [(0, half), (half,...  1.01 us
  transfers between devices with their start and end apart: 15, of which 8 were waited for; matrix products, arithmetic and copies ran while one was open for 0% of the time, Pallas kernels for 9%

profile of v9, /device:TPU:0, one launch (start us, length us, event | category | flops | bytes accessed | tf_op | source)
XLA Modules:
  0.0 42.7 jit_solution(8236260469196916855)
XLA Ops:
  0.6 2.4 %shard_map.58 = (bf16[136,512]{1,0:T(8,128)(2,1)S(1)}, bf16[136,512]{1,0:T(8,128)(2,1)S(1)}, bf16[3072,512]{1,0:T(8,128)(2,1)S(1)}, s32[1,3072]{1,0:T(1,128)S(1)}, f32[2,64]{1,0:T(2,128)S(1)}) custom-call(s32[1,3072]{1,0:T(1,128)} %bitcast.2, bf16[3072,512]{1,0:T(8,128)(2,1)} %rows_hbm.1, s32[1,64]{1,0:T(1,128)} %bitcast.3), custom_call_target="tpu_custom_call" | custom-call | tf_op jit(solution)/shard_map/pallas_call | solution.py:158
  3.1 4.0 %collective-permute-start = (bf16[136,512]{1,0:T(8,128)(2,1)S(1)}, bf16[136,512]{1,0:T(8,128)(2,1)S(1)}, u32[]{:S(2)}, u32[]{:S(2)}) collective-permute-start(bf16[136,512]{1,0:T(8,128)(2,1)S(1)} %get-tuple-element.27), channel_id=1, source_target_pairs={{0,6},{1,7},{2,4},{3,5},{4,2},{5,3},{6,0},{7,1},{8,14},{9,15},{10,... | collective-permute-start | bytes 417800 | tf_op jit(solution)/shard_map/ppermute | solution.py:29
  7.0 0.5 %collective-permute-start.1 = (bf16[136,512]{1,0:T(8,128)(2,1)S(1)}, bf16[136,512]{1,0:T(8,128)(2,1)S(1)}, u32[]{:S(2)}, u32[]{:S(2)}) collective-permute-start(bf16[136,512]{1,0:T(8,128)(2,1)S(1)} %get-tuple-element.28), channel_id=1, source_target_pairs={{0,2},{1,5},{2,0},{3,7},{4,6},{5,1},{6,4},{7,3},{8,10},{9,13},{10,... | collective-permute-start | bytes 417800 | tf_op jit(solution)/shard_map/ppermute | solution.py:29
  7.6 1.0 %shard_map.59 = (bf16[136,512]{1,0:T(8,128)(2,1)S(1)}, f32[128,512]{1,0:T(8,128)S(1)}, f32[8,256]{1,0:T(8,128)S(1)}) custom-call(s32[1,3072]{1,0:T(1,128)S(1)} %get-tuple-element.29.label_ref, bf16[3072,512]{1,0:T(8,128)(2,1)S(1)} %get-tuple-element.30.rows_ref, f32[2,64]{1,0:T(2,128)S(1)} %get-tuple-element.31.digits_ref), custom_call_target="tpu_custom_call" | custom-call | flops 99999997952 | bytes 300000000 | tf_op jit(solution)/shard_map/pallas_call | solution.py:181
  8.7 2.4 %collective-permute-done.three = bf16[136,512]{1,0:T(8,128)(2,1)S(1)} collective-permute-done((bf16[136,512]{1,0:T(8,128)(2,1)S(1)}, bf16[136,512]{1,0:T(8,128)(2,1)S(1)}, u32[]{:S(2)}, u32[]{:S(2)}) %collective-permute-start) | collective-permute-done | bytes 139296 | tf_op jit(solution)/shard_map/ppermute | solution.py:29
  11.1 2.9 %collective-permute-done.1.one = bf16[136,512]{1,0:T(8,128)(2,1)S(1)} collective-permute-done((bf16[136,512]{1,0:T(8,128)(2,1)S(1)}, bf16[136,512]{1,0:T(8,128)(2,1)S(1)}, u32[]{:S(2)}, u32[]{:S(2)}) %collective-permute-start.1) | collective-permute-done | bytes 139296 | tf_op jit(solution)/shard_map/ppermute | solution.py:29
  14.1 1.6 %collective-permute-start.3 = (bf16[72,512]{1,0:T(8,128)(2,1)S(1)}, bf16[72,512]{1,0:T(8,128)(2,1)S(1)}, u32[]{:S(2)}, u32[]{:S(2)}) collective-permute-start(bf16[72,512]{1,0:T(8,128)(2,1)S(1)} %get-tuple-element.35), channel_id=1, source_target_pairs={{0,8},{1,17},{2,10},{3,19},{4,12},{5,21},{6,14},{7,23},{8,0},{9,25... | collective-permute-start | bytes 221192 | tf_op jit(solution)/shard_map/ppermute | solution.py:29
  15.8 2.6 %collective-permute-start.4 = (bf16[72,512]{1,0:T(8,128)(2,1)S(1)}, bf16[72,512]{1,0:T(8,128)(2,1)S(1)}, u32[]{:S(2)}, u32[]{:S(2)}) collective-permute-start(bf16[72,512]{1,0:T(8,128)(2,1)S(1)} %get-tuple-element.36), channel_id=1, source_target_pairs={{0,16},{1,9},{2,18},{3,11},{4,20},{5,13},{6,22},{7,15},{8,24},{9,1... | collective-permute-start | bytes 221192 | tf_op jit(solution)/shard_map/ppermute | solution.py:29
  18.4 0.7 %collective-permute-done.3.two = bf16[72,512]{1,0:T(8,128)(2,1)S(1)} collective-permute-done((bf16[72,512]{1,0:T(8,128)(2,1)S(1)}, bf16[72,512]{1,0:T(8,128)(2,1)S(1)}, u32[]{:S(2)}, u32[]{:S(2)}) %collective-permute-start.3) | collective-permute-done | bytes 73760 | tf_op jit(solution)/shard_map/ppermute | solution.py:29
  19.1 2.7 %collective-permute-done.4.one = bf16[72,512]{1,0:T(8,128)(2,1)S(1)} collective-permute-done((bf16[72,512]{1,0:T(8,128)(2,1)S(1)}, bf16[72,512]{1,0:T(8,128)(2,1)S(1)}, u32[]{:S(2)}, u32[]{:S(2)}) %collective-permute-start.4) | collective-permute-done | bytes 73760 | tf_op jit(solution)/shard_map/ppermute | solution.py:29
  22.4 2.0 %collective-permute-start.10 = (bf16[64,512]{1,0:T(8,128)(2,1)S(1)}, bf16[64,512]{1,0:T(8,128)(2,1)S(1)}, u32[]{:S(2)}, u32[]{:S(2)}) collective-permute-start(bf16[64,512]{1,0:T(8,128)(2,1)S(1)} %get-tuple-element.41.refs_6_), channel_id=1, source_target_pairs={{0,16},{1,17},{2,18},{3,19},{4,20},{5,21},{6,22},{7,23},{8,24},{9,... | collective-permute-start | bytes 196616 | tf_op jit(solution)/shard_map/ppermute | solution.py:29
  24.4 2.0 %collective-permute-start.9 = (bf16[64,512]{1,0:T(8,128)(2,1)S(1)}, bf16[64,512]{1,0:T(8,128)(2,1)S(1)}, u32[]{:S(2)}, u32[]{:S(2)}) collective-permute-start(bf16[64,512]{1,0:T(8,128)(2,1)S(1)} %get-tuple-element.41.refs_6_), channel_id=1, source_target_pairs={{0,24},{1,25},{2,26},{3,27},{4,28},{5,29},{6,30},{7,31},{8,16},{9,... | collective-permute-start | bytes 196616 | tf_op jit(solution)/shard_map/ppermute | solution.py:29
  26.5 0.5 %collective-permute-done.5.got = bf16[72,512]{1,0:T(8,128)(2,1)S(1)} collective-permute-done((bf16[72,512]{1,0:T(8,128)(2,1)S(1)}, bf16[72,512]{1,0:T(8,128)(2,1)S(1)}, u32[]{:S(2)}, u32[]{:S(2)}) %collective-permute-start.5) | collective-permute-done | bytes 73760 | tf_op jit(solution)/shard_map/ppermute | solution.py:29
  27.1 1.6 %collective-permute-start.8 = (bf16[128,512]{1,0:T(8,128)(2,1)S(1)}, bf16[128,512]{1,0:T(8,128)(2,1)S(1)}, u32[]{:S(2)}, u32[]{:S(2)}) collective-permute-start(bf16[128,512]{1,0:T(8,128)(2,1)S(1)} %get-tuple-element.40.refs_0_), channel_id=1, source_target_pairs={{0,6},{1,7},{2,4},{3,5},{4,2},{5,3},{6,0},{7,1},{8,14},{9,15},{10,... | collective-permute-start | bytes 393224 | tf_op jit(solution)/shard_map/ppermute | solution.py:29
  28.7 2.3 %collective-permute-start.7 = (bf16[128,512]{1,0:T(8,128)(2,1)S(1)}, bf16[128,512]{1,0:T(8,128)(2,1)S(1)}, u32[]{:S(2)}, u32[]{:S(2)}) collective-permute-start(bf16[128,512]{1,0:T(8,128)(2,1)S(1)} %get-tuple-element.40.refs_0_), channel_id=1, source_target_pairs={{0,4},{1,3},{2,6},{3,1},{4,0},{5,7},{6,2},{7,5},{8,12},{9,11},{10,... | collective-permute-start | bytes 393224 | tf_op jit(solution)/shard_map/ppermute | solution.py:29
  31.0 1.5 %collective-permute-start.13 = (bf16[128,512]{1,0:T(8,128)(2,1)S(1)}, bf16[128,512]{1,0:T(8,128)(2,1)S(1)}, u32[]{:S(2)}, u32[]{:S(2)}) collective-permute-start(bf16[128,512]{1,0:T(8,128)(2,1)S(1)} %shard_map.63.refs_4_.refs_7_), channel_id=1, source_target_pairs={{0,6},{1,7},{2,4},{3,5},{4,2},{5,3},{6,0},{7,1},{8,14},{9,15},{10,... | collective-permute-start | bytes 393224 | tf_op jit(solution)/shard_map/ppermute | solution.py:29
  32.5 2.0 %collective-permute-start.12 = (bf16[128,512]{1,0:T(8,128)(2,1)S(1)}, bf16[128,512]{1,0:T(8,128)(2,1)S(1)}, u32[]{:S(2)}, u32[]{:S(2)}) collective-permute-start(bf16[128,512]{1,0:T(8,128)(2,1)S(1)} %shard_map.63.refs_4_.refs_7_), channel_id=1, source_target_pairs={{0,4},{1,3},{2,6},{3,1},{4,0},{5,7},{6,2},{7,5},{8,12},{9,11},{10,... | collective-permute-start | bytes 393224 | tf_op jit(solution)/shard_map/ppermute | solution.py:29
  34.5 1.8 %collective-permute-start.11 = (bf16[128,512]{1,0:T(8,128)(2,1)S(1)}, bf16[128,512]{1,0:T(8,128)(2,1)S(1)}, u32[]{:S(2)}, u32[]{:S(2)}) collective-permute-start(bf16[128,512]{1,0:T(8,128)(2,1)S(1)} %shard_map.63.refs_4_.refs_7_), channel_id=1, source_target_pairs={{0,2},{1,5},{2,0},{3,7},{4,6},{5,1},{6,4},{7,3},{8,10},{9,13},{10,... | collective-permute-start | bytes 393224 | tf_op jit(solution)/shard_map/ppermute | solution.py:29
  36.4 0.9 %collective-permute-done.7.refs_2_ = bf16[128,512]{1,0:T(8,128)(2,1)S(1)} collective-permute-done((bf16[128,512]{1,0:T(8,128)(2,1)S(1)}, bf16[128,512]{1,0:T(8,128)(2,1)S(1)}, u32[]{:S(2)}, u32[]{:S(2)}) %collective-permute-start.7) | collective-permute-done | bytes 131104 | tf_op jit(solution)/shard_map/ppermute | solution.py:29
  37.2 1.6 %shard_map.64 = (f32[1024,512]{1,0:T(8,128)S(1)}, f32[1024,128]{1,0:T(8,128)S(1)}, bf16[64,512]{1,0:T(8,128)(2,1)S(1)}, bf16[64,512]{1,0:T(8,128)(2,1)}) custom-call(bf16[128,512]{1,0:T(8,128)(2,1)S(1)} %get-tuple-element.40.refs_0_, bf16[128,512]{1,0:T(8,128)(2,1)S(1)} %collective-permute-done.6.refs_1_, ...), custom_call_target="tpu_custom_call" | custom-call | tf_op jit(solution)/shard_map/pallas_call | solution.py:405
  38.8 1.2 %collective-permute-done.12.refs_1_ = bf16[128,512]{1,0:T(8,128)(2,1)S(1)} collective-permute-done((bf16[128,512]{1,0:T(8,128)(2,1)S(1)}, bf16[128,512]{1,0:T(8,128)(2,1)S(1)}, u32[]{:S(2)}, u32[]{:S(2)}) %collective-permute-start.12) | collective-permute-done | bytes 131104 | tf_op jit(solution)/shard_map/ppermute | solution.py:29
  40.1 0.6 %shard_map.65 = (bf16[512,512]{1,0:T(8,128)(2,1)S(1)}, bf16[64,512]{1,0:T(8,128)(2,1)S(1)}) custom-call(bf16[128,512]{1,0:T(8,128)(2,1)S(1)} %collective-permute-done.11.refs_0_, bf16[128,512]{1,0:T(8,128)(2,1)S(1)} %collective-permute-done.12.refs_1_, bf16[128,512]{1,0:T(8,128)(2,1)S(1)} %collective-permute-done.13.refs_2_, ...), custom_call_target="tpu_custom_call" | custom-call | tf_op jit(solution)/shard_map/pallas_call | solution.py:453
  40.8 1.1 %shard_map.66 = (bf16[64,512]{1,0:T(8,128)(2,1)}, f32[64,512]{1,0:T(8,128)S(1)}) custom-call(bf16[128,512]{1,0:T(8,128)(2,1)S(1)} %collective-permute-done.11.refs_0_, bf16[128,512]{1,0:T(8,128)(2,1)S(1)} %collective-permute-done.12.refs_1_, bf16[128,512]{1,0:T(8,128)(2,1)S(1)} %collective-permute-done.13.refs_2_, ...), custom_call_target="tpu_custom_call" | custom-call | tf_op jit(solution)/shard_map/pallas_call | solution.py:484
  42.1 0.7 %convert_add_fusion = f32[64,512]{1,0:T(8,128)} fusion(f32[64,512]{1,0:T(8,128)S(1)} %get-tuple-element.49, bf16[64,512]{1,0:T(8,128)(2,1)S(1)} %collective-permute-done.14), kind=kLoop, calls=%fused_computation | loop fusion | flops 65536 | bytes 327680 | tf_op jit(solution)/shard_map/add | solution.py:569
  (16 shorter events, 1.3 us)
Async XLA Ops:
  3.1 8.0 %collective-permute-start = (bf16[136,512]{1,0:T(8,128)(2,1)S(1)}, bf16[136,512]{1,0:T(8,128)(2,1)S(1)}, u32[]{:S(2)}, u32[]{:S(2)}) collective-permute-start(bf16[136,512]{1,0:T(8,128)(2,1)S(1)} %get-tuple-element.27), channel_id=1, source_target_pairs={{0,6},{1,7},{2,4},{3,5},{4,2},{5,3},{6,0},{7,1},{8,14},{9,15},{10,... | collective-permute-start | bytes 417800 | tf_op jit(solution)/shard_map/ppermute | solution.py:29
  7.0 7.0 %collective-permute-start.1 = (bf16[136,512]{1,0:T(8,128)(2,1)S(1)}, bf16[136,512]{1,0:T(8,128)(2,1)S(1)}, u32[]{:S(2)}, u32[]{:S(2)}) collective-permute-start(bf16[136,512]{1,0:T(8,128)(2,1)S(1)} %get-tuple-element.28), channel_id=1, source_target_pairs={{0,2},{1,5},{2,0},{3,7},{4,6},{5,1},{6,4},{7,3},{8,10},{9,13},{10,... | collective-permute-start | bytes 417800 | tf_op jit(solution)/shard_map/ppermute | solution.py:29
  8.6 5.4 %collective-permute-start.2 = (bf16[136,512]{1,0:T(8,128)(2,1)S(1)}, bf16[136,512]{1,0:T(8,128)(2,1)S(1)}, u32[]{:S(2)}, u32[]{:S(2)}) collective-permute-start(bf16[136,512]{1,0:T(8,128)(2,1)S(1)} %get-tuple-element.32), channel_id=1, source_target_pairs={{0,4},{1,3},{2,6},{3,1},{4,0},{5,7},{6,2},{7,5},{8,12},{9,11},{10,... | collective-permute-start | bytes 417800 | tf_op jit(solution)/shard_map/ppermute | solution.py:29
  14.1 5.0 %collective-permute-start.3 = (bf16[72,512]{1,0:T(8,128)(2,1)S(1)}, bf16[72,512]{1,0:T(8,128)(2,1)S(1)}, u32[]{:S(2)}, u32[]{:S(2)}) collective-permute-start(bf16[72,512]{1,0:T(8,128)(2,1)S(1)} %get-tuple-element.35), channel_id=1, source_target_pairs={{0,8},{1,17},{2,10},{3,19},{4,12},{5,21},{6,14},{7,23},{8,0},{9,25... | collective-permute-start | bytes 221192 | tf_op jit(solution)/shard_map/ppermute | solution.py:29
  15.8 6.0 %collective-permute-start.4 = (bf16[72,512]{1,0:T(8,128)(2,1)S(1)}, bf16[72,512]{1,0:T(8,128)(2,1)S(1)}, u32[]{:S(2)}, u32[]{:S(2)}) collective-permute-start(bf16[72,512]{1,0:T(8,128)(2,1)S(1)} %get-tuple-element.36), channel_id=1, source_target_pairs={{0,16},{1,9},{2,18},{3,11},{4,20},{5,13},{6,22},{7,15},{8,24},{9,1... | collective-permute-start | bytes 221192 | tf_op jit(solution)/shard_map/ppermute | solution.py:29
  22.0 5.0 %collective-permute-start.5 = (bf16[72,512]{1,0:T(8,128)(2,1)S(1)}, bf16[72,512]{1,0:T(8,128)(2,1)S(1)}, u32[]{:S(2)}, u32[]{:S(2)}) collective-permute-start(bf16[72,512]{1,0:T(8,128)(2,1)S(1)} %get-tuple-element.39.own), channel_id=1, source_target_pairs={{0,8},{1,9},{2,10},{3,11},{4,12},{5,13},{6,14},{7,15},{8,0},{9,1},... | collective-permute-start | bytes 221192 | tf_op jit(solution)/shard_map/ppermute | solution.py:29
  22.4 8.5 %collective-permute-start.10 = (bf16[64,512]{1,0:T(8,128)(2,1)S(1)}, bf16[64,512]{1,0:T(8,128)(2,1)S(1)}, u32[]{:S(2)}, u32[]{:S(2)}) collective-permute-start(bf16[64,512]{1,0:T(8,128)(2,1)S(1)} %get-tuple-element.41.refs_6_), channel_id=1, source_target_pairs={{0,16},{1,17},{2,18},{3,19},{4,20},{5,21},{6,22},{7,23},{8,24},{9,... | collective-permute-start | bytes 196616 | tf_op jit(solution)/shard_map/ppermute | solution.py:29
  24.4 6.5 %collective-permute-start.9 = (bf16[64,512]{1,0:T(8,128)(2,1)S(1)}, bf16[64,512]{1,0:T(8,128)(2,1)S(1)}, u32[]{:S(2)}, u32[]{:S(2)}) collective-permute-start(bf16[64,512]{1,0:T(8,128)(2,1)S(1)} %get-tuple-element.41.refs_6_), channel_id=1, source_target_pairs={{0,24},{1,25},{2,26},{3,27},{4,28},{5,29},{6,30},{7,31},{8,16},{9,... | collective-permute-start | bytes 196616 | tf_op jit(solution)/shard_map/ppermute | solution.py:29
  27.1 7.4 %collective-permute-start.8 = (bf16[128,512]{1,0:T(8,128)(2,1)S(1)}, bf16[128,512]{1,0:T(8,128)(2,1)S(1)}, u32[]{:S(2)}, u32[]{:S(2)}) collective-permute-start(bf16[128,512]{1,0:T(8,128)(2,1)S(1)} %get-tuple-element.40.refs_0_), channel_id=1, source_target_pairs={{0,6},{1,7},{2,4},{3,5},{4,2},{5,3},{6,0},{7,1},{8,14},{9,15},{10,... | collective-permute-start | bytes 393224 | tf_op jit(solution)/shard_map/ppermute | solution.py:29
  28.7 8.6 %collective-permute-start.7 = (bf16[128,512]{1,0:T(8,128)(2,1)S(1)}, bf16[128,512]{1,0:T(8,128)(2,1)S(1)}, u32[]{:S(2)}, u32[]{:S(2)}) collective-permute-start(bf16[128,512]{1,0:T(8,128)(2,1)S(1)} %get-tuple-element.40.refs_0_), channel_id=1, source_target_pairs={{0,4},{1,3},{2,6},{3,1},{4,0},{5,7},{6,2},{7,5},{8,12},{9,11},{10,... | collective-permute-start | bytes 393224 | tf_op jit(solution)/shard_map/ppermute | solution.py:29
  31.0 6.3 %collective-permute-start.6 = (bf16[128,512]{1,0:T(8,128)(2,1)S(1)}, bf16[128,512]{1,0:T(8,128)(2,1)S(1)}, u32[]{:S(2)}, u32[]{:S(2)}) collective-permute-start(bf16[128,512]{1,0:T(8,128)(2,1)S(1)} %get-tuple-element.40.refs_0_), channel_id=1, source_target_pairs={{0,2},{1,5},{2,0},{3,7},{4,6},{5,1},{6,4},{7,3},{8,10},{9,13},{10,... | collective-permute-start | bytes 393224 | tf_op jit(solution)/shard_map/ppermute | solution.py:29
  31.0 7.8 %collective-permute-start.13 = (bf16[128,512]{1,0:T(8,128)(2,1)S(1)}, bf16[128,512]{1,0:T(8,128)(2,1)S(1)}, u32[]{:S(2)}, u32[]{:S(2)}) collective-permute-start(bf16[128,512]{1,0:T(8,128)(2,1)S(1)} %shard_map.63.refs_4_.refs_7_), channel_id=1, source_target_pairs={{0,6},{1,7},{2,4},{3,5},{4,2},{5,3},{6,0},{7,1},{8,14},{9,15},{10,... | collective-permute-start | bytes 393224 | tf_op jit(solution)/shard_map/ppermute | solution.py:29
  32.5 7.5 %collective-permute-start.12 = (bf16[128,512]{1,0:T(8,128)(2,1)S(1)}, bf16[128,512]{1,0:T(8,128)(2,1)S(1)}, u32[]{:S(2)}, u32[]{:S(2)}) collective-permute-start(bf16[128,512]{1,0:T(8,128)(2,1)S(1)} %shard_map.63.refs_4_.refs_7_), channel_id=1, source_target_pairs={{0,4},{1,3},{2,6},{3,1},{4,0},{5,7},{6,2},{7,5},{8,12},{9,11},{10,... | collective-permute-start | bytes 393224 | tf_op jit(solution)/shard_map/ppermute | solution.py:29
  34.5 5.5 %collective-permute-start.11 = (bf16[128,512]{1,0:T(8,128)(2,1)S(1)}, bf16[128,512]{1,0:T(8,128)(2,1)S(1)}, u32[]{:S(2)}, u32[]{:S(2)}) collective-permute-start(bf16[128,512]{1,0:T(8,128)(2,1)S(1)} %shard_map.63.refs_4_.refs_7_), channel_id=1, source_target_pairs={{0,2},{1,5},{2,0},{3,7},{4,6},{5,1},{6,4},{7,3},{8,10},{9,13},{10,... | collective-permute-start | bytes 393224 | tf_op jit(solution)/shard_map/ppermute | solution.py:29
  40.7 1.3 %collective-permute-start.14 = (bf16[64,512]{1,0:T(8,128)(2,1)S(1)}, bf16[64,512]{1,0:T(8,128)(2,1)S(1)}, u32[]{:S(2)}, u32[]{:S(2)}) collective-permute-start(bf16[64,512]{1,0:T(8,128)(2,1)S(1)} %get-tuple-element.50), channel_id=1, source_target_pairs={{0,1},{1,0},{2,3},{3,2},{4,5},{5,4},{6,7},{7,6},{8,9},{9,8},{10,11... | collective-permute-start | bytes 196616 | tf_op jit(solution)/shard_map/ppermute | solution.py:29

commit v10 on v7

--- a/solution.py
+++ b/solution.py
@@ -151,7 +151,7 @@
     count, width = rows.shape
     pair = 2 * cent
     send = jax.ShapeDtypeStruct((pair + META, width), BF16)
-    edges = [count * part // 12 for part in (0, 3, 6, 9, 12)]
+    edges = [count * part // 12 for part in (0, 2, 4, 6, 8, 10, 12)]
     chunks = list(zip(edges[:-1], edges[1:]))
     half = count // 2
     hbm = pl.BlockSpec(memory_space=pltpu.HBM)

time: 42.1 us -> 42.1 us (level)
  transfers between devices with their start and end apart: 15 -> 15, of which waited for: 12 -> 11; matrix products, arithmetic and copies ran while one was open for 0% -> 0% of each run, Pallas kernels for 9% -> 9%
where the time goes in v10:
time: 42.1 us; the launch traced here: 41.9 us
  starting transfers between devices  20.9 us (50%)
  waiting for transfers between devices  12.3 us (29%)
  Pallas kernels  7.22 us (17%)
  between operations  0.71 us (2%)
  other arithmetic  0.67 us (2%)
    ppermute x15, starting transfers between devices, exchanged(): return lax.ppermute(value, ('dp', 'mp'), pairs)  20.9 us
    ppermute x15, waiting for transfers between devices, exchanged(): return lax.ppermute(value, ('dp', 'mp'), pairs)  12.3 us
    pallas_call x1, Pallas kernels, band_sums(): pl.pallas_call(functools.partial(first_kernel, devices, cent, chunks), in...  2.46 us
    pallas_call x1, Pallas kernels, gathered_sums(): pl.pallas_call(functools.partial(gather_kernel, picks), in_specs=[whole()...  1.58 us
    pallas_call x1, Pallas kernels, kept_scores(): pl.pallas_call(functools.partial(keep_kernel, owned, picks), in_specs=[wh...  1.1 us
    pallas_call x1, Pallas kernels, band_sums(): pl.pallas_call(functools.partial(second_kernel, cent, [(0, half), (half,...  1.01 us
  transfers between devices with their start and end apart: 15, of which 11 were waited for; matrix products, arithmetic and copies ran while one was open for 0% of the time, Pallas kernels for 9%

profile of v10, /device:TPU:0, one launch (start us, length us, event | category | flops | bytes accessed | tf_op | source)
XLA Modules:
  0.0 41.9 jit_solution(13733566970920243593)
XLA Ops:
  0.6 2.5 %shard_map.58 = (bf16[136,512]{1,0:T(8,128)(2,1)S(1)}, bf16[136,512]{1,0:T(8,128)(2,1)S(1)}, bf16[3072,512]{1,0:T(8,128)(2,1)S(1)}, s32[1,3072]{1,0:T(1,128)S(1)}, f32[2,64]{1,0:T(2,128)S(1)}) custom-call(s32[1,3072]{1,0:T(1,128)} %bitcast.2, bf16[3072,512]{1,0:T(8,128)(2,1)} %rows_hbm.1, s32[1,64]{1,0:T(1,128)} %bitcast.3), custom_call_target="tpu_custom_call" | custom-call | tf_op jit(solution)/shard_map/pallas_call | solution.py:158
  3.1 4.0 %collective-permute-start = (bf16[136,512]{1,0:T(8,128)(2,1)S(1)}, bf16[136,512]{1,0:T(8,128)(2,1)S(1)}, u32[]{:S(2)}, u32[]{:S(2)}) collective-permute-start(bf16[136,512]{1,0:T(8,128)(2,1)S(1)} %get-tuple-element.27), channel_id=1, source_target_pairs={{0,6},{1,7},{2,4},{3,5},{4,2},{5,3},{6,0},{7,1},{8,14},{9,15},{10,... | collective-permute-start | bytes 417800 | tf_op jit(solution)/shard_map/ppermute | solution.py:29
  7.6 1.0 %shard_map.59 = (bf16[136,512]{1,0:T(8,128)(2,1)S(1)}, f32[128,512]{1,0:T(8,128)S(1)}, f32[8,256]{1,0:T(8,128)S(1)}) custom-call(s32[1,3072]{1,0:T(1,128)S(1)} %get-tuple-element.29.label_ref, bf16[3072,512]{1,0:T(8,128)(2,1)S(1)} %get-tuple-element.30.rows_ref, f32[2,64]{1,0:T(2,128)S(1)} %get-tuple-element.31.digits_ref), custom_call_target="tpu_custom_call" | custom-call | flops 99999997952 | bytes 300000000 | tf_op jit(solution)/shard_map/pallas_call | solution.py:181
  8.8 2.4 %collective-permute-done.three = bf16[136,512]{1,0:T(8,128)(2,1)S(1)} collective-permute-done((bf16[136,512]{1,0:T(8,128)(2,1)S(1)}, bf16[136,512]{1,0:T(8,128)(2,1)S(1)}, u32[]{:S(2)}, u32[]{:S(2)}) %collective-permute-start) | collective-permute-done | bytes 139296 | tf_op jit(solution)/shard_map/ppermute | solution.py:29
  11.1 2.9 %collective-permute-done.1.one = bf16[136,512]{1,0:T(8,128)(2,1)S(1)} collective-permute-done((bf16[136,512]{1,0:T(8,128)(2,1)S(1)}, bf16[136,512]{1,0:T(8,128)(2,1)S(1)}, u32[]{:S(2)}, u32[]{:S(2)}) %collective-permute-start.1) | collective-permute-done | bytes 139296 | tf_op jit(solution)/shard_map/ppermute | solution.py:29
  14.2 2.7 %collective-permute-start.3 = (bf16[72,512]{1,0:T(8,128)(2,1)S(1)}, bf16[72,512]{1,0:T(8,128)(2,1)S(1)}, u32[]{:S(2)}, u32[]{:S(2)}) collective-permute-start(bf16[72,512]{1,0:T(8,128)(2,1)S(1)} %get-tuple-element.35), channel_id=1, source_target_pairs={{0,16},{1,17},{2,18},{3,19},{4,20},{5,21},{6,22},{7,23},{8,24},{9,... | collective-permute-start | bytes 221192 | tf_op jit(solution)/shard_map/ppermute | solution.py:29
  16.8 1.6 %collective-permute-start.4 = (bf16[72,512]{1,0:T(8,128)(2,1)S(1)}, bf16[72,512]{1,0:T(8,128)(2,1)S(1)}, u32[]{:S(2)}, u32[]{:S(2)}) collective-permute-start(bf16[72,512]{1,0:T(8,128)(2,1)S(1)} %get-tuple-element.36), channel_id=1, source_target_pairs={{0,8},{1,9},{2,10},{3,11},{4,12},{5,13},{6,14},{7,15},{8,0},{9,1},... | collective-permute-start | bytes 221192 | tf_op jit(solution)/shard_map/ppermute | solution.py:29
  18.4 1.8 %collective-permute-done.3.two = bf16[72,512]{1,0:T(8,128)(2,1)S(1)} collective-permute-done((bf16[72,512]{1,0:T(8,128)(2,1)S(1)}, bf16[72,512]{1,0:T(8,128)(2,1)S(1)}, u32[]{:S(2)}, u32[]{:S(2)}) %collective-permute-start.3) | collective-permute-done | bytes 73760 | tf_op jit(solution)/shard_map/ppermute | solution.py:29
  20.2 1.0 %collective-permute-done.4.one = bf16[72,512]{1,0:T(8,128)(2,1)S(1)} collective-permute-done((bf16[72,512]{1,0:T(8,128)(2,1)S(1)}, bf16[72,512]{1,0:T(8,128)(2,1)S(1)}, u32[]{:S(2)}, u32[]{:S(2)}) %collective-permute-start.4) | collective-permute-done | bytes 73760 | tf_op jit(solution)/shard_map/ppermute | solution.py:29
  21.3 1.6 %collective-permute-start.5 = (bf16[72,512]{1,0:T(8,128)(2,1)S(1)}, bf16[72,512]{1,0:T(8,128)(2,1)S(1)}, u32[]{:S(2)}, u32[]{:S(2)}) collective-permute-start(bf16[72,512]{1,0:T(8,128)(2,1)S(1)} %get-tuple-element.39.own), channel_id=1, source_target_pairs={{0,8},{1,9},{2,10},{3,11},{4,12},{5,13},{6,14},{7,15},{8,0},{9,1},... | collective-permute-start | bytes 221192 | tf_op jit(solution)/shard_map/ppermute | solution.py:29
  23.0 1.8 %collective-permute-start.10 = (bf16[64,512]{1,0:T(8,128)(2,1)S(1)}, bf16[64,512]{1,0:T(8,128)(2,1)S(1)}, u32[]{:S(2)}, u32[]{:S(2)}) collective-permute-start(bf16[64,512]{1,0:T(8,128)(2,1)S(1)} %get-tuple-element.41.refs_6_), channel_id=1, source_target_pairs={{0,16},{1,17},{2,18},{3,19},{4,20},{5,21},{6,22},{7,23},{8,24},{9,... | collective-permute-start | bytes 196616 | tf_op jit(solution)/shard_map/ppermute | solution.py:29
  24.8 1.0 %collective-permute-start.9 = (bf16[64,512]{1,0:T(8,128)(2,1)S(1)}, bf16[64,512]{1,0:T(8,128)(2,1)S(1)}, u32[]{:S(2)}, u32[]{:S(2)}) collective-permute-start(bf16[64,512]{1,0:T(8,128)(2,1)S(1)} %get-tuple-element.41.refs_6_), channel_id=1, source_target_pairs={{0,24},{1,25},{2,26},{3,27},{4,28},{5,29},{6,30},{7,31},{8,16},{9,... | collective-permute-start | bytes 196616 | tf_op jit(solution)/shard_map/ppermute | solution.py:29
  26.0 1.7 %collective-permute-start.8 = (bf16[128,512]{1,0:T(8,128)(2,1)S(1)}, bf16[128,512]{1,0:T(8,128)(2,1)S(1)}, u32[]{:S(2)}, u32[]{:S(2)}) collective-permute-start(bf16[128,512]{1,0:T(8,128)(2,1)S(1)} %get-tuple-element.40.refs_0_), channel_id=1, source_target_pairs={{0,6},{1,7},{2,4},{3,5},{4,2},{5,3},{6,0},{7,1},{8,14},{9,15},{10,... | collective-permute-start | bytes 393224 | tf_op jit(solution)/shard_map/ppermute | solution.py:29
  27.7 1.5 %collective-permute-start.7 = (bf16[128,512]{1,0:T(8,128)(2,1)S(1)}, bf16[128,512]{1,0:T(8,128)(2,1)S(1)}, u32[]{:S(2)}, u32[]{:S(2)}) collective-permute-start(bf16[128,512]{1,0:T(8,128)(2,1)S(1)} %get-tuple-element.40.refs_0_), channel_id=1, source_target_pairs={{0,4},{1,3},{2,6},{3,1},{4,0},{5,7},{6,2},{7,5},{8,12},{9,11},{10,... | collective-permute-start | bytes 393224 | tf_op jit(solution)/shard_map/ppermute | solution.py:29
  29.6 1.3 %collective-permute-done.9.second = bf16[64,512]{1,0:T(8,128)(2,1)S(1)} collective-permute-done((bf16[64,512]{1,0:T(8,128)(2,1)S(1)}, bf16[64,512]{1,0:T(8,128)(2,1)S(1)}, u32[]{:S(2)}, u32[]{:S(2)}) %collective-permute-start.9) | collective-permute-done | bytes 65568 | tf_op jit(solution)/shard_map/ppermute | solution.py:29
  30.9 1.6 %collective-permute-start.13 = (bf16[128,512]{1,0:T(8,128)(2,1)S(1)}, bf16[128,512]{1,0:T(8,128)(2,1)S(1)}, u32[]{:S(2)}, u32[]{:S(2)}) collective-permute-start(bf16[128,512]{1,0:T(8,128)(2,1)S(1)} %shard_map.63.refs_4_.refs_7_), channel_id=1, source_target_pairs={{0,6},{1,7},{2,4},{3,5},{4,2},{5,3},{6,0},{7,1},{8,14},{9,15},{10,... | collective-permute-start | bytes 393224 | tf_op jit(solution)/shard_map/ppermute | solution.py:29
  32.5 1.2 %collective-permute-start.12 = (bf16[128,512]{1,0:T(8,128)(2,1)S(1)}, bf16[128,512]{1,0:T(8,128)(2,1)S(1)}, u32[]{:S(2)}, u32[]{:S(2)}) collective-permute-start(bf16[128,512]{1,0:T(8,128)(2,1)S(1)} %shard_map.63.refs_4_.refs_7_), channel_id=1, source_target_pairs={{0,4},{1,3},{2,6},{3,1},{4,0},{5,7},{6,2},{7,5},{8,12},{9,11},{10,... | collective-permute-start | bytes 393224 | tf_op jit(solution)/shard_map/ppermute | solution.py:29
  33.7 1.1 %collective-permute-start.11 = (bf16[128,512]{1,0:T(8,128)(2,1)S(1)}, bf16[128,512]{1,0:T(8,128)(2,1)S(1)}, u32[]{:S(2)}, u32[]{:S(2)}) collective-permute-start(bf16[128,512]{1,0:T(8,128)(2,1)S(1)} %shard_map.63.refs_4_.refs_7_), channel_id=1, source_target_pairs={{0,2},{1,5},{2,0},{3,7},{4,6},{5,1},{6,4},{7,3},{8,10},{9,13},{10,... | collective-permute-start | bytes 393224 | tf_op jit(solution)/shard_map/ppermute | solution.py:29
  35.5 1.6 %shard_map.64 = (f32[1024,512]{1,0:T(8,128)S(1)}, f32[1024,128]{1,0:T(8,128)S(1)}, bf16[64,512]{1,0:T(8,128)(2,1)S(1)}, bf16[64,512]{1,0:T(8,128)(2,1)}) custom-call(bf16[128,512]{1,0:T(8,128)(2,1)S(1)} %get-tuple-element.40.refs_0_, bf16[128,512]{1,0:T(8,128)(2,1)S(1)} %collective-permute-done.6.refs_1_, ...), custom_call_target="tpu_custom_call" | custom-call | tf_op jit(solution)/shard_map/pallas_call | solution.py:391
  37.1 0.9 %collective-permute-done.13.refs_2_ = bf16[128,512]{1,0:T(8,128)(2,1)S(1)} collective-permute-done((bf16[128,512]{1,0:T(8,128)(2,1)S(1)}, bf16[128,512]{1,0:T(8,128)(2,1)S(1)}, u32[]{:S(2)}, u32[]{:S(2)}) %collective-permute-start.13) | collective-permute-done | bytes 131104 | tf_op jit(solution)/shard_map/ppermute | solution.py:29
  38.0 1.1 %collective-permute-done.12.refs_1_ = bf16[128,512]{1,0:T(8,128)(2,1)S(1)} collective-permute-done((bf16[128,512]{1,0:T(8,128)(2,1)S(1)}, bf16[128,512]{1,0:T(8,128)(2,1)S(1)}, u32[]{:S(2)}, u32[]{:S(2)}) %collective-permute-start.12) | collective-permute-done | bytes 131104 | tf_op jit(solution)/shard_map/ppermute | solution.py:29
  39.2 0.6 %shard_map.65 = (bf16[512,512]{1,0:T(8,128)(2,1)S(1)}, bf16[64,512]{1,0:T(8,128)(2,1)S(1)}) custom-call(bf16[128,512]{1,0:T(8,128)(2,1)S(1)} %collective-permute-done.11.refs_0_, bf16[128,512]{1,0:T(8,128)(2,1)S(1)} %collective-permute-done.12.refs_1_, bf16[128,512]{1,0:T(8,128)(2,1)S(1)} %collective-permute-done.13.refs_2_, ...), custom_call_target="tpu_custom_call" | custom-call | tf_op jit(solution)/shard_map/pallas_call | solution.py:439
  39.9 1.1 %shard_map.66 = (bf16[64,512]{1,0:T(8,128)(2,1)}, f32[64,512]{1,0:T(8,128)S(1)}) custom-call(bf16[128,512]{1,0:T(8,128)(2,1)S(1)} %collective-permute-done.11.refs_0_, bf16[128,512]{1,0:T(8,128)(2,1)S(1)} %collective-permute-done.12.refs_1_, bf16[128,512]{1,0:T(8,128)(2,1)S(1)} %collective-permute-done.13.refs_2_, ...), custom_call_target="tpu_custom_call" | custom-call | tf_op jit(solution)/shard_map/pallas_call | solution.py:470
  41.2 0.7 %convert_add_fusion = f32[64,512]{1,0:T(8,128)} fusion(f32[64,512]{1,0:T(8,128)S(1)} %get-tuple-element.49, bf16[64,512]{1,0:T(8,128)(2,1)S(1)} %collective-permute-done.14), kind=kLoop, calls=%fused_computation | loop fusion | flops 65536 | bytes 327680 | tf_op jit(solution)/shard_map/add | solution.py:554
  (16 shorter events, 2.6 us)
Async XLA Ops:
  3.1 8.0 %collective-permute-start = (bf16[136,512]{1,0:T(8,128)(2,1)S(1)}, bf16[136,512]{1,0:T(8,128)(2,1)S(1)}, u32[]{:S(2)}, u32[]{:S(2)}) collective-permute-start(bf16[136,512]{1,0:T(8,128)(2,1)S(1)} %get-tuple-element.27), channel_id=1, source_target_pairs={{0,6},{1,7},{2,4},{3,5},{4,2},{5,3},{6,0},{7,1},{8,14},{9,15},{10,... | collective-permute-start | bytes 417800 | tf_op jit(solution)/shard_map/ppermute | solution.py:29
  7.1 6.9 %collective-permute-start.1 = (bf16[136,512]{1,0:T(8,128)(2,1)S(1)}, bf16[136,512]{1,0:T(8,128)(2,1)S(1)}, u32[]{:S(2)}, u32[]{:S(2)}) collective-permute-start(bf16[136,512]{1,0:T(8,128)(2,1)S(1)} %get-tuple-element.28), channel_id=1, source_target_pairs={{0,2},{1,5},{2,0},{3,7},{4,6},{5,1},{6,4},{7,3},{8,10},{9,13},{10,... | collective-permute-start | bytes 417800 | tf_op jit(solution)/shard_map/ppermute | solution.py:29
  8.6 5.4 %collective-permute-start.2 = (bf16[136,512]{1,0:T(8,128)(2,1)S(1)}, bf16[136,512]{1,0:T(8,128)(2,1)S(1)}, u32[]{:S(2)}, u32[]{:S(2)}) collective-permute-start(bf16[136,512]{1,0:T(8,128)(2,1)S(1)} %get-tuple-element.32), channel_id=1, source_target_pairs={{0,4},{1,3},{2,6},{3,1},{4,0},{5,7},{6,2},{7,5},{8,12},{9,11},{10,... | collective-permute-start | bytes 417800 | tf_op jit(solution)/shard_map/ppermute | solution.py:29
  14.2 6.0 %collective-permute-start.3 = (bf16[72,512]{1,0:T(8,128)(2,1)S(1)}, bf16[72,512]{1,0:T(8,128)(2,1)S(1)}, u32[]{:S(2)}, u32[]{:S(2)}) collective-permute-start(bf16[72,512]{1,0:T(8,128)(2,1)S(1)} %get-tuple-element.35), channel_id=1, source_target_pairs={{0,16},{1,17},{2,18},{3,19},{4,20},{5,21},{6,22},{7,23},{8,24},{9,... | collective-permute-start | bytes 221192 | tf_op jit(solution)/shard_map/ppermute | solution.py:29
  16.8 4.4 %collective-permute-start.4 = (bf16[72,512]{1,0:T(8,128)(2,1)S(1)}, bf16[72,512]{1,0:T(8,128)(2,1)S(1)}, u32[]{:S(2)}, u32[]{:S(2)}) collective-permute-start(bf16[72,512]{1,0:T(8,128)(2,1)S(1)} %get-tuple-element.36), channel_id=1, source_target_pairs={{0,8},{1,9},{2,10},{3,11},{4,12},{5,13},{6,14},{7,15},{8,0},{9,1},... | collective-permute-start | bytes 221192 | tf_op jit(solution)/shard_map/ppermute | solution.py:29
  21.3 4.5 %collective-permute-start.5 = (bf16[72,512]{1,0:T(8,128)(2,1)S(1)}, bf16[72,512]{1,0:T(8,128)(2,1)S(1)}, u32[]{:S(2)}, u32[]{:S(2)}) collective-permute-start(bf16[72,512]{1,0:T(8,128)(2,1)S(1)} %get-tuple-element.39.own), channel_id=1, source_target_pairs={{0,8},{1,9},{2,10},{3,11},{4,12},{5,13},{6,14},{7,15},{8,0},{9,1},... | collective-permute-start | bytes 221192 | tf_op jit(solution)/shard_map/ppermute | solution.py:29
  23.0 6.6 %collective-permute-start.10 = (bf16[64,512]{1,0:T(8,128)(2,1)S(1)}, bf16[64,512]{1,0:T(8,128)(2,1)S(1)}, u32[]{:S(2)}, u32[]{:S(2)}) collective-permute-start(bf16[64,512]{1,0:T(8,128)(2,1)S(1)} %get-tuple-element.41.refs_6_), channel_id=1, source_target_pairs={{0,16},{1,17},{2,18},{3,19},{4,20},{5,21},{6,22},{7,23},{8,24},{9,... | collective-permute-start | bytes 196616 | tf_op jit(solution)/shard_map/ppermute | solution.py:29
  24.8 6.1 %collective-permute-start.9 = (bf16[64,512]{1,0:T(8,128)(2,1)S(1)}, bf16[64,512]{1,0:T(8,128)(2,1)S(1)}, u32[]{:S(2)}, u32[]{:S(2)}) collective-permute-start(bf16[64,512]{1,0:T(8,128)(2,1)S(1)} %get-tuple-element.41.refs_6_), channel_id=1, source_target_pairs={{0,24},{1,25},{2,26},{3,27},{4,28},{5,29},{6,30},{7,31},{8,16},{9,... | collective-permute-start | bytes 196616 | tf_op jit(solution)/shard_map/ppermute | solution.py:29
  26.0 7.7 %collective-permute-start.8 = (bf16[128,512]{1,0:T(8,128)(2,1)S(1)}, bf16[128,512]{1,0:T(8,128)(2,1)S(1)}, u32[]{:S(2)}, u32[]{:S(2)}) collective-permute-start(bf16[128,512]{1,0:T(8,128)(2,1)S(1)} %get-tuple-element.40.refs_0_), channel_id=1, source_target_pairs={{0,6},{1,7},{2,4},{3,5},{4,2},{5,3},{6,0},{7,1},{8,14},{9,15},{10,... | collective-permute-start | bytes 393224 | tf_op jit(solution)/shard_map/ppermute | solution.py:29
  27.7 7.8 %collective-permute-start.7 = (bf16[128,512]{1,0:T(8,128)(2,1)S(1)}, bf16[128,512]{1,0:T(8,128)(2,1)S(1)}, u32[]{:S(2)}, u32[]{:S(2)}) collective-permute-start(bf16[128,512]{1,0:T(8,128)(2,1)S(1)} %get-tuple-element.40.refs_0_), channel_id=1, source_target_pairs={{0,4},{1,3},{2,6},{3,1},{4,0},{5,7},{6,2},{7,5},{8,12},{9,11},{10,... | collective-permute-start | bytes 393224 | tf_op jit(solution)/shard_map/ppermute | solution.py:29
  29.2 6.3 %collective-permute-start.6 = (bf16[128,512]{1,0:T(8,128)(2,1)S(1)}, bf16[128,512]{1,0:T(8,128)(2,1)S(1)}, u32[]{:S(2)}, u32[]{:S(2)}) collective-permute-start(bf16[128,512]{1,0:T(8,128)(2,1)S(1)} %get-tuple-element.40.refs_0_), channel_id=1, source_target_pairs={{0,2},{1,5},{2,0},{3,7},{4,6},{5,1},{6,4},{7,3},{8,10},{9,13},{10,... | collective-permute-start | bytes 393224 | tf_op jit(solution)/shard_map/ppermute | solution.py:29
  30.9 7.1 %collective-permute-start.13 = (bf16[128,512]{1,0:T(8,128)(2,1)S(1)}, bf16[128,512]{1,0:T(8,128)(2,1)S(1)}, u32[]{:S(2)}, u32[]{:S(2)}) collective-permute-start(bf16[128,512]{1,0:T(8,128)(2,1)S(1)} %shard_map.63.refs_4_.refs_7_), channel_id=1, source_target_pairs={{0,6},{1,7},{2,4},{3,5},{4,2},{5,3},{6,0},{7,1},{8,14},{9,15},{10,... | collective-permute-start | bytes 393224 | tf_op jit(solution)/shard_map/ppermute | solution.py:29
  32.5 6.6 %collective-permute-start.12 = (bf16[128,512]{1,0:T(8,128)(2,1)S(1)}, bf16[128,512]{1,0:T(8,128)(2,1)S(1)}, u32[]{:S(2)}, u32[]{:S(2)}) collective-permute-start(bf16[128,512]{1,0:T(8,128)(2,1)S(1)} %shard_map.63.refs_4_.refs_7_), channel_id=1, source_target_pairs={{0,4},{1,3},{2,6},{3,1},{4,0},{5,7},{6,2},{7,5},{8,12},{9,11},{10,... | collective-permute-start | bytes 393224 | tf_op jit(solution)/shard_map/ppermute | solution.py:29
  33.7 5.5 %collective-permute-start.11 = (bf16[128,512]{1,0:T(8,128)(2,1)S(1)}, bf16[128,512]{1,0:T(8,128)(2,1)S(1)}, u32[]{:S(2)}, u32[]{:S(2)}) collective-permute-start(bf16[128,512]{1,0:T(8,128)(2,1)S(1)} %shard_map.63.refs_4_.refs_7_), channel_id=1, source_target_pairs={{0,2},{1,5},{2,0},{3,7},{4,6},{5,1},{6,4},{7,3},{8,10},{9,13},{10,... | collective-permute-start | bytes 393224 | tf_op jit(solution)/shard_map/ppermute | solution.py:29
  39.9 1.3 %collective-permute-start.14 = (bf16[64,512]{1,0:T(8,128)(2,1)S(1)}, bf16[64,512]{1,0:T(8,128)(2,1)S(1)}, u32[]{:S(2)}, u32[]{:S(2)}) collective-permute-start(bf16[64,512]{1,0:T(8,128)(2,1)S(1)} %get-tuple-element.50), channel_id=1, source_target_pairs={{0,1},{1,0},{2,3},{3,2},{4,5},{5,4},{6,7},{7,6},{8,9},{9,8},{10,11... | collective-permute-start | bytes 196616 | tf_op jit(solution)/shard_map/ppermute | solution.py:29
